TPU v7x, 32 devices: a whole 2x2x4 slice. The times are simulated.
32 devices in a mesh: pipe: 2 (over x), dp: 16 (over z, y, core).
Axes of the slice: x: 2, y: 2, z: 4, core: 2. Of those that a mesh axis runs over, the one named last changes fastest.
Arguments:
- fields: float32 [32, 48, 16, 128], P('dp', 'pipe'), may hold values from -13 to 13
- item_weights: int32 [32], P('dp'), may hold values from 1 to 96, as said below
- live_counts: int32 [16], P('dp'), may hold values from 0 to 2
- running_stats: float32 [2, 48], P(None, 'pipe'), may hold values from 0.5 to 2
- embed_weight: bfloat16 [48, 4, 1024], replicated, may hold values from -3 to 3
- variable_embed: bfloat16 [48, 1024], replicated, may hold values from -3 to 3
- variable_query: bfloat16 [1024], replicated, may hold values from -6 to 6
- attend_weight: bfloat16 [2, 3, 1024, 1024], P('pipe'), may hold values from -0.1875 to 0.1875
- merge_weight: bfloat16 [2, 1024, 1024], P('pipe'), may hold values from -1 to 1
- position_embed: bfloat16 [512, 1024], replicated, may hold values from -3 to 3
- norm_gain: float32 [2, 1024], replicated, may hold values from 0.5 to 1.5
- norm_bias: float32 [2, 1024], replicated, may hold values from -2 to 2
- up_weight: bfloat16 [1024, 4096], replicated, may hold values from -0.1875 to 0.1875
- hidden_bias: float32 [4096], replicated, may hold values from -3 to 3
- down_weight: bfloat16 [4096, 1024], replicated, may hold values from -0.09375 to 0.09375
- output_bias: float32 [1024], replicated, may hold values from -4 to 4
- cotangent: bfloat16 [32, 512, 1024], P('dp'), may hold values from -6 to 6
Outputs:
- statistics: float32 [2, 48], P(None, 'pipe')
- section_outputs: bfloat16 [2, 32, 512, 1024], P('pipe', 'dp')
- field_grads: float32 [32, 48, 16, 128], P('dp', 'pipe')
- embed_grads: float32 [48, 4, 1024], replicated
- variable_grads: float32 [48, 1024], replicated
- query_grads: float32 [1024], replicated
- attend_grads: float32 [2, 3, 1024, 1024], P('pipe', None, 'dp')
- merge_grads: float32 [2, 1024, 1024], P('pipe', 'dp')
- position_grads: float32 [512, 1024], replicated
- gain_grads: float32 [2, 1024], replicated
- bias_grads: float32 [2, 1024], replicated
- up_grads: float32 [1024, 4096], P(None, ('pipe', 'dp'))
- hidden_grads: float32 [4096], P(('pipe', 'dp'))
- down_grads: float32 [4096, 1024], P(('pipe', 'dp'))
- output_grads: float32 [1024], replicated
Inputs may be any that keep to these rules, and one draw needn't show every extreme that they name: `item_weights`: whole numbers.
All inputs are finite; a program needn't handle non-finite values.
Results may differ from a plain program's by a relative error of at most 0.015.
The roundings to bfloat16 on the way count: a program that leaves them out, or rounds other values in their place, can miss the bound.
Values may be sent and summed in bfloat16 or wider, within the bound.
No kernel may reach another device: no remote copies, remote signals or barrier semaphores. Data moves between devices by JAX's collectives and lax.ppermute only.
A program may use at most 448 MiB of HBM per device.

v0:
```python
import functools

import jax
import jax.numpy as jnp
from jax import lax
from jax.experimental import pallas as pl
from jax.experimental.pallas import tpu as pltpu
from jax.sharding import PartitionSpec as P

D = 1024
HEADS = 16
HDIM = 64
FF = 4096
VARS = 48
PATCH = 2
PATCHES = 512
PIECES = PATCH * PATCH
ROWS_TABLE = VARS * (PIECES + 1)
HALF = D // 2
QUARTER = D // 4
TABLE_PAD = 256
FF_TILE = 512
FF_STEPS = FF // FF_TILE
PAIRS = HEADS // 2
LANES = 2 * HDIM
CHUNK = 64
TOKENS_BACK = 2

PRECISE = lax.Precision.HIGHEST
EPSILON = 1e-05
MOMENTUM = 0.1
BF = jnp.bfloat16
F32 = jnp.float32
VMEM_LIMIT = 56 * 1024 * 1024


def dot(left, right, left_dim, right_dim):
    return lax.dot_general(
        left, right, (((left_dim,), (right_dim,)), ((), ())), preferred_element_type=F32
    )


VMEM = pl.BlockSpec(memory_space=pltpu.VMEM)
SMEM = pl.BlockSpec(memory_space=pltpu.SMEM)
ANYWHERE = pl.BlockSpec(memory_space=pl.ANY)


def shape(dims, kind):
    return jax.ShapeDtypeStruct(dims, kind)


def params(grid=0):
    semantics = ("arbitrary",) * grid if grid else None
    return pltpu.CompilerParams(vmem_limit_bytes=VMEM_LIMIT, dimension_semantics=semantics)


def cost():
    return pl.CostEstimate(flops=1000, bytes_accessed=1000, transcendentals=0)


def section_copies(place_ref, section, own, brought, targets, sems):
    core, side = place_ref[1], place_ref[2]

    def rows(core, side):
        return pl.ds(pl.multiple_of((2 * core + side) * QUARTER, QUARTER), QUARTER)

    @pl.when(place_ref[0] == section)
    def _():
        for n, target in enumerate(targets):
            for quarter in range(4):
                part = pl.ds(quarter * QUARTER, QUARTER)
                pltpu.make_async_copy(
                    own[n].at[part], target.at[part], sems.at[n, quarter]
                ).start()

    @pl.when(place_ref[0] != section)
    def _():
        for n, target in enumerate(targets):
            for other in range(2):
                for turn in range(2):
                    place = rows(core + other - 2 * core * other, side + turn - 2 * side * turn)
                    pltpu.make_async_copy(
                        brought[n][other].at[turn], target.at[place], sems.at[n, 2 * other + turn]
                    ).start()

    def wait(n):
        for quarter in range(4):
            part = pl.ds(quarter * QUARTER, QUARTER)
            pltpu.make_async_copy(
                brought[n][0].at[0], targets[n].at[part], sems.at[n, quarter]
            ).wait()

    return wait


def normalized(values):
    center = values - jnp.mean(values, axis=-1, keepdims=True)
    spread = jnp.mean(center * center, axis=-1, keepdims=True)
    inverse = lax.rsqrt(spread + EPSILON)
    return center * inverse, inverse


def norm_back(xhat, inverse, gain, grad):
    scaled = grad * gain
    first = jnp.mean(scaled, axis=-1, keepdims=True)
    second = jnp.mean(scaled * xhat, axis=-1, keepdims=True)
    return (scaled - first - xhat * second) * inverse


def row_chunks(body):
    def step(i, carry):
        body(pl.ds(pl.multiple_of(i * CHUNK, CHUNK), CHUNK))
        return carry

    lax.fori_loop(0, PATCHES // CHUNK, step, 0)


def column_tiles(width, body):
    def step(i, carry):
        body(pl.ds(pl.multiple_of(i * width, width), width))
        return carry

    lax.fori_loop(0, D // width, step, 0)


def head_rows(width):
    row = lax.broadcasted_iota(jnp.int32, (HEADS, width), 0)
    column = lax.broadcasted_iota(jnp.int32, (HEADS, width), 1)
    start = row * HDIM
    return (column >= start) & (column < start + HDIM)


def tables_kernel(query_ref, table_ref, weight_ref, low_ref, keys_ref, value_ref):
    given = jnp.broadcast_to(query_ref[...], (HEADS, D)).astype(BF)
    query = dot(given, weight_ref[0], 1, 0).astype(BF).astype(F32)
    low_ref[...] = query
    spread = jnp.where(head_rows(D), query, 0.0).astype(BF)
    key_query = (dot(spread, weight_ref[1], 1, 1) * HDIM ** (-0.5)).astype(BF)
    keys_ref[...] = dot(table_ref[...], key_query, 1, 1)
    values = dot(table_ref[...], weight_ref[2], 1, 0)
    value_ref[...] = jnp.concatenate([values, key_query.astype(F32)], axis=0).T


def tables(query, table, weights):
    return pl.pallas_call(
        tables_kernel,
        out_shape=(
            shape((HEADS, D), F32),
            shape((ROWS_TABLE, HEADS), F32),
            shape((D, TABLE_PAD), F32),
        ),
        in_specs=[VMEM] * 3,
        out_specs=(VMEM,) * 3,
        compiler_params=params(),
        cost_estimate=cost(),
        name="tables",
    )(query, table, weights)


COLS = 128
STRIPES = 16


def column_order():
    row = lax.broadcasted_iota(jnp.int32, (COLS, COLS), 0)
    column = lax.broadcasted_iota(jnp.int32, (COLS, COLS), 1)
    place = jnp.where(column < COLS // 2, 2 * column, 2 * column - COLS + 1)
    return (row == place).astype(F32)


def exact(left, right, right_dim):
    return lax.dot_general(
        left,
        right,
        (((1,), (right_dim,)), ((), ())),
        precision=PRECISE,
        preferred_element_type=F32,
    )


def head_keys(keys_ref, h):
    keys = keys_ref[...]
    lane = lax.broadcasted_iota(jnp.int32, keys.shape, 1)
    return jnp.sum(jnp.where(lane == h, keys, 0.0), axis=1, keepdims=True)


def mixed_rows(shares, pixels_ref):
    return jnp.concatenate(
        [(shares * pixels_ref[k]).astype(BF) for k in range(PIECES)]
        + [shares.astype(BF), jnp.zeros((TABLE_PAD - ROWS_TABLE, PATCHES), BF)],
        axis=0,
    )


def aggregate_kernel(
    place_ref,
    alive_ref,
    own_field_ref,
    other_field_ref,
    center_ref,
    scale_ref,
    keys_ref,
    tvt_ref,
    position_ref,
    own_ref,
    brought_ref,
    beside_ref,
    tokens_ref,
    heads_ref,
    shares_ref,
    pixels_ref,
    merge_ref,
    grid_ref,
    sems,
):
    wait = section_copies(
        place_ref, 0, [own_ref], [(brought_ref, beside_ref)], [merge_ref], sems
    )
    alive = alive_ref[0]
    order = column_order()
    half = VARS // 2 * STRIPES
    own, other = own_field_ref[...], other_field_ref[...]
    grid_ref[:half] = exact(jnp.where(place_ref[0] == 0, own, other), order, 0)
    grid_ref[half:] = exact(jnp.where(place_ref[0] == 0, other, own), order, 0)
    center, scale = center_ref[...], scale_ref[...]
    low_lane = lax.broadcasted_iota(jnp.int32, (VARS, COLS), 1) < COLS // 2

    def stripe(r):
        values = grid_ref[pl.ds(r, VARS, stride=STRIPES), :]
        return ((values - center) * scale).astype(BF).astype(F32)

    for a in range(PATCH):
        for j in range(PATCHES // COLS):
            even, odd = stripe(4 * j + a), stripe(4 * j + 2 + a)
            columns = slice(j * COLS, (j + 1) * COLS)
            pixels_ref[2 * a, :, columns] = jnp.where(
                low_lane, even, pltpu.roll(odd, COLS // 2, 1)
            )
            pixels_ref[2 * a + 1, :, columns] = jnp.where(
                low_lane, pltpu.roll(even, COLS // 2, 1), odd
            )

    def head(h, carry):
        keys = head_keys(keys_ref, h)
        scores = keys[PIECES * VARS :]
        for k in range(PIECES):
            scores = scores + keys[k * VARS : (k + 1) * VARS] * pixels_ref[k]
        top = jnp.max(scores, axis=0, keepdims=True)
        powers = jnp.exp(scores - top)
        shares = powers / jnp.sum(powers, axis=0, keepdims=True)
        shares_ref[h] = shares
        rows = pl.ds(pl.multiple_of(h * HDIM, HDIM), HDIM)
        heads_ref[rows, :] = dot(tvt_ref[rows, :], mixed_rows(shares, pixels_ref), 1, 0).astype(
            BF
        )
        return carry

    lax.fori_loop(0, HEADS, head, 0)
    wait(0)
    heads = heads_ref[...]

    def tile(columns):
        merged = dot(heads, merge_ref[:, columns], 0, 0)
        tokens_ref[:, columns] = (alive * (merged + position_ref[:, columns].astype(F32))).astype(
            BF
        )

    column_tiles(256, tile)


def aggregate(place, alive, own_field, other_field, center, scale, keys, tvt, position, merge):
    return pl.pallas_call(
        aggregate_kernel,
        out_shape=(
            shape((PATCHES, D), BF),
            shape((D, PATCHES), BF),
            shape((HEADS, VARS, PATCHES), F32),
            shape((PIECES, VARS, PATCHES), F32),
        ),
        in_specs=[SMEM, SMEM] + [VMEM] * 7 + [ANYWHERE] * 3,
        out_specs=(VMEM,) * 4,
        scratch_shapes=[
            pltpu.VMEM((D, D), BF),
            pltpu.VMEM((VARS * STRIPES, COLS), F32),
            pltpu.SemaphoreType.DMA((1, 4)),
        ],
        compiler_params=params(),
        cost_estimate=cost(),
        name="aggregate",
    )(place, alive, own_field, other_field, center, scale, keys, tvt, position, *merge)


def attend_kernel(place_ref, tokens_ref, gain_ref, bias_ref, attend_ref, *refs):
    brought = [(refs[2 * n], refs[2 * n + 1]) for n in range(3)]
    pack_ref, proj_ref, lse_ref, weight_ref, first_ref, sems = refs[6:]
    wait = section_copies(
        place_ref,
        1,
        [attend_ref.at[j] for j in range(3)],
        brought,
        [weight_ref.at[j] for j in range(3)],
        sems,
    )

    def first_norm(rows):
        xhat, _ = normalized(tokens_ref[rows, :].astype(F32))
        first_ref[rows, :] = (xhat * gain_ref[0:1, :] + bias_ref[0:1, :]).astype(BF)

    row_chunks(first_norm)
    pack_ref[:D, :] = first_ref[...].T
    for j in range(3):
        wait(j)
        column_tiles(
            256,
            lambda columns: proj_ref.__setitem__(
                (j, slice(None), columns),
                dot(first_ref[...], weight_ref[j, :, columns], 1, 0).astype(BF),
            ),
        )

    lane = lax.broadcasted_iota(jnp.int32, (PATCHES, LANES), 1)

    def pair(i, carry):
        columns = pl.ds(pl.multiple_of(i * LANES, LANES), LANES)
        queries = proj_ref[0, :, columns]
        keys = proj_ref[1, :, columns]
        values = proj_ref[2, :, columns].T
        for side in range(2):
            inside = (lane < HDIM) if side == 0 else (lane >= HDIM)
            key = jnp.where(inside, keys * HDIM ** (-0.5), jnp.zeros_like(keys)).astype(BF)
            scores = dot(key, queries, 1, 1)
            top = jnp.max(scores, axis=0, keepdims=True)
            powers = jnp.exp(scores - top)
            whole = jnp.sum(powers, axis=0, keepdims=True)
            probs = (powers * (1.0 / whole)).astype(BF)
            lse_ref[i, side : side + 1, :] = top + jnp.log(whole)
            value = values[side * HDIM : (side + 1) * HDIM]
            rows = pl.ds(pl.multiple_of(D + i * LANES + side * HDIM, HDIM), HDIM)
            pack_ref[rows, :] = dot(value, probs, 1, 0).astype(BF)
        return carry

    lax.fori_loop(0, PAIRS, pair, 0)


def attend(place, tokens, gain, bias, own_attend, brought):
    return pl.pallas_call(
        attend_kernel,
        out_shape=(
            shape((2 * D, PATCHES), BF),
            shape((3, PATCHES, D), BF),
            shape((PAIRS, 2, PATCHES), F32),
        ),
        in_specs=[SMEM] + [VMEM] * 3 + [ANYWHERE] * 7,
        out_specs=(VMEM,) * 3,
        scratch_shapes=[
            pltpu.VMEM((3, D, D), BF),
            pltpu.VMEM((PATCHES, D), BF),
            pltpu.SemaphoreType.DMA((3, 4)),
        ],
        compiler_params=params(),
        cost_estimate=cost(),
        name="attend",
    )(place, tokens, gain, bias, own_attend, *brought)


def merge_kernel(
    place_ref,
    tokens_ref,
    pack_ref,
    gain_ref,
    bias_ref,
    own_ref,
    brought_ref,
    beside_ref,
    middle_ref,
    second_ref,
    merge_ref,
    sems,
):
    wait = section_copies(
        place_ref, 1, [own_ref], [(brought_ref, beside_ref)], [merge_ref], sems
    )
    wait(0)
    context = pack_ref[...]
    column_tiles(
        256,
        lambda columns: middle_ref.__setitem__(
            (slice(None), columns),
            tokens_ref[:, columns].astype(F32) + dot(context, merge_ref[:, columns], 0, 0),
        ),
    )

    def second_norm(rows):
        xhat, _ = normalized(middle_ref[rows, :])
        second_ref[rows, :] = (xhat * gain_ref[1:2, :] + bias_ref[1:2, :]).astype(BF)

    row_chunks(second_norm)


def merge(place, tokens, pack, gain, bias, weights):
    return pl.pallas_call(
        merge_kernel,
        grid=(1,),
        out_shape=(shape((PATCHES, D), F32), shape((PATCHES, D), BF)),
        in_specs=[SMEM, VMEM, pl.BlockSpec((D, PATCHES), lambda i: (1, 0)), VMEM, VMEM]
        + [ANYWHERE] * 3,
        out_specs=(VMEM,) * 2,
        scratch_shapes=[pltpu.VMEM((D, D), BF), pltpu.SemaphoreType.DMA((1, 4))],
        compiler_params=params(1),
        cost_estimate=cost(),
        name="merge",
    )(place, tokens, pack, gain, bias, *weights)


def gelu_parts(hidden):
    inverse = 1.0 / (1.0 + 0.23164190 * jnp.abs(hidden))
    decay = jnp.exp2(hidden * hidden * (-0.72134752))
    series = 0.5 * 1.061405429
    for factor in (-1.453152027, 1.421413741, -0.284496736, 0.254829592):
        series = series * inverse + 0.5 * factor
    tail = series * inverse * decay
    cdf = jnp.where(hidden >= 0.0, 1.0 - tail, tail)
    return cdf, decay * 0.3989422804014327


FF_PART = 256
UNITS = FF + HALF


def copy(source, target, sem):
    return pltpu.make_async_copy(source, target, sem)


def aligned(index, size):
    return pl.ds(pl.multiple_of(index * size, size), size)


def start_either(choice, source, if_true, if_false, sem):
    @pl.when(choice)
    def _():
        copy(source, if_true, sem).start()

    @pl.when(jnp.logical_not(choice))
    def _():
        copy(source, if_false, sem).start()


def expand_kernel(
    place_ref,
    second_ref,
    out_ref,
    bias_ref,
    up_any,
    down_any,
    after_any,
    units_any,
    sum_ref,
    up_ref,
    down_ref,
    tile_ref,
    in_sems,
    out_sems,
):
    def fetch(j):
        part = aligned(j, FF_TILE)
        return (
            copy(up_any.at[:, part], up_ref.at[:, part], in_sems.at[j, 0]),
            copy(down_any.at[part], down_ref.at[part], in_sems.at[j, 1]),
        )

    def put(j, slot):
        return copy(
            tile_ref.at[slot], units_any.at[:, :, aligned(j, FF_TILE)], out_sems.at[slot]
        )

    for j in range(FF_STEPS):
        for one in fetch(j):
            one.start()

    def step(j, carry):
        slot = lax.rem(j, 2)

        @pl.when(j >= 2)
        def _():
            put(j - 2, slot).wait()

        for one in fetch(j):
            one.wait()
        for part in range(FF_TILE // FF_PART):
            inner = slice(part * FF_PART, (part + 1) * FF_PART)
            start = pl.multiple_of(j * FF_TILE + part * FF_PART, FF_PART)
            columns = pl.ds(start, FF_PART)
            hidden = dot(second_ref[...], up_ref[:, columns], 1, 0) + bias_ref[:, columns]
            grad = dot(out_ref[...], down_ref[columns, :], 1, 1)
            cdf, density = gelu_parts(hidden)
            tile_ref[slot, 0, :, inner] = (hidden * cdf).astype(BF)
            low = (grad * (cdf + hidden * density)).astype(BF)
            tile_ref[slot, 1, :, inner] = low
            sum_ref[:, columns] = jnp.sum(low.astype(F32), axis=0, keepdims=True)
        put(j, slot).start()
        return carry

    lax.fori_loop(0, FF_STEPS, step, 0)
    others = aligned(1 - place_ref[1], HALF)
    put(FF_STEPS - 2, 0).wait()
    tile_ref[0, 0] = out_ref[:, others]
    tile_ref[0, 1] = second_ref[:, others]
    put(FF_STEPS, 0).start()
    put(FF_STEPS - 1, 1).wait()
    put(FF_STEPS, 0).wait()


def expand(place, second, out_low, up, bias, down, after):
    return pl.pallas_call(
        expand_kernel,
        out_shape=(shape((2, PATCHES, UNITS), BF), shape((1, FF), F32)),
        in_specs=[SMEM, VMEM, VMEM, VMEM, ANYWHERE, ANYWHERE, ANYWHERE],
        out_specs=(ANYWHERE, VMEM),
        scratch_shapes=[
            pltpu.VMEM((D, FF), BF),
            pltpu.VMEM((FF, D), BF),
            pltpu.VMEM((2, 2, PATCHES, FF_TILE), BF),
            pltpu.SemaphoreType.DMA((FF_STEPS, 2)),
            pltpu.SemaphoreType.DMA((2,)),
        ],
        compiler_params=params(),
        cost_estimate=cost(),
        name="expand",
    )(place, second, out_low, bias.reshape(1, FF), up, down, after)


DEPTHS = 4
DEPTH = FF // DEPTHS


def contract_kernel(
    place_ref,
    scalars_ref,
    gain_ref,
    bias_ref,
    units_any,
    up_any,
    down_any,
    middle_any,
    cotangent_any,
    result_ref,
    grad_ref,
    branch_ref,
    gain_grad_ref,
    bias_grad_ref,
    out_grad_ref,
    units_ref,
    up_ref,
    down_ref,
    middle_ref,
    cotangent_ref,
    total_ref,
    second_ref,
    sems,
):
    def fetch(n):
        which, c = divmod(n, DEPTHS)
        part = slice(c * DEPTH, (c + 1) * DEPTH)
        if which == 0:
            weight = copy(down_any.at[part], down_ref.at[part], sems.at[n, 1])
        else:
            weight = copy(up_any.at[:, part], up_ref.at[:, part], sems.at[n, 1])
        return (
            copy(units_any.at[which, :, part], units_ref.at[which, :, part], sems.at[n, 0]),
            weight,
        )

    rest = (
        copy(middle_any, middle_ref, sems.at[2 * DEPTHS, 0]),
        copy(cotangent_any.at[place_ref[0]], cotangent_ref, sems.at[2 * DEPTHS, 1]),
    )
    for n in range(2 * DEPTHS):
        for one in fetch(n):
            one.start()
    for one in rest:
        one.start()
    for n in range(2 * DEPTHS):
        which, c = divmod(n, DEPTHS)
        part = slice(c * DEPTH, (c + 1) * DEPTH)
        for one in fetch(n):
            one.wait()
        ref = second_ref if which else total_ref
        if which:
            product = dot(units_ref[1, :, part], up_ref[:, part], 1, 1)
        else:
            product = dot(units_ref[0, :, part], down_ref[part, :], 1, 0)
        if c:
            ref[...] += product
        else:
            ref[...] = product
    for one in rest:
        one.wait()
    alive, hat = scalars_ref[0], scalars_ref[1]
    gain_grad_ref[...] = jnp.zeros_like(gain_grad_ref)
    bias_grad_ref[...] = jnp.zeros_like(bias_grad_ref)
    out_grad_ref[...] = jnp.zeros_like(out_grad_ref)

    def chunk(rows):
        middle = middle_ref[rows, :]
        result_ref[rows, :] = (alive * (middle + total_ref[rows, :] + bias_ref[...])).astype(BF)
        xhat, inverse = normalized(middle)
        grad = second_ref[rows, :]
        gain_grad_ref[...] += jnp.sum(grad * xhat, axis=0, keepdims=True)
        bias_grad_ref[...] += jnp.sum(grad, axis=0, keepdims=True)
        out = cotangent_ref[rows, :].astype(F32) * hat
        out_grad_ref[...] += jnp.sum(out, axis=0, keepdims=True)
        whole = out + norm_back(xhat, inverse, gain_ref[...], grad)
        grad_ref[rows, :] = whole
        branch_ref[rows, :] = whole.astype(BF)

    row_chunks(chunk)


def contract(place, scalars, units, up, down, middle, cotangent, gain, bias):
    return pl.pallas_call(
        contract_kernel,
        out_shape=(
            shape((PATCHES, D), BF),
            shape((PATCHES, D), F32),
            shape((PATCHES, D), BF),
            shape((1, D), F32),
            shape((1, D), F32),
            shape((1, D), F32),
        ),
        in_specs=[SMEM, SMEM, VMEM, VMEM] + [ANYWHERE] * 5,
        out_specs=(VMEM,) * 6,
        scratch_shapes=[
            pltpu.VMEM((2, PATCHES, FF), BF),
            pltpu.VMEM((D, FF), BF),
            pltpu.VMEM((FF, D), BF),
            pltpu.VMEM((PATCHES, D), F32),
            pltpu.VMEM((PATCHES, D), BF),
            pltpu.VMEM((PATCHES, D), F32),
            pltpu.VMEM((PATCHES, D), F32),
            pltpu.SemaphoreType.DMA((2 * DEPTHS + 1, 2)),
        ],
        compiler_params=params(),
        cost_estimate=cost(),
        name="contract",
    )(place, scalars, gain, bias, units, up, down, middle, cotangent)


def attend_back_kernel(
    place_ref,
    grad_ref,
    branch_ref,
    proj_ref,
    lse_ref,
    tokens_ref,
    gain_ref,
    attend_ref,
    merge_ref,
    *refs,
):
    brought = [(refs[2 * n], refs[2 * n + 1]) for n in range(4)]
    outs = refs[8 + TOKENS_BACK :]
    keep_ref, send_ref, token_grad_ref, gain_grad_ref, bias_grad_ref = outs[:5]
    weight_ref, context_ref, first_ref, proj_grad_ref, sems = outs[5:]
    wait = section_copies(
        place_ref,
        1,
        [merge_ref] + [attend_ref.at[j] for j in range(3)],
        brought[3:] + brought[:3],
        [weight_ref.at[j] for j in range(4)],
        sems,
    )
    wait(0)
    branch = branch_ref[...]

    def context_tile(columns):
        context_ref[:, columns] = dot(branch, weight_ref[0, columns, :], 1, 1).astype(BF)

    column_tiles(256, context_tile)
    lane = lax.broadcasted_iota(jnp.int32, (PATCHES, LANES), 1)

    def pair(i, carry):
        columns = pl.ds(pl.multiple_of(i * LANES, LANES), LANES)
        queries = proj_ref[0, :, columns]
        keys = proj_ref[1, :, columns]
        values = proj_ref[2, :, columns]
        grads = context_ref[:, columns]
        keys_turned = keys.T
        blank = jnp.zeros_like(keys)
        query_grads, key_grads, value_grads = [], [], []
        for side in range(2):
            inside = (lane < HDIM) if side == 0 else (lane >= HDIM)
            key = jnp.where(inside, keys * HDIM ** (-0.5), blank).astype(BF)
            value = jnp.where(inside, values, blank)
            probs = jnp.exp(dot(key, queries, 1, 1) - lse_ref[i, side : side + 1, :])
            share_grad = dot(value, grads, 1, 1)
            weighted = probs * share_grad
            inner = jnp.sum(weighted, axis=0, keepdims=True)
            score_low = (weighted - probs * inner).astype(BF)
            value_grads.append(dot(probs.astype(BF), grads, 1, 0))
            key_grads.append(dot(score_low, queries, 1, 0))
            query_grads.append(
                dot(keys_turned[side * HDIM : (side + 1) * HDIM], score_low, 1, 0)
            )
        low = lane < HDIM
        query_grad = jnp.concatenate(query_grads, axis=0) * HDIM ** (-0.5)
        proj_grad_ref[0, :, columns] = query_grad.T.astype(BF)
        proj_grad_ref[1, :, columns] = (
            jnp.where(low, key_grads[0], key_grads[1]) * HDIM ** (-0.5)
        ).astype(BF)
        proj_grad_ref[2, :, columns] = jnp.where(low, value_grads[0], value_grads[1]).astype(BF)
        return carry

    lax.fori_loop(0, PAIRS, pair, 0)
    core = place_ref[1]
    owns = pl.ds(pl.multiple_of(core * HALF, HALF), HALF)
    others = pl.ds(pl.multiple_of((1 - core) * HALF, HALF), HALF)
    for j in range(3):
        keep_ref[j] = proj_grad_ref[j, :, owns]
        send_ref[j] = proj_grad_ref[j, :, others]
    keep_ref[3] = branch_ref[:, owns]
    send_ref[3] = branch_ref[:, others]
    for j in range(3):
        wait(j + 1)

    def first_tile(columns):
        total = dot(proj_grad_ref[0], weight_ref[1, columns, :], 1, 1)
        for j in range(1, 3):
            total = total + dot(proj_grad_ref[j], weight_ref[j + 1, columns, :], 1, 1)
        first_ref[:, columns] = total

    column_tiles(256, first_tile)
    gain_grad_ref[...] = jnp.zeros_like(gain_grad_ref)
    bias_grad_ref[...] = jnp.zeros_like(bias_grad_ref)

    def chunk(rows):
        xhat, inverse = normalized(tokens_ref[rows, :].astype(F32))
        grad = first_ref[rows, :]
        gain_grad_ref[...] += jnp.sum(grad * xhat, axis=0, keepdims=True)
        bias_grad_ref[...] += jnp.sum(grad, axis=0, keepdims=True)
        token_grad_ref[rows, :] = (
            grad_ref[rows, :] + norm_back(xhat, inverse, gain_ref[0:1, :], grad)
        ).astype(BF)

    row_chunks(chunk)


def attend_back(
    place, grad, branch, proj, lse, tokens, gain, own_attend, own_merge, brought, after
):
    return pl.pallas_call(
        attend_back_kernel,
        out_shape=(
            shape((4, PATCHES, HALF), BF),
            shape((4, PATCHES, HALF), BF),
            shape((PATCHES, D), BF),
            shape((1, D), F32),
            shape((1, D), F32),
        ),
        in_specs=[SMEM] + [VMEM] * 6 + [ANYWHERE] * (10 + TOKENS_BACK),
        out_specs=(VMEM,) * 5,
        scratch_shapes=[
            pltpu.VMEM((4, D, D), BF),
            pltpu.VMEM((PATCHES, D), BF),
            pltpu.VMEM((PATCHES, D), F32),
            pltpu.VMEM((3, PATCHES, D), BF),
            pltpu.SemaphoreType.DMA((4, 4)),
        ],
        compiler_params=params(),
        cost_estimate=cost(),
        name="attend_back",
    )(place, grad, branch, proj, lse, tokens, gain, own_attend, own_merge, *brought, *after)


MIX_AT = PATCHES
SMALL_AT = PATCHES + TABLE_PAD
KEYS_AT = SMALL_AT + 16
TAIL = KEYS_AT + ROWS_TABLE


def aggregate_back_kernel(
    place_ref,
    alive_ref,
    token_grad_ref,
    pixels_ref,
    keys_ref,
    tvt_ref,
    shares_ref,
    gain_first_ref,
    gain_second_ref,
    bias_first_ref,
    bias_second_ref,
    output_ref,
    hidden_ref,
    own_ref,
    brought_ref,
    beside_ref,
    keep_ref,
    send_ref,
    field_ref,
    key_grad_ref,
    head_ref,
    merge_ref,
    mix_ref,
    pixel_grad_ref,
    grid_ref,
    sems,
):
    wait = section_copies(
        place_ref, 0, [own_ref], [(brought_ref, beside_ref)], [merge_ref], sems
    )
    core = place_ref[1]
    owns = pl.ds(pl.multiple_of(core * HALF, HALF), HALF)
    others = pl.ds(pl.multiple_of((1 - core) * HALF, HALF), HALF)
    alive = alive_ref[0]
    pre = (token_grad_ref[...].astype(F32) * alive).astype(BF)
    keep_ref[:PATCHES, :] = (token_grad_ref[:, owns].astype(F32) * alive).astype(BF)
    send_ref[:PATCHES, :] = (token_grad_ref[:, others].astype(F32) * alive).astype(BF)
    wait(0)

    def head_tile(rows):
        head_ref[rows, :] = dot(merge_ref[rows, :], pre, 1, 1).astype(BF)

    column_tiles(256, head_tile)
    pixel_grad_ref[...] = jnp.zeros_like(pixel_grad_ref)
    key_grad_ref[...] = jnp.zeros_like(key_grad_ref)
    lane = lax.broadcasted_iota(jnp.int32, (VARS, HEADS), 1)

    def head(h, carry):
        rows = pl.ds(pl.multiple_of(h * HDIM, HDIM), HDIM)
        keys = head_keys(keys_ref, h)
        grads = head_ref[rows, :]
        shares = shares_ref[h]
        mix_ref[rows, :] = dot(grads, mixed_rows(shares, pixels_ref), 1, 1)
        row_grads = dot(tvt_ref[rows, :], grads, 0, 0)
        share_grads = row_grads[PIECES * VARS : ROWS_TABLE]
        for k in range(PIECES):
            share_grads = share_grads + row_grads[k * VARS : (k + 1) * VARS] * pixels_ref[k]
        inner = jnp.sum(shares * share_grads, axis=0, keepdims=True)
        scores = shares * (share_grads - inner)
        for k in range(PIECES + 1):
            piece = slice(k * VARS, (k + 1) * VARS)
            if k < PIECES:
                pixel_grad_ref[k] += shares * row_grads[piece] + scores * keys[piece]
                total = jnp.sum(scores * pixels_ref[k], axis=1, keepdims=True)
            else:
                total = jnp.sum(scores, axis=1, keepdims=True)
            key_grad_ref[piece, :] += jnp.where(lane == h, total, 0.0)
        return carry

    lax.fori_loop(0, HEADS, head, 0)
    for ref, start in ((keep_ref, core * HALF), (send_ref, (1 - core) * HALF)):
        for part in range(2):
            rows = pl.ds(pl.multiple_of(start + part * TABLE_PAD, TABLE_PAD), TABLE_PAD)
            ref[MIX_AT:SMALL_AT, part * TABLE_PAD : (part + 1) * TABLE_PAD] = mix_ref[
                rows, :
            ].astype(BF)
        columns = pl.ds(pl.multiple_of(start, HALF), HALF)
        small = [
            one[:, columns]
            for one in (
                gain_first_ref,
                gain_second_ref,
                bias_first_ref,
                bias_second_ref,
                output_ref,
            )
        ]
        for part in range(FF // D):
            small.append(hidden_ref[:, pl.ds(pl.multiple_of(part * D + start, HALF), HALF)])
        small.append(jnp.zeros((16 - len(small), HALF), F32))
        ref[SMALL_AT:KEYS_AT, :] = jnp.concatenate(small, axis=0).astype(BF)
        ref[KEYS_AT:, :] = jnp.concatenate(
            [key_grad_ref[...], jnp.zeros((ROWS_TABLE, HALF - HEADS), F32)], axis=1
        ).astype(BF)
    low_lane = lax.broadcasted_iota(jnp.int32, (VARS, COLS), 1) < COLS // 2
    for a in range(PATCH):
        for j in range(PATCHES // COLS):
            columns = slice(j * COLS, (j + 1) * COLS)
            low, high = pixel_grad_ref[2 * a, :, columns], pixel_grad_ref[2 * a + 1, :, columns]
            even = jnp.where(low_lane, low, pltpu.roll(high, COLS // 2, 1))
            odd = jnp.where(low_lane, pltpu.roll(low, COLS // 2, 1), high)
            grid_ref[pl.ds(4 * j + a, VARS, stride=STRIPES), :] = even
            grid_ref[pl.ds(4 * j + 2 + a, VARS, stride=STRIPES), :] = odd
    field_ref[...] = exact(grid_ref[...], column_order(), 1)


def aggregate_back(place, alive, token_grad, pixels, keys, tvt, shares, small, merge):
    return pl.pallas_call(
        aggregate_back_kernel,
        out_shape=(
            shape((TAIL, HALF), BF),
            shape((TAIL, HALF), BF),
            shape((VARS * STRIPES, COLS), F32),
        ),
        in_specs=[SMEM, SMEM] + [VMEM] * 11 + [ANYWHERE] * 3,
        out_specs=(VMEM,) * 3,
        scratch_shapes=[
            pltpu.VMEM((ROWS_TABLE, HEADS), F32),
            pltpu.VMEM((D, PATCHES), BF),
            pltpu.VMEM((D, D), BF),
            pltpu.VMEM((D, TABLE_PAD), F32),
            pltpu.VMEM((PIECES, VARS, PATCHES), F32),
            pltpu.VMEM((VARS * STRIPES, COLS), F32),
            pltpu.SemaphoreType.DMA((1, 4)),
        ],
        compiler_params=params(),
        cost_estimate=cost(),
        name="aggregate_back",
    )(place, alive, token_grad, pixels, keys, tvt, shares, *small, *merge)


BLOCKS = 16
BLOCK = FF // BLOCKS
SPANS = BLOCKS // 2
SPAN = 4 * BLOCK


def wide_kernel(which, by_pipe, place_ref, left_any, own_any, beside_any, *refs):
    send_any, keep_any, left_ref, turned_ref, right_ref, product_ref, sems, out_sems = refs[-8:]
    place, core = place_ref[0], place_ref[1]
    side, z_low = jnp.bitwise_and(place, 1), jnp.bitwise_and(lax.shift_right_logical(place, 1), 1)

    def fetch(i):
        columns = aligned(jnp.bitwise_xor(3 - i, lax.shift_right_logical(place, 2)), SPAN)
        return [
            copy(
                source.at[which, :, columns],
                right_ref.at[i, pl.ds(n * PATCHES, PATCHES)],
                sems.at[i, n],
            )
            for n, source in enumerate((own_any, beside_any))
        ]

    lefts = (
        copy(left_any.at[:, aligned(core, HALF)], left_ref.at[0], sems.at[4, 0]),
        copy(beside_any.at[which, :, pl.ds(FF, HALF)], left_ref.at[1], sems.at[4, 1]),
    )
    for one in lefts:
        one.start()
    for i in range(4):
        for one in fetch(i):
            one.start()
    for n, one in enumerate(lefts):
        one.wait()
        turned_ref[:, n * PATCHES : (n + 1) * PATCHES] = left_ref[n].T

    def put(i, block):
        source = product_ref.at[i % 2, :, pl.ds(block * BLOCK, BLOCK)]
        return source, out_sems.at[i % 2, block]

    def wait(i):
        for block in range(4):
            source, sem = put(i, block)
            copy(source, send_any.at[0, 0, 0], sem).wait()

    for i in range(4):
        for one in fetch(i):
            one.wait()
        if i >= 2:
            wait(i - 2)
        product_ref[i % 2] = dot(turned_ref[...], right_ref[i], 1, 0).astype(BF)
        pipe, z_high = divmod(3 - i, 2)
        for block in range(4):
            source, sem = put(i, block)
            to_side = jnp.bitwise_xor(block % 2, side)
            to_z = jnp.bitwise_xor(block // 2, z_low)
            if by_pipe:
                target = send_any if pipe else keep_any
                copy(source, target.at[to_side, z_high, to_z], sem).start()
            else:
                start_either(
                    to_side == 1,
                    source,
                    send_any.at[pipe, z_high, to_z],
                    keep_any.at[pipe, z_high, to_z],
                    sem,
                )
    wait(2)
    wait(3)


def wide_grads(place, left, right, which, by_pipe, after, name):
    return pl.pallas_call(
        functools.partial(wide_kernel, which, by_pipe),
        in_specs=[SMEM] + [ANYWHERE] * (3 + len(after)),
        out_specs=(ANYWHERE, ANYWHERE),
        out_shape=(shape((2, 2, 2, HALF, BLOCK), BF), shape((2, 2, 2, HALF, BLOCK), BF)),
        scratch_shapes=[
            pltpu.VMEM((2, PATCHES, HALF), BF),
            pltpu.VMEM((HALF, 2 * PATCHES), BF),
            pltpu.VMEM((4, 2 * PATCHES, SPAN), BF),
            pltpu.VMEM((2, HALF, SPAN), BF),
            pltpu.SemaphoreType.DMA((5, 2)),
            pltpu.SemaphoreType.DMA((2, 4)),
        ],
        compiler_params=params(),
        cost_estimate=cost(),
        name=name,
    )(place, left, *right, *after)


ROWS = D // SPANS
PARTS = 2 * ROWS


def square_kernel(
    place_ref,
    tail_own,
    tail_beside,
    heads_own,
    heads_beside,
    pack_own,
    pack_beside,
    right_own,
    right_beside,
    *refs,
):
    send_any, keep_any, cross_send_any, cross_keep_any = refs[-9:-5]
    left_ref, right_ref, product_ref, sems, out_sems = refs[-5:]
    pipe, place = place_ref[0], place_ref[1]
    side, z = jnp.bitwise_and(place, 1), lax.shift_right_logical(place, 1)
    lefts = [
        (pack_own.at[pl.ds(0, D)], pack_beside.at[pl.ds(0, D)]),
        (pack_own.at[pl.ds(D, D)], pack_beside.at[pl.ds(D, D)]),
        (heads_own, heads_beside),
    ]
    left_copies = [
        [
            copy(one, left_ref.at[n, :, pl.ds(m * PATCHES, PATCHES)], sems.at[n, m])
            for m, one in enumerate(pair)
        ]
        for n, pair in enumerate(lefts)
    ]
    right_copies = [
        [
            copy(one.at[n], right_ref.at[n, pl.ds(m * PATCHES, PATCHES)], sems.at[3 + n, m])
            for m, one in enumerate((right_own, right_beside))
        ]
        for n in range(4)
    ]
    for n in (0, 3, 1, 2):
        for one in (left_copies[n] if n < 3 else []) + right_copies[n]:
            one.start()
    right_ref[4, :PATCHES] = tail_own[:PATCHES]
    right_ref[4, PATCHES:] = tail_beside[:PATCHES]

    def put(slot, block):
        return product_ref.at[slot, pl.ds(block * ROWS, ROWS)], out_sems.at[slot, block]

    def wait(slot):
        for block in range(SPANS):
            source, sem = put(slot, block)
            copy(source, send_any.at[0, pl.ds(0, ROWS)], sem).wait()

    def share(slot, part):
        rows = pl.ds(part * ROWS, ROWS)
        for block in range(SPANS):
            source, sem = put(slot, block)
            to_z = jnp.bitwise_xor(block // 2, z)
            start_either(
                side != block % 2, source, send_any.at[to_z, rows], keep_any.at[to_z, rows], sem
            )

    def cross(slot, part, goal):
        rows = pl.ds(part * ROWS, ROWS)
        for block in range(SPANS):
            source, sem = put(slot, block)
            to_side = jnp.bitwise_xor(block % 2, side)
            to_z = jnp.bitwise_xor(block // 2, z)
            start_either(
                pipe != goal,
                source,
                cross_send_any.at[to_side, to_z, rows],
                cross_keep_any.at[to_side, to_z, rows],
                sem,
            )

    product_ref[0] = (tail_own[...].astype(F32) + tail_beside[...].astype(F32)).astype(BF)
    share(0, 1)
    for step, (left, right) in enumerate(((0, 0), (1, 3), (2, 4), (0, 1), (0, 2))):
        slot = (step + 1) % 2
        if step in (0, 1, 2):
            for one in left_copies[left]:
                one.wait()
        if right < 4:
            for one in right_copies[right]:
                one.wait()
        if step >= 1:
            wait(slot)
        for tile in range(2):
            rows = slice(tile * HALF, (tile + 1) * HALF)
            product_ref[slot, rows] = dot(left_ref[left, rows], right_ref[right], 1, 0).astype(BF)
        if step == 0:
            share(slot, 0)
        elif step == 1:
            cross(slot, 0, 1)
        elif step == 2:
            cross(slot, 0, 0)
        else:
            cross(slot, 1, step - 3)
    wait(0)
    wait(1)


def square_grads(place, tail, heads, pack, right, after):
    return pl.pallas_call(
        square_kernel,
        in_specs=[SMEM, VMEM, VMEM] + [ANYWHERE] * (6 + len(after)),
        out_specs=(ANYWHERE,) * 4,
        out_shape=(
            shape((4, PARTS, HALF), BF),
            shape((4, PARTS, HALF), BF),
            shape((2, 4, PARTS, HALF), BF),
            shape((2, 4, PARTS, HALF), BF),
        ),
        scratch_shapes=[
            pltpu.VMEM((3, D, 2 * PATCHES), BF),
            pltpu.VMEM((5, 2 * PATCHES, HALF), BF),
            pltpu.VMEM((2, D, HALF), BF),
            pltpu.SemaphoreType.DMA((7, 2)),
            pltpu.SemaphoreType.DMA((2, SPANS)),
        ],
        compiler_params=params(),
        cost_estimate=cost(),
        name="square_grads",
    )(place, *tail, *heads, *pack, *right, *after)


def finish_kernel(
    chips,
    place_ref,
    tail_ref,
    table_ref,
    weight_ref,
    position_ref,
    mix_ref,
    small_ref,
    keys_ref,
    key_query_ref,
    low_ref,
    query_ref,
    whole_ref,
):
    pipe, core, chip = place_ref[0], place_ref[1], place_ref[2]
    part = TAIL // (2 * chips)
    for c in range(2):
        for n in range(chips):
            for p in range(2):
                start = (2 * n + p) * part
                whole_ref[c, start : start + part, :] = tail_ref[
                    jnp.bitwise_xor(c, core), jnp.bitwise_xor(n, chip), jnp.bitwise_xor(p, pipe)
                ].astype(F32)
    for c in range(2):
        columns = slice(c * HALF, (c + 1) * HALF)
        position_ref[:, columns] = whole_ref[c, :PATCHES, :]
        small_ref[:, columns] = whole_ref[c, SMALL_AT:KEYS_AT, :]
        for n in range(2):
            start = c * HALF + n * TABLE_PAD
            mix_ref[start : start + TABLE_PAD, :] = whole_ref[
                c, MIX_AT:SMALL_AT, n * TABLE_PAD : (n + 1) * TABLE_PAD
            ]
    keys = whole_ref[0, KEYS_AT:, :HEADS]
    keys_ref[...] = keys
    grads = lax.dot_general(
        keys,
        table_ref[...].astype(F32),
        (((0,), (0,)), ((), ())),
        precision=PRECISE,
        preferred_element_type=F32,
    ).astype(BF)
    key_query_ref[...] = grads.astype(F32)
    low = jnp.where(head_rows(D), dot(grads, weight_ref[1], 1, 0), 0.0)
    low = jnp.sum(low, axis=0, keepdims=True) * HDIM ** (-0.5)
    low = jnp.broadcast_to(low, (HEADS, D)).astype(BF)
    low_ref[...] = low.astype(F32)
    query_ref[...] = dot(low, weight_ref[0], 1, 1)


def finish(place, tail, table, weights, chips):
    return pl.pallas_call(
        functools.partial(finish_kernel, chips),
        out_shape=(
            shape((PATCHES, D), F32),
            shape((D, TABLE_PAD), F32),
            shape((16, D), F32),
            shape((ROWS_TABLE, HEADS), F32),
            shape((HEADS, D), F32),
            shape((HEADS, D), F32),
            shape((HEADS, D), F32),
        ),
        in_specs=[SMEM] + [VMEM] * 3,
        out_specs=(VMEM,) * 7,
        scratch_shapes=[pltpu.VMEM((2, TAIL, HALF), F32)],
        compiler_params=params(),
        cost_estimate=cost(),
        name="finish",
    )(place, tail, table, weights)


def partner(block, axis, distance):
    size = lax.axis_size(axis)
    return lax.ppermute(block, axis, [(i, i ^ distance) for i in range(size)])


def swap(block):
    return partner(block, "pipe", 1)


def pick(array, index, axis=0):
    return lax.dynamic_index_in_dim(array, index, axis, keepdims=False)


def tree_sum(terms):
    while len(terms) > 1:
        terms = [terms[2 * i] + terms[2 * i + 1] for i in range(len(terms) // 2)]
    return terms[0]


class Places:
    def __init__(self):
        self.pipe = lax.axis_index("pipe")
        self.dp = lax.axis_index("dp")
        self.size = lax.axis_size("dp")
        self.core = self.dp % 2
        self.chips = self.size // 2
        bits = self.size.bit_length() - 2
        low = bits % 2 if bits % 2 else 2
        self.groups = []
        at = 1
        while bits > 0:
            width = low if at == 1 else 2
            self.groups.append((at, width))
            at += width
            bits -= width

    def relative(self, array, place):
        for bit in range(array.shape[0].bit_length() - 1):
            paired = array.reshape(-1, 2, 2**bit, *array.shape[1:])
            flipped = jnp.where((place // 2**bit) % 2 == 1, paired[:, ::-1], paired)
            array = flipped.reshape(array.shape)
        return array

    def grouped(self, array):
        counts = [2**width for _, width in reversed(self.groups)]
        dims = array.shape[1:]
        array = array.reshape(*counts, *dims)
        order = list(range(len(counts)))[::-1] + list(range(len(counts), array.ndim))
        return array.transpose(order)

    def reduced(self, array, groups):
        for n, (at, width) in enumerate(groups):
            terms = [array[0].astype(F32)]
            for distance in range(1, 2**width):
                terms.append(partner(array[distance], "dp", distance * 2**at).astype(F32))
            array = tree_sum(terms)
            if n < len(groups) - 1:
                array = array.astype(BF)
        return array

    def over_cores(self, array):
        brought = partner(pick(array, 1 - self.core).astype(BF), "dp", 1).astype(F32)
        own = pick(array, self.core)
        return jnp.concatenate(
            [jnp.where(self.core == 0, own, brought), jnp.where(self.core == 0, brought, own)],
            axis=-1,
        )

    def gather(self, block):
        blocks = block[None]
        for at, width in reversed(self.groups):
            parts = [partner(blocks, "dp", m * 2**at) for m in range(1, 2**width)]
            blocks = jnp.stack([blocks] + parts, axis=1).reshape(-1, *block.shape)
        return blocks

    def total(self, block):
        for bit in range(self.size.bit_length() - 1):
            block = block + partner(block, "dp", 2**bit)
        return block


def on_device(
    fields,
    item_weights,
    live_counts,
    running_stats,
    embed_weight,
    variable_embed,
    variable_query,
    attend_weight,
    merge_weight,
    position_embed,
    norm_gain,
    norm_bias,
    up_weight,
    hidden_bias,
    down_weight,
    output_bias,
    cotangent,
):
    at = Places()
    pipe, core = at.pipe, at.core
    first = pipe == 0
    side = (at.dp // 2) % 2
    chip = at.dp // 2
    place = jnp.stack([pipe, core, side]).astype(jnp.int32)
    micro, half_vars, rows, cols = fields.shape
    scale_heads = HDIM ** (-0.5)

    own_attend, own_merge = attend_weight[0], merge_weight[0]

    def quarter(weight):
        return lax.dynamic_slice_in_dim(weight, (2 * core + side) * QUARTER, QUARTER, 0)

    def quarter_of(j):
        start = (jnp.int32(j), (2 * core + side) * QUARTER, jnp.int32(0))
        return lax.dynamic_slice(own_attend, start, (1, QUARTER, D))[0]

    def passed_on(block):
        pair = jnp.stack([block, partner(block, "dp", 2)])
        return pair, partner(pair, "dp", 1)

    def after(value, *others):
        return lax.optimization_barrier((value, others))[0]

    chunk_first = swap(jnp.where(first, quarter(own_merge), quarter_of(0)))

    flat_fields = fields.reshape(micro, half_vars * rows, cols)
    other_fields = swap(pick(flat_fields, 1 - pipe))
    own_fields = pick(flat_fields, pipe)
    slots = jnp.arange(micro, dtype=jnp.int32)
    alive = (slots < live_counts[0]).astype(F32)
    omega = item_weights.astype(F32) * alive
    plain_sums = jnp.sum(fields, axis=(2, 3))
    square_sums = jnp.sum(fields * fields, axis=(2, 3))
    sums = jnp.concatenate(
        [
            jnp.sum(omega[:, None] * plain_sums, axis=0),
            jnp.sum(omega[:, None] * square_sums, axis=0),
            jnp.sum(omega)[None],
            jnp.sum(alive)[None],
        ]
    )
    sums = at.total(sums)
    total, live_total = sums[2 * half_vars], sums[2 * half_vars + 1]
    first_moment = sums[:half_vars] / (total * rows * cols)
    second_moment = sums[half_vars : 2 * half_vars] / (total * rows * cols)
    center_new = (1.0 - MOMENTUM) * running_stats[0] + MOMENTUM * first_moment
    spread_new = (1.0 - MOMENTUM) * running_stats[1] + MOMENTUM * (
        second_moment - first_moment * first_moment
    )
    statistics = jnp.stack([center_new, spread_new])
    other_statistics = swap(statistics)
    all_statistics = jnp.concatenate(
        [
            jnp.where(first, statistics, other_statistics),
            jnp.where(first, other_statistics, statistics),
        ],
        axis=1,
    )
    center = all_statistics[0].reshape(VARS, 1)
    scale = lax.rsqrt(all_statistics[1] + EPSILON).reshape(VARS, 1)
    weight_hat = pick(omega, pipe) * live_total / total
    alive_own = pick(alive, pipe)[None]
    out_low = (pick(cotangent, pipe).astype(F32) * weight_hat).astype(BF)

    table = jnp.concatenate(
        [embed_weight.transpose(1, 0, 2).reshape(VARS * PIECES, D), variable_embed], axis=0
    )
    query, table_keys, table_value = tables(
        variable_query.astype(F32).reshape(1, D), table, own_attend
    )

    def from_first(block):
        return jnp.where(first, block, lax.ppermute(block, "pipe", [(0, 1)]))

    tvt = from_first(table_value.astype(BF))
    keys = from_first(table_keys)

    chunk = chunk_first
    passed = [passed_on(chunk)]
    chunks = [chunk]
    chunk = swap(after(jnp.where(first, quarter_of(2), quarter_of(1)), chunk))
    passed.append(passed_on(chunk))
    chunk = lax.ppermute(after(quarter_of(2), chunk, passed[0][0]), "pipe", [(1, 0)])
    passed.append(passed_on(chunk))
    chunk = lax.ppermute(after(quarter(own_merge), chunk, passed[1][0]), "pipe", [(1, 0)])
    passed.append(passed_on(chunk))
    brought = [block for pair in passed for block in pair]

    tokens, heads, shares, pixels = aggregate(
        place,
        alive_own,
        own_fields,
        other_fields,
        center,
        scale,
        keys,
        tvt,
        position_embed,
        (own_merge, *passed[0]),
    )
    heads_beside = partner(heads, "dp", 1)
    pack, proj, lse = attend(place, tokens, norm_gain, norm_bias, own_attend, brought[:6])
    middle, second_low = merge(
        place, tokens, pack, norm_gain, norm_bias, (own_merge, *brought[6:])
    )
    pack_beside = partner(pack, "dp", 1)
    units, hidden_sum = expand(
        place, second_low, out_low, up_weight, hidden_bias, down_weight, heads_beside
    )
    units_beside = partner(units, "dp", 1)
    scalars = jnp.stack([alive_own[0], weight_hat])
    result, middle_grad, branch_low, gain_second, bias_second, output_sum = contract(
        place,
        scalars,
        units,
        up_weight,
        down_weight,
        middle,
        cotangent,
        norm_gain[1:2],
        output_bias.reshape(1, D),
    )
    ff_width = FF // (2 * at.size)
    d_width = D // at.size
    direct = 2 * at.chips == BLOCKS
    wide_place = jnp.stack([pipe * SPANS + chip if direct else 0 * chip, core]).astype(jnp.int32)
    square_place = jnp.stack([pipe, chip if direct else 0 * chip]).astype(jnp.int32)
    both_units = (units, units_beside)
    down_send, down_keep = wide_grads(
        wide_place,
        out_low,
        both_units,
        0,
        True,
        (branch_low,),
        "down_grads",
    )
    up_send, up_keep = wide_grads(
        wide_place,
        second_low,
        both_units,
        1,
        False,
        (down_keep,),
        "up_grads",
    )
    right_own, right_send, token_grad, gain_first, bias_first = attend_back(
        place,
        middle_grad,
        branch_low,
        proj,
        lse,
        tokens,
        norm_gain,
        own_attend,
        own_merge,
        brought,
        (down_keep, up_keep),
    )
    right_beside = partner(right_send, "dp", 1)
    tail_own, tail_send, field_grads = aggregate_back(
        place,
        alive_own,
        token_grad,
        pixels,
        keys,
        tvt,
        shares,
        (gain_first, gain_second, bias_first, bias_second, output_sum, hidden_sum),
        (own_merge, *passed[0]),
    )
    tail_beside = partner(tail_send, "dp", 1)

    if direct:
        groups = at.groups[1:]
        down_sum = after(down_keep, tail_own).astype(F32) + swap(down_send).astype(F32)
        down_sum = down_sum.astype(BF).reshape(2, 4, HALF, BLOCK)
        up_sum = after(up_keep, tail_own).astype(F32) + partner(up_send, "dp", 2).astype(F32)
        up_sum = up_sum.astype(BF).reshape(2, 4, HALF, BLOCK)
        down_brought = partner(down_sum[1], "dp", 2)
        up_brought = swap(up_sum[1])
        started = (down_sum, up_sum)
    else:
        groups = at.groups
        started = (down_keep, up_keep)

        def spread(array):
            array = array.transpose(4, 0, 1, 2, 3, 5).reshape(HALF, 2 * at.chips, -1)
            array = at.relative(array.transpose(1, 0, 2), pipe * at.chips + chip)
            array = array.reshape(2, at.chips, HALF, -1)
            total = array[0].astype(F32) + swap(array[1]).astype(F32)
            return at.grouped(total.astype(BF))

        down_wide = jnp.stack([down_keep, down_send]).transpose(0, 2, 3, 1, 4, 5)
        wide = [spread(down_wide), spread(jnp.stack([up_keep, up_send], axis=3))]

    send, keep, cross_send, cross_keep = square_grads(
        square_place,
        (tail_own, tail_beside),
        (heads, heads_beside),
        (pack, pack_beside),
        (right_own, right_beside),
        started,
    )
    if direct:
        wide = [
            (down_sum[0].astype(F32) + after(down_brought, send).astype(F32)).astype(BF),
            (up_sum[0].astype(F32) + after(up_brought, send).astype(F32)).astype(BF),
        ]
        wide = jnp.stack(wide, axis=1)
        shared = partner(after(send, wide), "dp", 2)
        crossed = swap(after(cross_send, wide))
        cross = (cross_keep.astype(F32) + crossed.astype(F32)).astype(BF)
        cross_brought = partner(cross[1], "dp", 2)
        keep = after(keep, cross)
        square = (keep.astype(F32) + shared.astype(F32)).astype(BF)
        cross = (cross[0].astype(F32) + after(cross_brought, square).astype(F32)).astype(BF)
        square = jnp.concatenate([square, cross], axis=1)
        wide = at.reduced(wide, groups)
        square = at.reduced(after(square, wide), groups)
        field_grads, result = after((field_grads, result), cross_brought)
    else:
        wide = jnp.stack([at.reduced(array, groups) for array in wide])

        def rows_of(array):
            return at.relative(array.reshape(at.chips, -1, HALF), chip)

        whole = jnp.stack([keep, send], axis=1).reshape(SPANS, PARTS, HALF)
        cross = (cross_keep.astype(F32) + swap(cross_send).astype(F32)).astype(BF)
        cross = cross.transpose(1, 0, 2, 3).reshape(SPANS, PARTS, HALF)
        square = [
            rows_of(array[:, n * ROWS : (n + 1) * ROWS]) for array in (whole, cross) for n in (0, 1)
        ]
        square = at.reduced(at.grouped(jnp.concatenate(square, axis=1)), groups)

    wide = wide.reshape(2, HALF, 2, ff_width)
    other = partner(pick(wide, 1 - core, 2).astype(BF), "dp", 1).astype(F32)
    own = pick(wide, core, 2)
    wide = jnp.concatenate(
        [jnp.where(core == 0, own, other), jnp.where(core == 0, other, own)], axis=1
    )
    down_part, up_part = wide[0].T, wide[1]

    lot = 2 * d_width
    part = TAIL // (2 * at.chips)
    query_part = square[:lot]
    tail = square[lot : lot + 2 * part]
    merge_sum = square[lot + 2 * part : 2 * lot + 2 * part]
    cross = square[2 * lot + 2 * part :]
    sent = jnp.concatenate(
        [query_part, cross, jnp.where(first, tail[part:], tail[:part])], axis=0
    ).astype(BF)
    came = swap(sent).astype(F32)
    section_sum = jnp.stack(
        [merge_sum, query_part + came[:lot], came[lot : 2 * lot], cross]
    )
    tail = (jnp.where(first, tail[:part], tail[part:]) + came[2 * lot :]).astype(BF)
    section_sum = section_sum.reshape(4, 2, d_width, HALF).transpose(1, 0, 2, 3)
    section_part = at.over_cores(section_sum)
    merge_part = section_part[0]
    second_attend = section_part[1:]

    tail = at.gather(jnp.stack([tail, swap(tail)]))
    tail = jnp.stack([tail, partner(tail, "dp", 1)])
    spot = jnp.stack([pipe, core, chip]).astype(jnp.int32)
    position_sum, table_mix, small, key_grads, key_query_grads, query_low, query_sum = finish(
        spot, tail, table, own_attend, at.chips
    )
    table_mix = table_mix[:, :ROWS_TABLE].astype(BF)
    hidden_sum = small[5:9].reshape(FF)

    came = swap(jnp.where(first, result, tokens))
    outputs = jnp.stack([jnp.where(first, tokens, came), jnp.where(first, came, result)])
    field_halves = field_grads.reshape(2, half_vars, rows, cols)
    field_came = swap(pick(field_halves, 1 - pipe).astype(BF)).astype(F32)
    field_own = pick(field_halves, pipe)
    own_scale = lax.rsqrt(spread_new + EPSILON)
    field_out = (
        jnp.stack(
            [
                jnp.where(first, field_own, field_came),
                jnp.where(first, field_came, field_own),
            ]
        )
        * own_scale[None, :, None, None]
    )

    query_sum = from_first(query_sum[:1])
    own_rows = at.dp * d_width
    query_rows = lax.dynamic_slice_in_dim(variable_query, own_rows, d_width).astype(F32)
    key_rows = lax.dynamic_slice_in_dim(key_query_grads, own_rows, d_width, 1)
    key_rows = key_rows.T[:, :, None] * query[0].reshape(1, HEADS, HDIM) * scale_heads
    table_rows = lax.dynamic_slice_in_dim(table, own_rows, d_width, 1)
    first_attend = jnp.stack(
        [
            query_rows[:, None] * query_low[:1],
            key_rows.reshape(d_width, D),
            dot(table_rows, table_mix, 0, 1),
        ]
    )
    attend_part = jnp.where(first, first_attend, second_attend)

    value_pair = passed[1][0]
    value_pair = jnp.where(side == 0, value_pair, value_pair[::-1]).reshape(HALF, D)
    value_own = lax.dynamic_slice(own_attend, (jnp.int32(2), core * HALF, jnp.int32(0)), (1, HALF, D))
    value_own = jnp.where(first, value_own[0], value_pair)
    table_half = dot(table_mix, value_own, 0, 1)
    beside = partner(table_half, "dp", 1)
    key_query = tvt[:, ROWS_TABLE:].astype(F32)
    table_sum = jnp.concatenate(
        [jnp.where(core == 0, table_half, beside), jnp.where(core == 0, beside, table_half)],
        axis=1,
    ) + lax.dot_general(
        key_grads, key_query, (((1,), (1,)), ((), ())), precision=PRECISE
    )
    embed_grads = table_sum[: VARS * PIECES].reshape(PIECES, VARS, D).transpose(1, 0, 2)
    variable_grads = table_sum[VARS * PIECES :]
    hidden_part = lax.dynamic_slice_in_dim(
        hidden_sum, (pipe * at.size + at.dp) * ff_width, ff_width
    )
    return (
        statistics,
        outputs[None],
        field_out,
        embed_grads,
        variable_grads,
        query_sum.reshape(D),
        attend_part[None],
        merge_part[None],
        position_sum,
        small[0:2],
        small[2:4],
        up_part,
        hidden_part,
        down_part,
        small[4],
    )


def solution(mesh):
    return jax.shard_map(
        on_device,
        mesh=mesh,
        in_specs=(
            P("dp", "pipe", None, None),
            P("dp"),
            P("dp"),
            P(None, "pipe"),
            P(),
            P(),
            P(),
            P("pipe", None, None, None),
            P("pipe", None, None),
            P(),
            P(),
            P(),
            P(),
            P(),
            P(),
            P(),
            P("dp", None, None),
        ),
        out_specs=(
            P(None, "pipe"),
            P("pipe", "dp", None, None),
            P("dp", "pipe", None, None),
            P(),
            P(),
            P(),
            P("pipe", None, "dp", None),
            P("pipe", "dp", None),
            P(),
            P(),
            P(),
            P(None, ("pipe", "dp")),
            P(("pipe", "dp")),
            P(("pipe", "dp"), None),
            P(),
        ),
        check_vma=False,
    )
```

profile of v0, /device:TPU:0, one launch (start us, length us, event | category | flops | bytes accessed | tf_op | source)
XLA Modules:
  0.0 488.8 jit_solution(12963395466865338938)
XLA Ops:
  2.7 3.0 collective-permute-start.8
  10.3 5.7 %tables.1 = (f32[16,1024]{1,0:T(8,128)}, f32[240,16]{1,0:T(8,128)}, f32[1024,256]{1,0:T(8,128)}) custom-call(f32[1,1024]{1,0:T(1,128)} %bitcast.229, bf16[240,1024]{1,0:T(8,128)(2,1)} %pad_maximum_fusion.9.table_ref, bf16[3,1024,1024]{2,1,0:T(8,128)(2,1)} %bitcast.187), custom_call_target="tpu_custom_call" | custom-call | flops 1000 | bytes 1000 | tf_op jit(solution)/shard_map/tables/pallas_call | solution.py:145
  28.8 9.6 %collective-permute-done.1 = f32[50]{0:T(128)S(1)} collective-permute-done((f32[50]{0:T(128)S(1)}, f32[50]{0:T(128)S(1)}, u32[]{:S(2)}, u32[]{:S(2)}) %collective-permute-start.1) | collective-permute-done | bytes 232 | tf_op jit(solution)/shard_map/ppermute | solution.py:1202
  51.5 3.4 collective-permute-start.5
  55.0 5.7 %collective-permute-done.12 = bf16[256,1024]{1,0:T(8,128)(2,1)S(1)} collective-permute-done((bf16[256,1024]{1,0:T(8,128)(2,1)S(1)}, bf16[256,1024]{1,0:T(8,128)(2,1)S(1)}, u32[]{:S(2)}, u32[]{:S(2)}) %collective-permute-start.12) | collective-permute-done | bytes 524320 | tf_op jit(solution)/shard_map/ppermute | solution.py:1202
  66.1 3.5 collective-permute-start.4
  69.6 6.7 %collective-permute-done.17 = bf16[256,1024]{1,0:T(8,128)(2,1)} collective-permute-done((bf16[256,1024]{1,0:T(8,128)(2,1)}, bf16[256,1024]{1,0:T(8,128)(2,1)}, u32[]{:S(2)}, u32[]{:S(2)}) %collective-permute-start.17) | collective-permute-done | bytes 524320 | tf_op jit(solution)/shard_map/ppermute | solution.py:1386
  83.3 5.6 %collective-permute-done.18 = bf16[256,1024]{1,0:T(8,128)(2,1)S(1)} collective-permute-done((bf16[256,1024]{1,0:T(8,128)(2,1)}, bf16[256,1024]{1,0:T(8,128)(2,1)S(1)}, u32[]{:S(2)}, u32[]{:S(2)}) %collective-permute-start.18) | collective-permute-done | bytes 524320 | tf_op jit(solution)/shard_map/ppermute | solution.py:1202
  91.3 11.9 %aggregate.1 = (bf16[512,1024]{1,0:T(8,128)(2,1)}, bf16[1024,512]{1,0:T(8,128)(2,1)}, f32[16,48,512]{2,1,0:T(8,128)}, f32[4,48,512]{2,1,0:T(8,128)}) custom-call(s32[3]{0:T(128)} %pad_add_fusion.place_ref, f32[1]{0:T(128)} %dynamic_slice.66.alive_ref, f32[384,128]{1,0:T(8,128)} %get-tuple-element.170.own_field_ref, f32[384,128]{1,0:T(8,128)} %copy-done.28, ...), custom_call_target="tpu_custom_call" | custom-call | flops 1000 | bytes 1000 | tf_op jit(solution)/shard_map/aggregate/pallas_call | solution.py:272
  107.4 20.4 %attend.1 = (bf16[2048,512]{1,0:T(8,128)(2,1)}, bf16[3,512,1024]{2,1,0:T(8,128)(2,1)}, f32[8,2,512]{2,1,0:T(2,128)}) custom-call(s32[3]{0:T(128)} %pad_add_fusion.place_ref, bf16[512,1024]{1,0:T(8,128)(2,1)} %get-tuple-element.74.tokens_ref, f32[2,1024]{1,0:T(2,128)} %gain_ref.5, f32[2,1024]{1,0:T(2,128)} %bias_ref.3, bf16[3,1024,1024]{2,1,0:T(8,128)(2,1)} %bitcast.188, ...), custom_call_target="tpu_custom_call" | custom-call | flops 1000 | bytes 1000 | tf_op jit(solution)/shard_map/attend/pallas_call | solution.py:346
  127.9 8.5 %merge.1 = (f32[512,1024]{1,0:T(8,128)}, bf16[512,1024]{1,0:T(8,128)(2,1)}) custom-call(s32[3]{0:T(128)} %pad_add_fusion.place_ref, bf16[512,1024]{1,0:T(8,128)(2,1)} %get-tuple-element.74.tokens_ref, bf16[2048,512]{1,0:T(8,128)(2,1)} %get-tuple-element.77.pack_ref.pack_own, f32[2,1024]{1,0:T(2,128)} %gain_ref.5, f32[2,1024]{1,0:T(2,128)} %bias_ref.3, ...), custom_call_target="tpu_custom_call" | custom-call | flops 1000 | bytes 1000 | tf_op jit(solution)/shard_map/merge/pallas_call | solution.py:401
  137.3 21.9 %expand.1 = (bf16[2,512,4608]{2,1,0:T(8,128)(2,1)}, f32[1,4096]{1,0:T(1,128)}) custom-call(s32[3]{0:T(128)} %pad_add_fusion.place_ref, bf16[512,1024]{1,0:T(8,128)(2,1)} %get-tuple-element.79.second_ref.left_any, bf16[512,1024]{1,0:T(8,128)(2,1)} %fusion.1.out_ref.left_any, f32[1,4096]{1,0:T(1,128)} %bitcast.225, bf16[1024,4096]{1,0:T(8,128)(2,1)} %up_any.3, ...), custom_call_target="tpu_custom_call" | custom-call | flops 1000 | bytes 1000 | tf_op jit(solution)/shard_map/expand/pallas_call | solution.py:514
  161.7 16.7 %contract.1 = (bf16[512,1024]{1,0:T(8,128)(2,1)}, f32[512,1024]{1,0:T(8,128)}, bf16[512,1024]{1,0:T(8,128)(2,1)}, f32[1,1024]{1,0:T(1,128)}, f32[1,1024]{1,0:T(1,128)}, /*index=5*/f32[1,1024]{1,0:T(1,128)}) custom-call(s32[3]{0:T(128)} %pad_add_fusion.place_ref, f32[2]{0:T(128)} %pad_maximum_fusion.18.scalars_ref, f32[1,1024]{1,0:T(1,128)} %slice.156.gain_ref, ...), custom_call_target="tpu_custom_call" | custom-call | flops 1000 | bytes 1000 | tf_op jit(solution)/shard_map/contract/pallas_call | solution.py:620
  178.5 8.7 %down_grads.1 = (bf16[2,2,2,512,256]{4,3,2,1,0:T(8,128)(2,1)}, bf16[2,2,2,512,256]{4,3,2,1,0:T(8,128)(2,1)}) custom-call(s32[2]{0:T(128)} %pad_add_fusion.2.place_ref, bf16[512,1024]{1,0:T(8,128)(2,1)} %fusion.1.out_ref.left_any, bf16[2,512,4608]{2,1,0:T(8,128)(2,1)} %get-tuple-element.81.units_any.own_any, ...), custom_call_target="tpu_custom_call" | custom-call | flops 1000 | bytes 1000 | tf_op jit(solution)/shard_map/down_grads/pallas_call | solution.py:983
  187.3 8.8 %up_grads.1 = (bf16[2,2,2,512,256]{4,3,2,1,0:T(8,128)(2,1)}, bf16[2,2,2,512,256]{4,3,2,1,0:T(8,128)(2,1)}) custom-call(s32[2]{0:T(128)} %pad_add_fusion.2.place_ref, bf16[512,1024]{1,0:T(8,128)(2,1)} %get-tuple-element.79.second_ref.left_any, bf16[2,512,4608]{2,1,0:T(8,128)(2,1)} %get-tuple-element.81.units_any.own_any, ...), custom_call_target="tpu_custom_call" | custom-call | flops 1000 | bytes 1000 | tf_op jit(solution)/shard_map/up_grads/pallas_call | solution.py:983
  197.7 3.4 collective-permute-start.25
  201.1 29.4 %attend_back.1 = (bf16[4,512,512]{2,1,0:T(8,128)(2,1)}, bf16[4,512,512]{2,1,0:T(8,128)(2,1)}, bf16[512,1024]{1,0:T(8,128)(2,1)}, f32[1,1024]{1,0:T(1,128)}, f32[1,1024]{1,0:T(1,128)}) custom-call(s32[3]{0:T(128)} %pad_add_fusion.place_ref, f32[512,1024]{1,0:T(8,128)} %get-tuple-element.83.grad_ref, bf16[512,1024]{1,0:T(8,128)(2,1)} %get-tuple-element.84.refs_0_.branch_ref, ...), custom_call_target="tpu_custom_call" | custom-call | flops 1000 | bytes 1000 | tf_op jit(solution)/shard_map/attend_back/pallas_call | solution.py:750
  231.1 16.2 %aggregate_back.1 = (bf16[1024,512]{1,0:T(8,128)(2,1)}, bf16[1024,512]{1,0:T(8,128)(2,1)}, f32[768,128]{1,0:T(8,128)}) custom-call(s32[3]{0:T(128)} %pad_add_fusion.place_ref, f32[1]{0:T(128)} %dynamic_slice.66.alive_ref, bf16[512,1024]{1,0:T(8,128)(2,1)} %get-tuple-element.89.token_grad_ref, f32[4,48,512]{2,1,0:T(8,128)} %get-tuple-element.90.pixels_ref, ...), custom_call_target="tpu_custom_call" | custom-call | flops 1000 | bytes 1000 | tf_op jit(solution)/shard_map/aggregate_back/pallas_call | solution.py:888
  259.6 11.4 %square_grads.1 = (bf16[4,256,512]{2,1,0:T(8,128)(2,1)}, bf16[4,256,512]{2,1,0:T(8,128)(2,1)}, bf16[2,4,256,512]{3,2,1,0:T(8,128)(2,1)}, bf16[2,4,256,512]{3,2,1,0:T(8,128)(2,1)}) custom-call(s32[2]{0:T(128)} %pad_add_fusion.3.place_ref, bf16[1024,512]{1,0:T(8,128)(2,1)} %get-tuple-element.100.tail_own, ...), custom_call_target="tpu_custom_call" | custom-call | flops 1000 | bytes 1000 | tf_op jit(solution)/shard_map/square_grads/pallas_call | solution.py:1106
  276.1 3.1 copy.66
  279.3 3.7 collective-permute-done.27
  288.8 3.8 collective-permute-start.36
  293.2 40.1 %collective-permute-done.29 = bf16[2,4,256,512]{3,2,1,0:T(8,128)(2,1)S(1)} collective-permute-done((bf16[2,4,256,512]{3,2,1,0:T(8,128)(2,1)S(1)}, bf16[2,4,256,512]{3,2,1,0:T(8,128)(2,1)S(1)}, u32[]{:S(2)}, u32[]{:S(2)}) %collective-permute-start.29) | collective-permute-done | bytes 2097184 | tf_op jit(solution)/shard_map/ppermute | solution.py:1202
  337.8 19.8 %collective-permute-done.30 = bf16[4,256,512]{2,1,0:T(8,128)(2,1)S(1)} collective-permute-done((bf16[4,256,512]{2,1,0:T(8,128)(2,1)S(1)}, bf16[4,256,512]{2,1,0:T(8,128)(2,1)S(1)}, u32[]{:S(2)}, u32[]{:S(2)}) %collective-permute-start.30) | collective-permute-done | bytes 1048608 | tf_op jit(solution)/shard_map/ppermute | solution.py:1202
  359.3 3.6 collective-permute-start.39
  366.5 9.8 %collective-permute-done.39 = bf16[512,512]{1,0:T(8,128)(2,1)} collective-permute-done((bf16[512,512]{1,0:T(8,128)(2,1)}, bf16[512,512]{1,0:T(8,128)(2,1)}, u32[]{:S(2)}, u32[]{:S(2)}) %collective-permute-start.39) | collective-permute-done | bytes 524320 | tf_op jit(solution)/shard_map/ppermute | solution.py:1202
  376.3 29.3 %collective-permute-done.38 = bf16[512,512]{1,0:T(8,128)(2,1)} collective-permute-done((bf16[512,512]{1,0:T(8,128)(2,1)}, bf16[512,512]{1,0:T(8,128)(2,1)}, u32[]{:S(2)}, u32[]{:S(2)}) %collective-permute-start.38) | collective-permute-done | bytes 524320 | tf_op jit(solution)/shard_map/ppermute | solution.py:1202
  411.0 5.2 %collective-permute-done.40 = bf16[320,512]{1,0:T(8,128)(2,1)S(1)} collective-permute-done((bf16[320,512]{1,0:T(8,128)(2,1)S(1)}, bf16[320,512]{1,0:T(8,128)(2,1)S(1)}, u32[]{:S(2)}, u32[]{:S(2)}) %collective-permute-start.40) | collective-permute-done | bytes 327712 | tf_op jit(solution)/shard_map/ppermute | solution.py:1202
  436.9 5.9 %collective-permute-done.45 = bf16[4,2,64,512]{3,2,1,0:T(8,128)(2,1)S(1)} collective-permute-done((bf16[4,2,64,512]{3,2,1,0:T(8,128)(2,1)S(1)}, bf16[4,2,64,512]{3,2,1,0:T(8,128)(2,1)S(1)}, u32[]{:S(2)}, u32[]{:S(2)}) %collective-permute-start.45) | collective-permute-done | bytes 524320 | tf_op jit(solution)/shard_map/ppermute | solution.py:1202
  444.8 11.0 %collective-permute-done.31 = bf16[512,1024]{1,0:T(8,128)(2,1)S(1)} collective-permute-done((bf16[512,1024]{1,0:T(8,128)(2,1)S(1)}, bf16[512,1024]{1,0:T(8,128)(2,1)S(1)}, u32[]{:S(2)}, u32[]{:S(2)}) %collective-permute-start.31) | collective-permute-done | bytes 1048608 | tf_op jit(solution)/shard_map/ppermute | solution.py:1202
  459.9 5.8 %finish.1 = (f32[512,1024]{1,0:T(8,128)}, f32[1024,256]{1,0:T(8,128)}, f32[16,1024]{1,0:T(8,128)}, f32[240,16]{1,0:T(8,128)}, f32[16,1024]{1,0:T(8,128)}, /*index=5*/f32[16,1024]{1,0:T(8,128)}, f32[16,1024]{1,0:T(8,128)}) custom-call(s32[3]{0:T(128)} %pad_add_fusion.4.place_ref, bf16[2,8,2,64,512]{4,3,2,1,0:T(8,128)(2,1)} %pad_maximum_fusion.2.tail_ref, ...), custom_call_target="tpu_custom_call" | custom-call | flops 1000 | bytes 1000 | tf_op jit(solution)/shard_map/finish/pallas_call | solution.py:1180
  471.9 3.6 collective-permute-start.48
  (272 shorter events, 138.4 us)
Async XLA Ops:
  2.7 21.2 %collective-permute-start.8 = (bf16[256,1024]{1,0:T(8,128)(2,1)S(1)}, bf16[256,1024]{1,0:T(8,128)(2,1)S(1)}, u32[]{:S(2)}, u32[]{:S(2)}) collective-permute-start(bf16[256,1024]{1,0:T(8,128)(2,1)S(1)} %get-tuple-element.139), channel_id=1, source_target_pairs={{0,16},{16,0},{1,17},{17,1},{2,18},{18,2},{3,19},{19,3},{4,20},{20... | collective-permute-start | bytes 1572872 | tf_op jit(solution)/shard_map/ppermute | solution.py:1202
  8.7 19.2 %collective-permute-start = (f32[50]{0:T(128)S(1)}, f32[50]{0:T(128)S(1)}, u32[]{:S(2)}, u32[]{:S(2)}) collective-permute-start(f32[50]{0:T(128)S(1)} %pad_maximum_fusion.17), channel_id=1, source_target_pairs={{0,1},{1,0},{2,3},{3,2},{4,5},{5,4},{6,7},{7,6},{8,9},{9,8},{10,11... | collective-permute-start | bytes 608 | tf_op jit(solution)/shard_map/ppermute | solution.py:1202
  16.1 50.1 %collective-permute-start.6 = (f32[240,16]{1,0:T(8,128)}, f32[240,16]{1,0:T(8,128)}, u32[]{:S(2)}, u32[]{:S(2)}) collective-permute-start(f32[240,16]{1,0:T(8,128)} %get-tuple-element.72), channel_id=1, source_target_pairs={{0,16},{1,17},{2,18},{3,19},{4,20},{5,21},{6,22},{7,23},{8,24},{9,... | collective-permute-start | bytes 46088 | tf_op jit(solution)/shard_map/ppermute | solution.py:1374
  20.7 58.6 %collective-permute-start.7 = (bf16[1024,256]{1,0:T(8,128)(2,1)}, bf16[1024,256]{1,0:T(8,128)(2,1)}, u32[]{:S(2)}, u32[]{:S(2)}) collective-permute-start(bf16[1024,256]{1,0:T(8,128)(2,1)} %convert_element_type.162), channel_id=1, source_target_pairs={{0,16},{1,17},{2,18},{3,19},{4,20},{5,21},{6,22},{7,23},{8,24},{9,... | collective-permute-start | bytes 1572872 | tf_op jit(solution)/shard_map/ppermute | solution.py:1374
  23.9 23.7 %collective-permute-start.9 = (bf16[256,1024]{1,0:T(8,128)(2,1)S(1)}, bf16[256,1024]{1,0:T(8,128)(2,1)S(1)}, u32[]{:S(2)}, u32[]{:S(2)}) collective-permute-start(bf16[256,1024]{1,0:T(8,128)(2,1)S(1)} %collective-permute-done.8), channel_id=1, source_target_pairs={{0,2},{1,3},{2,0},{3,1},{4,6},{5,7},{6,4},{7,5},{8,10},{9,11},{10,... | collective-permute-start | bytes 1572872 | tf_op jit(solution)/shard_map/ppermute | solution.py:1202
  27.9 19.8 %collective-permute-start.11 = (bf16[256,1024]{1,0:T(8,128)(2,1)S(1)}, bf16[256,1024]{1,0:T(8,128)(2,1)S(1)}, u32[]{:S(2)}, u32[]{:S(2)}) collective-permute-start(bf16[256,1024]{1,0:T(8,128)(2,1)S(1)} %get-tuple-element.75), channel_id=1, source_target_pairs={{0,16},{16,0},{1,17},{17,1},{2,18},{18,2},{3,19},{19,3},{4,20},{20... | collective-permute-start | bytes 1572872 | tf_op jit(solution)/shard_map/ppermute | solution.py:1202
  61.3 14.9 %collective-permute-start.17 = (bf16[256,1024]{1,0:T(8,128)(2,1)}, bf16[256,1024]{1,0:T(8,128)(2,1)}, u32[]{:S(2)}, u32[]{:S(2)}) collective-permute-start(bf16[256,1024]{1,0:T(8,128)(2,1)} %dynamic-slice_bitcast_fusion.1), channel_id=1, source_target_pairs={{16,0},{17,1},{18,2},{19,3},{20,4},{21,5},{22,6},{23,7},{24,8},{25... | collective-permute-start | bytes 1572872 | tf_op jit(solution)/shard_map/ppermute | solution.py:1386
  62.9 27.2 %collective-permute-start.10 = (bf16[2,256,1024]{2,1,0:T(8,128)(2,1)S(1)}, bf16[2,256,1024]{2,1,0:T(8,128)(2,1)S(1)}, u32[]{:S(2)}, u32[]{:S(2)}) collective-permute-start(bf16[2,256,1024]{2,1,0:T(8,128)(2,1)S(1)} %pad_maximum_fusion.3.brought_ref.refs_0_), channel_id=1, source_target_pairs={{0,1},{1,0},{2,3},{3,2},{4,5},{5,4},{6,7},{7,6},{8,9},{9,8},{10,11... | collective-permute-start | bytes 3145736 | tf_op jit(solution)/shard_map/ppermute | solution.py:1202
  63.1 18.3 %collective-permute-start.15 = (bf16[256,1024]{1,0:T(8,128)(2,1)}, bf16[256,1024]{1,0:T(8,128)(2,1)}, u32[]{:S(2)}, u32[]{:S(2)}) collective-permute-start(bf16[256,1024]{1,0:T(8,128)(2,1)} %collective-permute-done.14), channel_id=1, source_target_pairs={{0,2},{1,3},{2,0},{3,1},{4,6},{5,7},{6,4},{7,5},{8,10},{9,11},{10,... | collective-permute-start | bytes 1572872 | tf_op jit(solution)/shard_map/ppermute | solution.py:1202
  66.1 24.0 %collective-permute-start.4 = (f32[384,128]{1,0:T(8,128)}, f32[384,128]{1,0:T(8,128)S(1)}, u32[]{:S(2)}, u32[]{:S(2)}) collective-permute-start(f32[384,128]{1,0:T(8,128)} %get-tuple-element.169), channel_id=1, source_target_pairs={{0,16},{16,0},{1,17},{17,1},{2,18},{18,2},{3,19},{19,3},{4,20},{20... | collective-permute-start | bytes 589832 | tf_op jit(solution)/shard_map/ppermute | solution.py:1202
  81.4 26.0 %collective-permute-start.13 = (bf16[2,256,1024]{2,1,0:T(8,128)(2,1)S(1)}, bf16[2,256,1024]{2,1,0:T(8,128)(2,1)}, u32[]{:S(2)}, u32[]{:S(2)}) collective-permute-start(bf16[2,256,1024]{2,1,0:T(8,128)(2,1)S(1)} %pad_maximum_fusion.4.refs_2_), channel_id=1, source_target_pairs={{0,1},{1,0},{2,3},{3,2},{4,5},{5,4},{6,7},{7,6},{8,9},{9,8},{10,11... | collective-permute-start | bytes 3145736 | tf_op jit(solution)/shard_map/ppermute | solution.py:1202
  82.7 24.7 %collective-permute-start.16 = (bf16[2,256,1024]{2,1,0:T(8,128)(2,1)S(1)}, bf16[2,256,1024]{2,1,0:T(8,128)(2,1)}, u32[]{:S(2)}, u32[]{:S(2)}) collective-permute-start(bf16[2,256,1024]{2,1,0:T(8,128)(2,1)S(1)} %pad_maximum_fusion.5.refs_4_), channel_id=1, source_target_pairs={{0,1},{1,0},{2,3},{3,2},{4,5},{5,4},{6,7},{7,6},{8,9},{9,8},{10,11... | collective-permute-start | bytes 3145736 | tf_op jit(solution)/shard_map/ppermute | solution.py:1202
  90.0 37.8 %collective-permute-start.19 = (bf16[2,256,1024]{2,1,0:T(8,128)(2,1)S(1)}, bf16[2,256,1024]{2,1,0:T(8,128)(2,1)}, u32[]{:S(2)}, u32[]{:S(2)}) collective-permute-start(bf16[2,256,1024]{2,1,0:T(8,128)(2,1)S(1)} %pad_maximum_fusion.6.brought_ref.refs_6_), channel_id=1, source_target_pairs={{0,1},{1,0},{2,3},{3,2},{4,5},{5,4},{6,7},{7,6},{8,9},{9,8},{10,11... | collective-permute-start | bytes 3145736 | tf_op jit(solution)/shard_map/ppermute | solution.py:1202
  103.2 33.2 %collective-permute-start.20 = (bf16[1024,512]{1,0:T(8,128)(2,1)}, bf16[1024,512]{1,0:T(8,128)(2,1)S(1)}, u32[]{:S(2)}, u32[]{:S(2)}) collective-permute-start(bf16[1024,512]{1,0:T(8,128)(2,1)} %get-tuple-element.80.heads_own), channel_id=1, source_target_pairs={{0,1},{1,0},{2,3},{3,2},{4,5},{5,4},{6,7},{7,6},{8,9},{9,8},{10,11... | collective-permute-start | bytes 3145736 | tf_op jit(solution)/shard_map/ppermute | solution.py:1202
  159.3 19.3 %collective-permute-start.21 = (bf16[2,512,4608]{2,1,0:T(8,128)(2,1)}, bf16[2,512,4608]{2,1,0:T(8,128)(2,1)}, u32[]{:S(2)}, u32[]{:S(2)}) collective-permute-start(bf16[2,512,4608]{2,1,0:T(8,128)(2,1)} %get-tuple-element.81.units_any.own_any), channel_id=1, source_target_pairs={{0,1},{1,0},{2,3},{3,2},{4,5},{5,4},{6,7},{7,6},{8,9},{9,8},{10,11... | collective-permute-start | bytes 28311560 | tf_op jit(solution)/shard_map/ppermute | solution.py:1202
  196.0 51.4 %collective-permute-start.26 = (bf16[2,2,2,512,256]{4,3,2,1,0:T(8,128)(2,1)}, bf16[2,2,2,512,256]{4,3,2,1,0:T(8,128)(2,1)S(1)}, u32[]{:S(2)}, u32[]{:S(2)}) collective-permute-start(bf16[2,2,2,512,256]{4,3,2,1,0:T(8,128)(2,1)} %get-tuple-element.107), channel_id=1, source_target_pairs={{0,2},{1,3},{2,0},{3,1},{4,6},{5,7},{6,4},{7,5},{8,10},{9,11},{10,... | collective-permute-start | bytes 6291464 | tf_op jit(solution)/shard_map/ppermute | solution.py:1202
  197.7 54.7 %collective-permute-start.25 = (bf16[2,2,2,512,256]{4,3,2,1,0:T(8,128)(2,1)}, bf16[2,2,2,512,256]{4,3,2,1,0:T(8,128)(2,1)}, u32[]{:S(2)}, u32[]{:S(2)}) collective-permute-start(bf16[2,2,2,512,256]{4,3,2,1,0:T(8,128)(2,1)} %get-tuple-element.105), channel_id=1, source_target_pairs={{0,16},{16,0},{1,17},{17,1},{2,18},{18,2},{3,19},{19,3},{4,20},{20... | collective-permute-start | bytes 6291464 | tf_op jit(solution)/shard_map/ppermute | solution.py:1202
  201.1 58.5 %collective-permute-start.23 = (bf16[2048,512]{1,0:T(8,128)(2,1)}, bf16[2048,512]{1,0:T(8,128)(2,1)}, u32[]{:S(2)}, u32[]{:S(2)}) collective-permute-start(bf16[2048,512]{1,0:T(8,128)(2,1)} %get-tuple-element.77.pack_ref.pack_own), channel_id=1, source_target_pairs={{0,1},{1,0},{2,3},{3,2},{4,5},{5,4},{6,7},{7,6},{8,9},{9,8},{10,11... | collective-permute-start | bytes 6291464 | tf_op jit(solution)/shard_map/ppermute | solution.py:1202
  230.5 29.1 %collective-permute-start.24 = (bf16[4,512,512]{2,1,0:T(8,128)(2,1)}, bf16[4,512,512]{2,1,0:T(8,128)(2,1)}, u32[]{:S(2)}, u32[]{:S(2)}) collective-permute-start(bf16[4,512,512]{2,1,0:T(8,128)(2,1)} %get-tuple-element.103), channel_id=1, source_target_pairs={{0,1},{1,0},{2,3},{3,2},{4,5},{5,4},{6,7},{7,6},{8,9},{9,8},{10,11... | collective-permute-start | bytes 6291464 | tf_op jit(solution)/shard_map/ppermute | solution.py:1202
  252.0 27.2 %collective-permute-start.28 = (bf16[4,512,256]{1,2,0:T(8,128)(2,1)}, bf16[4,512,256]{1,2,0:T(8,128)(2,1)}, u32[]{:S(2)}, u32[]{:S(2)}) collective-permute-start(bf16[4,512,256]{1,2,0:T(8,128)(2,1)} %copy.67), channel_id=1, source_target_pairs={{0,16},{16,0},{1,17},{17,1},{2,18},{18,2},{3,19},{19,3},{4,20},{20... | collective-permute-start | bytes 3145736 | tf_op jit(solution)/shard_map/ppermute | solution.py:1202
  257.4 25.5 %collective-permute-start.27 = (bf16[4,512,256]{1,2,0:T(8,128)(2,1)}, bf16[4,512,256]{1,2,0:T(8,128)(2,1)}, u32[]{:S(2)}, u32[]{:S(2)}) collective-permute-start(bf16[4,512,256]{1,2,0:T(8,128)(2,1)} %copy.65), channel_id=1, source_target_pairs={{0,2},{1,3},{2,0},{3,1},{4,6},{5,7},{6,4},{7,5},{8,10},{9,11},{10,... | collective-permute-start | bytes 3145736 | tf_op jit(solution)/shard_map/ppermute | solution.py:1202
  286.4 46.9 %collective-permute-start.29 = (bf16[2,4,256,512]{3,2,1,0:T(8,128)(2,1)S(1)}, bf16[2,4,256,512]{3,2,1,0:T(8,128)(2,1)S(1)}, u32[]{:S(2)}, u32[]{:S(2)}) collective-permute-start(bf16[2,4,256,512]{3,2,1,0:T(8,128)(2,1)S(1)} %copy-done.36), channel_id=1, source_target_pairs={{0,16},{16,0},{1,17},{17,1},{2,18},{18,2},{3,19},{19,3},{4,20},{20... | collective-permute-start | bytes 6291464 | tf_op jit(solution)/shard_map/ppermute | solution.py:1202
  288.2 49.3 %collective-permute-start.33 = (bf16[4,256,512]{2,1,0:T(8,128)(2,1)S(1)}, bf16[4,256,512]{2,1,0:T(8,128)(2,1)S(1)}, u32[]{:S(2)}, u32[]{:S(2)}) collective-permute-start(bf16[4,256,512]{2,1,0:T(8,128)(2,1)S(1)} %copy-done.37), channel_id=1, source_target_pairs={{0,2},{1,3},{2,0},{3,1},{4,6},{5,7},{6,4},{7,5},{8,10},{9,11},{10,... | collective-permute-start | bytes 3145736 | tf_op jit(solution)/shard_map/ppermute | solution.py:1202
  288.8 45.8 %collective-permute-start.36 = (bf16[2,512,256]{1,2,0:T(8,128)(2,1)S(1)}, bf16[2,512,256]{1,2,0:T(8,128)(2,1)S(1)}, u32[]{:S(2)}, u32[]{:S(2)}) collective-permute-start(bf16[2,512,256]{1,2,0:T(8,128)(2,1)S(1)} %get-tuple-element.145), channel_id=1, source_target_pairs={{0,12},{1,13},{2,14},{3,15},{4,8},{5,9},{6,10},{7,11},{8,4},{9,5},... | collective-permute-start | bytes 1572872 | tf_op jit(solution)/shard_map/ppermute | solution.py:1202
  292.5 43.8 %collective-permute-start.35 = (bf16[2,512,256]{1,2,0:T(8,128)(2,1)S(1)}, bf16[2,512,256]{1,2,0:T(8,128)(2,1)S(1)}, u32[]{:S(2)}, u32[]{:S(2)}) collective-permute-start(bf16[2,512,256]{1,2,0:T(8,128)(2,1)S(1)} %get-tuple-element.144), channel_id=1, source_target_pairs={{0,8},{1,9},{2,10},{3,11},{4,12},{5,13},{6,14},{7,15},{8,0},{9,1},... | collective-permute-start | bytes 1572872 | tf_op jit(solution)/shard_map/ppermute | solution.py:1202
  292.5 43.8 %collective-permute-start.34 = (bf16[2,512,256]{1,2,0:T(8,128)(2,1)S(1)}, bf16[2,512,256]{1,2,0:T(8,128)(2,1)S(1)}, u32[]{:S(2)}, u32[]{:S(2)}) collective-permute-start(bf16[2,512,256]{1,2,0:T(8,128)(2,1)S(1)} %get-tuple-element.143), channel_id=1, source_target_pairs={{0,4},{1,5},{2,6},{3,7},{4,0},{5,1},{6,2},{7,3},{8,12},{9,13},{10,... | collective-permute-start | bytes 1572872 | tf_op jit(solution)/shard_map/ppermute | solution.py:1202
  334.1 23.6 %collective-permute-start.30 = (bf16[4,256,512]{2,1,0:T(8,128)(2,1)S(1)}, bf16[4,256,512]{2,1,0:T(8,128)(2,1)S(1)}, u32[]{:S(2)}, u32[]{:S(2)}) collective-permute-start(bf16[4,256,512]{2,1,0:T(8,128)(2,1)S(1)} %slice_bitcast_fusion.1), channel_id=1, source_target_pairs={{0,2},{1,3},{2,0},{3,1},{4,6},{5,7},{6,4},{7,5},{8,10},{9,11},{10,... | collective-permute-start | bytes 3145736 | tf_op jit(solution)/shard_map/ppermute | solution.py:1202
  359.3 17.1 %collective-permute-start.39 = (bf16[512,512]{1,0:T(8,128)(2,1)}, bf16[512,512]{1,0:T(8,128)(2,1)}, u32[]{:S(2)}, u32[]{:S(2)}) collective-permute-start(bf16[512,512]{1,0:T(8,128)(2,1)} %get-tuple-element.141), channel_id=1, source_target_pairs={{0,12},{1,13},{2,14},{3,15},{4,8},{5,9},{6,10},{7,11},{8,4},{9,5},... | collective-permute-start | bytes 1572872 | tf_op jit(solution)/shard_map/ppermute | solution.py:1202
  362.8 42.8 %collective-permute-start.38 = (bf16[512,512]{1,0:T(8,128)(2,1)}, bf16[512,512]{1,0:T(8,128)(2,1)}, u32[]{:S(2)}, u32[]{:S(2)}) collective-permute-start(bf16[512,512]{1,0:T(8,128)(2,1)} %get-tuple-element.142), channel_id=1, source_target_pairs={{0,8},{1,9},{2,10},{3,11},{4,12},{5,13},{6,14},{7,15},{8,0},{9,1},... | collective-permute-start | bytes 1572872 | tf_op jit(solution)/shard_map/ppermute | solution.py:1202
  362.8 42.8 %collective-permute-start.37 = (bf16[512,512]{1,0:T(8,128)(2,1)}, bf16[512,512]{1,0:T(8,128)(2,1)}, u32[]{:S(2)}, u32[]{:S(2)}) collective-permute-start(bf16[512,512]{1,0:T(8,128)(2,1)} %get-tuple-element.140), channel_id=1, source_target_pairs={{0,4},{1,5},{2,6},{3,7},{4,0},{5,1},{6,2},{7,3},{8,12},{9,13},{10,... | collective-permute-start | bytes 1572872 | tf_op jit(solution)/shard_map/ppermute | solution.py:1202
  434.3 21.4 %collective-permute-start.31 = (bf16[512,1024]{1,0:T(8,128)(2,1)S(1)}, bf16[512,1024]{1,0:T(8,128)(2,1)S(1)}, u32[]{:S(2)}, u32[]{:S(2)}) collective-permute-start(bf16[512,1024]{1,0:T(8,128)(2,1)S(1)} %broadcast_select_fusion), channel_id=1, source_target_pairs={{0,16},{16,0},{1,17},{17,1},{2,18},{18,2},{3,19},{19,3},{4,20},{20... | collective-permute-start | bytes 3145736 | tf_op jit(solution)/shard_map/ppermute | solution.py:1202
  442.9 14.7 %collective-permute-start.46 = (bf16[8,2,64,512]{3,2,1,0:T(8,128)(2,1)S(1)}, bf16[8,2,64,512]{3,2,1,0:T(8,128)(2,1)S(1)}, u32[]{:S(2)}, u32[]{:S(2)}) collective-permute-start(bf16[8,2,64,512]{3,2,1,0:T(8,128)(2,1)S(1)} %bitcast.197), channel_id=1, source_target_pairs={{0,1},{1,0},{2,3},{3,2},{4,5},{5,4},{6,7},{7,6},{8,9},{9,8},{10,11... | collective-permute-start | bytes 3145736 | tf_op jit(solution)/shard_map/ppermute | solution.py:1202
  (57 other events, 609.0 us)
where the time goes:
time: 495 us; the launch traced here: 489 us
  Pallas kernels  165 us (33%)
  waiting for transfers between devices  160 us (32%)
  starting transfers between devices  66.2 us (13%)
  other arithmetic  50.2 us (10%)
  local copies, waits for them, and re-layouts  37.7 us (8%)
  between operations  5.22 us (1%)
    ppermute x46, waiting for transfers between devices, partner(): return lax.ppermute(block, axis, [(i, i ^ distance) for i in range(size)])  153 us
    ppermute x46, starting transfers between devices, partner(): return lax.ppermute(block, axis, [(i, i ^ distance) for i in range(size)])  55 us
    pallas_call x1, Pallas kernels, attend_back(): pl.pallas_call(attend_back_kernel, out_shape=(shape((4, PATCHES, HALF), B...  29.4 us
    pallas_call x1, Pallas kernels, expand(): pl.pallas_call(expand_kernel, out_shape=(shape((2, PATCHES, UNITS), BF),...  21.9 us
    pallas_call x1, Pallas kernels, attend(): pl.pallas_call(attend_kernel, out_shape=(shape((2 * D, PATCHES), BF), sha...  20.4 us
    pallas_call x2, Pallas kernels, wide_grads(): pl.pallas_call(functools.partial(wide_kernel, which, by_pipe), in_specs=[...  17.5 us
    pallas_call x1, Pallas kernels, contract(): pl.pallas_call(contract_kernel, out_shape=(shape((PATCHES, D), BF), shape...  16.7 us
    pallas_call x1, Pallas kernels, aggregate_back(): pl.pallas_call(aggregate_back_kernel, out_shape=(shape((TAIL, HALF), BF),...  16.2 us
  transfers between devices with their start and end apart: 51, of which 18 were waited for; matrix products, arithmetic and copies ran while one was open for 14% of the time, Pallas kernels for 25%

commit v1 on v0

--- a/solution.py
+++ b/solution.py
@@ -1126,75 +1126,216 @@
     )(place, *tail, *heads, *pack, *right, *after)
 
 
+def first_sums_kernel(down_keep, down_came, up_keep, up_came, after_any, down_ref, up_ref):
+    for z in range(4):
+        at = (0, z // 2, z % 2)
+        down_ref[z] = (down_keep[at].astype(F32) + down_came[at].astype(F32)).astype(BF)
+        up_ref[z] = (up_keep[at].astype(F32) + up_came[at].astype(F32)).astype(BF)
+
+
+def first_sums(down_keep, down_came, up_keep, up_came, after):
+    half = pl.BlockSpec((1, 2, 2, HALF, BLOCK), lambda i: (1, 0, 0, 0, 0))
+    return pl.pallas_call(
+        first_sums_kernel,
+        grid=(1,),
+        in_specs=[half] * 4 + [ANYWHERE],
+        out_specs=(VMEM, VMEM),
+        out_shape=(shape((4, HALF, BLOCK), BF), shape((4, HALF, BLOCK), BF)),
+        compiler_params=params(1),
+        cost_estimate=cost(),
+        name="first_sums",
+    )(down_keep, down_came, up_keep, up_came, after)
+
+
+def second_sums_kernel(
+    down_keep, down_came, down_brought, up_keep, up_came, up_brought, after_any, *outs
+):
+    def added(keep, came, brought, z):
+        at = (0, z // 2, z % 2)
+        one = (keep[at].astype(F32) + came[at].astype(F32)).astype(BF).astype(F32)
+        return (one + brought[z].astype(F32)).astype(BF)
+
+    for z in range(4):
+        outs[z][0] = added(down_keep, down_came, down_brought, z)
+        outs[z][1] = added(up_keep, up_came, up_brought, z)
+
+
+def second_sums(down_keep, down_came, down_brought, up_keep, up_came, up_brought, after):
+    half = pl.BlockSpec((1, 2, 2, HALF, BLOCK), lambda i: (0, 0, 0, 0, 0))
+    return pl.pallas_call(
+        second_sums_kernel,
+        grid=(1,),
+        in_specs=[half, half, VMEM] * 2 + [ANYWHERE],
+        out_specs=(VMEM,) * 4,
+        out_shape=(shape((2, HALF, BLOCK), BF),) * 4,
+        compiler_params=params(1),
+        cost_estimate=cost(),
+        name="second_sums",
+    )(down_keep, down_came, down_brought, up_keep, up_came, up_brought, after)
+
+
+def third_sums_kernel(keep, came, out_ref):
+    for z in range(4):
+        out_ref[z] = (keep[0, z].astype(F32) + came[0, z].astype(F32)).astype(BF)
+
+
+def third_sums(keep, came):
+    half = pl.BlockSpec((1, 4, PARTS, HALF), lambda i: (1, 0, 0, 0))
+    return pl.pallas_call(
+        third_sums_kernel,
+        grid=(1,),
+        in_specs=[half, half],
+        out_specs=VMEM,
+        out_shape=shape((4, PARTS, HALF), BF),
+        compiler_params=params(1),
+        cost_estimate=cost(),
+        name="third_sums",
+    )(keep, came)
+
+
+def fourth_sums_kernel(keep, came, cross_keep, cross_came, brought, *refs):
+    for z in range(4):
+        out_ref = refs[len(refs) - 4 + z]
+        out_ref[:PARTS] = (keep[z].astype(F32) + came[z].astype(F32)).astype(BF)
+        one = (cross_keep[0, z].astype(F32) + cross_came[0, z].astype(F32)).astype(BF)
+        out_ref[PARTS:] = (one.astype(F32) + brought[z].astype(F32)).astype(BF)
+
+
+def fourth_sums(keep, came, cross_keep, cross_came, brought, after):
+    half = pl.BlockSpec((1, 4, PARTS, HALF), lambda i: (0, 0, 0, 0))
+    return pl.pallas_call(
+        fourth_sums_kernel,
+        grid=(1,),
+        in_specs=[VMEM, VMEM, half, half, VMEM] + [ANYWHERE] * len(after),
+        out_specs=(VMEM,) * 4,
+        out_shape=(shape((2 * PARTS, HALF), BF),) * 4,
+        compiler_params=params(1),
+        cost_estimate=cost(),
+        name="fourth_sums",
+    )(keep, came, cross_keep, cross_came, brought, *after)
+
+
 def finish_kernel(
     chips,
     place_ref,
     tail_ref,
     table_ref,
-    weight_ref,
-    position_ref,
-    mix_ref,
-    small_ref,
-    keys_ref,
-    key_query_ref,
-    low_ref,
     query_ref,
-    whole_ref,
+    given_ref,
+    value_ref,
+    attend_ref,
+    *refs,
 ):
-    pipe, core, chip = place_ref[0], place_ref[1], place_ref[2]
-    part = TAIL // (2 * chips)
+    brought = [(refs[2 * n], refs[2 * n + 1]) for n in range(3)]
+    position_ref, gain_ref, bias_ref, output_ref, hidden_ref = refs[6:11]
+    embed_ref, variable_ref, attend_grad_ref, query_grad_ref = refs[11:15]
+    weight_ref, whole_ref, mix_ref, rows_ref, turned_ref, sems = refs[15:]
+    core, chip, spot = place_ref[1], place_ref[3], place_ref[4]
+    wait = section_copies(
+        place_ref,
+        0,
+        [attend_ref.at[j] for j in range(3)],
+        brought,
+        [weight_ref.at[j] for j in range(3)],
+        sems,
+    )
+    part = TAIL // chips
     for c in range(2):
         for n in range(chips):
-            for p in range(2):
-                start = (2 * n + p) * part
-                whole_ref[c, start : start + part, :] = tail_ref[
-                    jnp.bitwise_xor(c, core), jnp.bitwise_xor(n, chip), jnp.bitwise_xor(p, pipe)
-                ].astype(F32)
+            whole_ref[c, n * part : (n + 1) * part, :] = tail_ref[
+                jnp.bitwise_xor(c, core), jnp.bitwise_xor(n, chip)
+            ].astype(F32)
     for c in range(2):
         columns = slice(c * HALF, (c + 1) * HALF)
         position_ref[:, columns] = whole_ref[c, :PATCHES, :]
-        small_ref[:, columns] = whole_ref[c, SMALL_AT:KEYS_AT, :]
+        small = whole_ref[c, SMALL_AT:KEYS_AT, :]
+        gain_ref[:, columns] = small[0:2]
+        bias_ref[:, columns] = small[2:4]
+        output_ref[:, columns] = small[4:5]
+        hidden_ref[:, columns] = small[5:9]
         for n in range(2):
             start = c * HALF + n * TABLE_PAD
             mix_ref[start : start + TABLE_PAD, :] = whole_ref[
                 c, MIX_AT:SMALL_AT, n * TABLE_PAD : (n + 1) * TABLE_PAD
-            ]
+            ].astype(BF)
     keys = whole_ref[0, KEYS_AT:, :HEADS]
-    keys_ref[...] = keys
+    table = table_ref[...].astype(F32)
     grads = lax.dot_general(
         keys,
-        table_ref[...].astype(F32),
+        table,
         (((0,), (0,)), ((), ())),
         precision=PRECISE,
         preferred_element_type=F32,
     ).astype(BF)
-    key_query_ref[...] = grads.astype(F32)
-    low = jnp.where(head_rows(D), dot(grads, weight_ref[1], 1, 0), 0.0)
+    mask = head_rows(D)
+    wait(1)
+    low = jnp.where(mask, dot(grads, weight_ref[1], 1, 0), 0.0)
     low = jnp.sum(low, axis=0, keepdims=True) * HDIM ** (-0.5)
     low = jnp.broadcast_to(low, (HEADS, D)).astype(BF)
-    low_ref[...] = low.astype(F32)
-    query_ref[...] = dot(low, weight_ref[0], 1, 1)
-
-
-def finish(place, tail, table, weights, chips):
+    wait(0)
+    query_grad_ref[...] = dot(low, weight_ref[0], 1, 1)[:1]
+    mixed = mix_ref[...]
+    wait(2)
+    key_query = value_ref[...].astype(F32)[:, ROWS_TABLE:]
+    table_grad = dot(mixed, weight_ref[2], 0, 1)[:ROWS_TABLE] + lax.dot_general(
+        keys,
+        key_query,
+        (((1,), (1,)), ((), ())),
+        precision=PRECISE,
+        preferred_element_type=F32,
+    )
+    for k in range(PIECES):
+        embed_ref[:, k, :] = table_grad[k * VARS : (k + 1) * VARS]
+    variable_ref[...] = table_grad[PIECES * VARS :]
+    size = attend_grad_ref.shape[1]
+    rows = pl.ds(pl.multiple_of(spot * size, size), size)
+    rows_ref[...] = jnp.concatenate([grads.astype(F32), given_ref[...]], axis=0).T
+    turned_ref[...] = table.T
+    own = rows_ref[rows, :]
+    low = low.astype(F32)
+    spread = jnp.where(mask, query_ref[...] * HDIM ** (-0.5), 0.0)
+    attend_grad_ref[0] = own[:, HEADS : HEADS + 1] * low[:1]
+    attend_grad_ref[1] = lax.dot_general(
+        own[:, :HEADS],
+        spread,
+        (((1,), (0,)), ((), ())),
+        precision=PRECISE,
+        preferred_element_type=F32,
+    )
+    left = jnp.concatenate(
+        [turned_ref[rows, :], jnp.zeros((size, TABLE_PAD - ROWS_TABLE), F32)], axis=1
+    ).astype(BF)
+    attend_grad_ref[2] = dot(left, mixed, 1, 1)
+
+
+def finish(place, tail, table, query, given, value, weights, brought, chips, size):
     return pl.pallas_call(
         functools.partial(finish_kernel, chips),
         out_shape=(
             shape((PATCHES, D), F32),
-            shape((D, TABLE_PAD), F32),
-            shape((16, D), F32),
-            shape((ROWS_TABLE, HEADS), F32),
-            shape((HEADS, D), F32),
-            shape((HEADS, D), F32),
-            shape((HEADS, D), F32),
+            shape((2, D), F32),
+            shape((2, D), F32),
+            shape((1, D), F32),
+            shape((FF // D, D), F32),
+            shape((VARS, PIECES, D), F32),
+            shape((VARS, D), F32),
+            shape((3, size, D), F32),
+            shape((1, D), F32),
         ),
-        in_specs=[SMEM] + [VMEM] * 3,
-        out_specs=(VMEM,) * 7,
-        scratch_shapes=[pltpu.VMEM((2, TAIL, HALF), F32)],
+        in_specs=[SMEM] + [VMEM] * 5 + [ANYWHERE] * 7,
+        out_specs=(VMEM,) * 9,
+        scratch_shapes=[
+            pltpu.VMEM((3, D, D), BF),
+            pltpu.VMEM((2, TAIL, HALF), F32),
+            pltpu.VMEM((D, TABLE_PAD), BF),
+            pltpu.VMEM((D, 2 * HEADS), F32),
+            pltpu.VMEM((D, ROWS_TABLE), F32),
+            pltpu.SemaphoreType.DMA((3, 4)),
+        ],
         compiler_params=params(),
         cost_estimate=cost(),
         name="finish",
-    )(place, tail, table, weights)
+    )(place, tail, table, query, given, value, weights, *brought)
 
 
 def partner(block, axis, distance):
@@ -1264,6 +1405,12 @@
             [jnp.where(self.core == 0, own, brought), jnp.where(self.core == 0, brought, own)],
             axis=-1,
         )
+
+    def last(self, parts, group):
+        terms = [parts[0].astype(F32)]
+        for distance in range(1, 2 ** group[1]):
+            terms.append(partner(parts[distance], "dp", distance * 2 ** group[0]).astype(F32))
+        return tree_sum(terms)
 
     def gather(self, block):
         blocks = block[None]
@@ -1315,14 +1462,27 @@
         start = (jnp.int32(j), (2 * core + side) * QUARTER, jnp.int32(0))
         return lax.dynamic_slice(own_attend, start, (1, QUARTER, D))[0]
 
-    def passed_on(block):
-        pair = jnp.stack([block, partner(block, "dp", 2)])
-        return pair, partner(pair, "dp", 1)
-
     def after(value, *others):
         return lax.optimization_barrier((value, others))[0]
 
+    def passed_on(block, before, behind):
+        other = partner(after(block, *before), "dp", 2)
+        pair = jnp.stack([block, after(other, *behind)])
+        return pair, partner(pair, "dp", 1)
+
     chunk_first = swap(jnp.where(first, quarter(own_merge), quarter_of(0)))
+
+    table = jnp.concatenate(
+        [embed_weight.transpose(1, 0, 2).reshape(VARS * PIECES, D), variable_embed], axis=0
+    )
+    given = variable_query.astype(F32).reshape(1, D)
+    query, table_keys, table_value = tables(given, table, own_attend)
+
+    def from_first(block):
+        return jnp.where(first, block, lax.ppermute(block, "pipe", [(0, 1)]))
+
+    keys = from_first(table_keys)
+    tvt = from_first(table_value.astype(BF))
 
     flat_fields = fields.reshape(micro, half_vars * rows, cols)
     other_fields = swap(pick(flat_fields, 1 - pipe))
@@ -1340,9 +1500,9 @@
             jnp.sum(alive)[None],
         ]
     )
-    sums = at.total(sums)
+    sums = at.total(after(sums, table_value))
     total, live_total = sums[2 * half_vars], sums[2 * half_vars + 1]
-    first_moment = sums[:half_vars] / (total * rows * cols)
+    first_moment = after(sums, chunk_first)[:half_vars] / (total * rows * cols)
     second_moment = sums[half_vars : 2 * half_vars] / (total * rows * cols)
     center_new = (1.0 - MOMENTUM) * running_stats[0] + MOMENTUM * first_moment
     spread_new = (1.0 - MOMENTUM) * running_stats[1] + MOMENTUM * (
@@ -1363,29 +1523,18 @@
     alive_own = pick(alive, pipe)[None]
     out_low = (pick(cotangent, pipe).astype(F32) * weight_hat).astype(BF)
 
-    table = jnp.concatenate(
-        [embed_weight.transpose(1, 0, 2).reshape(VARS * PIECES, D), variable_embed], axis=0
-    )
-    query, table_keys, table_value = tables(
-        variable_query.astype(F32).reshape(1, D), table, own_attend
-    )
-
-    def from_first(block):
-        return jnp.where(first, block, lax.ppermute(block, "pipe", [(0, 1)]))
-
-    tvt = from_first(table_value.astype(BF))
-    keys = from_first(table_keys)
-
     chunk = chunk_first
-    passed = [passed_on(chunk)]
     chunks = [chunk]
+    passed = [passed_on(chunk, (sums,), ())]
     chunk = swap(after(jnp.where(first, quarter_of(2), quarter_of(1)), chunk))
-    passed.append(passed_on(chunk))
-    chunk = lax.ppermute(after(quarter_of(2), chunk, passed[0][0]), "pipe", [(1, 0)])
-    passed.append(passed_on(chunk))
-    chunk = lax.ppermute(after(quarter(own_merge), chunk, passed[1][0]), "pipe", [(1, 0)])
-    passed.append(passed_on(chunk))
-    brought = [block for pair in passed for block in pair]
+    passed.append(passed_on(chunk, (), ()))
+    chunk = swap(after(jnp.where(first, quarter_of(0), quarter_of(2)), chunk, passed[0][0]))
+    third = chunk
+    chunk = swap(
+        after(jnp.where(first, quarter_of(1), quarter(own_merge)), chunk, passed[1][0])
+    )
+    fourth = chunk
+    alive_own = after(alive_own, third)
 
     tokens, heads, shares, pixels = aggregate(
         place,
@@ -1399,8 +1548,12 @@
         position_embed,
         (own_merge, *passed[0]),
     )
+    passed.append(passed_on(third, (), (tokens,)))
     heads_beside = partner(heads, "dp", 1)
-    pack, proj, lse = attend(place, tokens, norm_gain, norm_bias, own_attend, brought[:6])
+    brought = [block for pair in passed for block in pair]
+    pack, proj, lse = attend(place, tokens, norm_gain, norm_bias, own_attend, brought)
+    passed.append(passed_on(fourth, (tokens,), (lse,)))
+    brought = [block for pair in passed for block in pair]
     middle, second_low = merge(
         place, tokens, pack, norm_gain, norm_bias, (own_merge, *brought[6:])
     )
@@ -1474,13 +1627,11 @@
 
     if direct:
         groups = at.groups[1:]
-        down_sum = after(down_keep, tail_own).astype(F32) + swap(down_send).astype(F32)
-        down_sum = down_sum.astype(BF).reshape(2, 4, HALF, BLOCK)
-        up_sum = after(up_keep, tail_own).astype(F32) + partner(up_send, "dp", 2).astype(F32)
-        up_sum = up_sum.astype(BF).reshape(2, 4, HALF, BLOCK)
-        down_brought = partner(down_sum[1], "dp", 2)
-        up_brought = swap(up_sum[1])
-        started = (down_sum, up_sum)
+        down_came, up_came = swap(down_send), partner(up_send, "dp", 2)
+        down_next, up_next = first_sums(down_keep, down_came, up_keep, up_came, tail_own)
+        down_brought = partner(down_next, "dp", 2)
+        up_brought = swap(up_next)
+        started = (down_next, up_next)
     else:
         groups = at.groups
         started = (down_keep, up_keep)
@@ -1504,22 +1655,22 @@
         started,
     )
     if direct:
-        wide = [
-            (down_sum[0].astype(F32) + after(down_brought, send).astype(F32)).astype(BF),
-            (up_sum[0].astype(F32) + after(up_brought, send).astype(F32)).astype(BF),
-        ]
-        wide = jnp.stack(wide, axis=1)
+        wide = second_sums(
+            down_keep, down_came, down_brought, up_keep, up_came, up_brought, send
+        )
         shared = partner(after(send, wide), "dp", 2)
         crossed = swap(after(cross_send, wide))
-        cross = (cross_keep.astype(F32) + crossed.astype(F32)).astype(BF)
-        cross_brought = partner(cross[1], "dp", 2)
-        keep = after(keep, cross)
-        square = (keep.astype(F32) + shared.astype(F32)).astype(BF)
-        cross = (cross[0].astype(F32) + after(cross_brought, square).astype(F32)).astype(BF)
-        square = jnp.concatenate([square, cross], axis=1)
-        wide = at.reduced(wide, groups)
-        square = at.reduced(after(square, wide), groups)
-        field_grads, result = after((field_grads, result), cross_brought)
+        wide = at.last(wide, groups[0])
+        cross_next = third_sums(cross_keep, crossed)
+        cross_brought = partner(cross_next, "dp", 2)
+        field_grads, result = after((field_grads, result), cross_next)
+        came = swap(jnp.where(first, result, tokens))
+        field_halves = field_grads.reshape(2, half_vars, rows, cols)
+        field_came = swap(pick(field_halves, 1 - pipe).astype(BF)).astype(F32)
+        square = fourth_sums(
+            keep, shared, cross_keep, crossed, cross_brought, (came, field_came, wide)
+        )
+        square = at.last(square, groups[0])
     else:
         wide = jnp.stack([at.reduced(array, groups) for array in wide])
 
@@ -1533,6 +1684,9 @@
             rows_of(array[:, n * ROWS : (n + 1) * ROWS]) for array in (whole, cross) for n in (0, 1)
         ]
         square = at.reduced(at.grouped(jnp.concatenate(square, axis=1)), groups)
+        came = swap(jnp.where(first, result, tokens))
+        field_halves = field_grads.reshape(2, half_vars, rows, cols)
+        field_came = swap(pick(field_halves, 1 - pipe).astype(BF)).astype(F32)
 
     wide = wide.reshape(2, HALF, 2, ff_width)
     other = partner(pick(wide, 1 - core, 2).astype(BF), "dp", 1).astype(F32)
@@ -1543,37 +1697,52 @@
     down_part, up_part = wide[0].T, wide[1]
 
     lot = 2 * d_width
-    part = TAIL // (2 * at.chips)
+    part = TAIL // at.chips
     query_part = square[:lot]
-    tail = square[lot : lot + 2 * part]
-    merge_sum = square[lot + 2 * part : 2 * lot + 2 * part]
-    cross = square[2 * lot + 2 * part :]
-    sent = jnp.concatenate(
-        [query_part, cross, jnp.where(first, tail[part:], tail[:part])], axis=0
-    ).astype(BF)
-    came = swap(sent).astype(F32)
+    tail = square[lot : lot + part]
+    merge_sum = square[lot + part : 2 * lot + part]
+    cross = square[2 * lot + part :]
+    tail_came = swap(tail.astype(BF)).astype(F32)
+    sent = jnp.concatenate([query_part, cross], axis=0).astype(BF)
+    section_came = swap(sent).astype(F32)
     section_sum = jnp.stack(
-        [merge_sum, query_part + came[:lot], came[lot : 2 * lot], cross]
-    )
-    tail = (jnp.where(first, tail[:part], tail[part:]) + came[2 * lot :]).astype(BF)
+        [merge_sum, query_part + section_came[:lot], section_came[lot:], cross]
+    )
+    tail = (tail.astype(BF).astype(F32) + tail_came).astype(BF)
     section_sum = section_sum.reshape(4, 2, d_width, HALF).transpose(1, 0, 2, 3)
     section_part = at.over_cores(section_sum)
     merge_part = section_part[0]
     second_attend = section_part[1:]
 
-    tail = at.gather(jnp.stack([tail, swap(tail)]))
+    tail = at.gather(tail)
     tail = jnp.stack([tail, partner(tail, "dp", 1)])
-    spot = jnp.stack([pipe, core, chip]).astype(jnp.int32)
-    position_sum, table_mix, small, key_grads, key_query_grads, query_low, query_sum = finish(
-        spot, tail, table, own_attend, at.chips
-    )
-    table_mix = table_mix[:, :ROWS_TABLE].astype(BF)
-    hidden_sum = small[5:9].reshape(FF)
-
-    came = swap(jnp.where(first, result, tokens))
+    spot = jnp.stack([pipe, core, side, chip, at.dp]).astype(jnp.int32)
+    (
+        position_sum,
+        gain_sum,
+        bias_sum,
+        output_sum,
+        hidden_sum,
+        embed_grads,
+        variable_grads,
+        first_attend,
+        query_sum,
+    ) = finish(
+        spot,
+        tail,
+        table,
+        query,
+        jnp.broadcast_to(given, (HEADS, D)),
+        tvt,
+        own_attend,
+        [*passed[2], *passed[3], *passed[1]],
+        at.chips,
+        d_width,
+    )
+    attend_part = jnp.where(first, first_attend, second_attend)
+    hidden_sum = hidden_sum.reshape(FF)
+
     outputs = jnp.stack([jnp.where(first, tokens, came), jnp.where(first, came, result)])
-    field_halves = field_grads.reshape(2, half_vars, rows, cols)
-    field_came = swap(pick(field_halves, 1 - pipe).astype(BF)).astype(F32)
     field_own = pick(field_halves, pipe)
     own_scale = lax.rsqrt(spread_new + EPSILON)
     field_out = (
@@ -1585,37 +1754,6 @@
         )
         * own_scale[None, :, None, None]
     )
-
-    query_sum = from_first(query_sum[:1])
-    own_rows = at.dp * d_width
-    query_rows = lax.dynamic_slice_in_dim(variable_query, own_rows, d_width).astype(F32)
-    key_rows = lax.dynamic_slice_in_dim(key_query_grads, own_rows, d_width, 1)
-    key_rows = key_rows.T[:, :, None] * query[0].reshape(1, HEADS, HDIM) * scale_heads
-    table_rows = lax.dynamic_slice_in_dim(table, own_rows, d_width, 1)
-    first_attend = jnp.stack(
-        [
-            query_rows[:, None] * query_low[:1],
-            key_rows.reshape(d_width, D),
-            dot(table_rows, table_mix, 0, 1),
-        ]
-    )
-    attend_part = jnp.where(first, first_attend, second_attend)
-
-    value_pair = passed[1][0]
-    value_pair = jnp.where(side == 0, value_pair, value_pair[::-1]).reshape(HALF, D)
-    value_own = lax.dynamic_slice(own_attend, (jnp.int32(2), core * HALF, jnp.int32(0)), (1, HALF, D))
-    value_own = jnp.where(first, value_own[0], value_pair)
-    table_half = dot(table_mix, value_own, 0, 1)
-    beside = partner(table_half, "dp", 1)
-    key_query = tvt[:, ROWS_TABLE:].astype(F32)
-    table_sum = jnp.concatenate(
-        [jnp.where(core == 0, table_half, beside), jnp.where(core == 0, beside, table_half)],
-        axis=1,
-    ) + lax.dot_general(
-        key_grads, key_query, (((1,), (1,)), ((), ())), precision=PRECISE
-    )
-    embed_grads = table_sum[: VARS * PIECES].reshape(PIECES, VARS, D).transpose(1, 0, 2)
-    variable_grads = table_sum[VARS * PIECES :]
     hidden_part = lax.dynamic_slice_in_dim(
         hidden_sum, (pipe * at.size + at.dp) * ff_width, ff_width
     )
@@ -1629,12 +1767,12 @@
         attend_part[None],
         merge_part[None],
         position_sum,
-        small[0:2],
-        small[2:4],
+        gain_sum,
+        bias_sum,
         up_part,
         hidden_part,
         down_part,
-        small[4],
+        output_sum.reshape(D),
     )
 
 

time: 495 us -> 457 us (0.923)
  other arithmetic: 50.2 us -> 31.2 us
  Pallas kernels: 165 us -> 183 us
  local copies, waits for them, and re-layouts: 37.7 us -> 21.1 us
  starting transfers between devices: 66.2 us -> 57.3 us
    pallas_call x0 -> x4, Pallas kernels: none -> 15.5 us  [the longest x1 4.63 us: second_sums(): pl.pallas_call(second_sums_kernel, grid=(1,), in_specs=[half, half, VMEM]...]
    slice x11 -> x1, local copies, waits for them, and re-layouts: 11.6 us -> 0.02 us  [on_device(): section_came[lot:]]
    unnamed x78 -> x94, local copies, waits for them, and re-layouts: 3.96 us -> 12.1 us
    ppermute x2 -> x0, waiting for transfers between devices: 7.23 us -> none  [the longest x1 6.69 us: on_device(): lax.ppermute(after(quarter(own_merge), chunk, passed[1][0]), 'pipe', [(1,...]
    convert_element_type x10 -> x4, other arithmetic: 7.7 us -> 1.37 us  [the longest x1 0.69 us: on_device(): field_came = swap(pick(field_halves, 1 - pipe).astype(BF)).astype(F32)]
    squeeze x5 -> x0, local copies, waits for them, and re-layouts: 6.09 us -> none  [the longest x1 2.45 us: on_device(): up_brought = swap(up_sum[1])]
    convert_element_type x3 -> x0, local copies, waits for them, and re-layouts: 5.15 us -> none  [the longest x1 3.11 us: on_device(): down_sum[0].astype(F32) + after(down_brought, send).astype(F32)]
    ppermute x46 -> x47, waiting for transfers between devices: 153 us -> 156 us  [partner(): return lax.ppermute(block, axis, [(i, i ^ distance) for i in range(size)])]
  transfers between devices with their start and end apart: 51 -> 49, of which waited for: 18 -> 19; matrix products, arithmetic and copies ran while one was open for 14% -> 7% of each run, Pallas kernels for 25% -> 30%
where the time goes in v1:
time: 457 us; the launch traced here: 454 us
  Pallas kernels  183 us (40%)
  waiting for transfers between devices  156 us (34%)
  starting transfers between devices  57.3 us (13%)
  other arithmetic  31.2 us (7%)
  local copies, waits for them, and re-layouts  21.1 us (5%)
  between operations  4.96 us (1%)
    ppermute x47, waiting for transfers between devices, partner(): return lax.ppermute(block, axis, [(i, i ^ distance) for i in range(size)])  156 us
    ppermute x47, starting transfers between devices, partner(): return lax.ppermute(block, axis, [(i, i ^ distance) for i in range(size)])  52.4 us
    pallas_call x1, Pallas kernels, attend_back(): pl.pallas_call(attend_back_kernel, out_shape=(shape((4, PATCHES, HALF), B...  29.4 us
    pallas_call x1, Pallas kernels, expand(): pl.pallas_call(expand_kernel, out_shape=(shape((2, PATCHES, UNITS), BF),...  21.6 us
    pallas_call x1, Pallas kernels, attend(): pl.pallas_call(attend_kernel, out_shape=(shape((2 * D, PATCHES), BF), sha...  20.5 us
    pallas_call x2, Pallas kernels, wide_grads(): pl.pallas_call(functools.partial(wide_kernel, which, by_pipe), in_specs=[...  17.6 us
    pallas_call x1, Pallas kernels, contract(): pl.pallas_call(contract_kernel, out_shape=(shape((PATCHES, D), BF), shape...  17 us
    pallas_call x1, Pallas kernels, aggregate_back(): pl.pallas_call(aggregate_back_kernel, out_shape=(shape((TAIL, HALF), BF),...  16 us
  transfers between devices with their start and end apart: 49, of which 19 were waited for; matrix products, arithmetic and copies ran while one was open for 7% of the time, Pallas kernels for 30%

profile of v1, /device:TPU:0, one launch (start us, length us, event | category | flops | bytes accessed | tf_op | source)
XLA Modules:
  0.0 453.7 jit_solution(6659519606395147132)
XLA Ops:
  2.9 3.0 collective-permute-start.4
  9.0 5.7 %tables.1 = (f32[16,1024]{1,0:T(8,128)}, f32[240,16]{1,0:T(8,128)}, f32[1024,256]{1,0:T(8,128)}) custom-call(f32[1,1024]{1,0:T(1,128)} %bitcast.157, bf16[240,1024]{1,0:T(8,128)(2,1)} %pad_maximum_fusion.9.table_ref, bf16[3,1024,1024]{2,1,0:T(8,128)(2,1)} %bitcast.123), custom_call_target="tpu_custom_call" | custom-call | flops 1000 | bytes 1000 | tf_op jit(solution)/shard_map/tables/pallas_call | solution.py:145
  19.0 3.4 collective-permute-start.10
  36.5 8.2 %collective-permute-done.6 = bf16[256,1024]{1,0:T(8,128)(2,1)S(1)} collective-permute-done((bf16[256,1024]{1,0:T(8,128)(2,1)S(1)}, bf16[256,1024]{1,0:T(8,128)(2,1)S(1)}, u32[]{:S(2)}, u32[]{:S(2)}) %collective-permute-start.6) | collective-permute-done | bytes 524320 | tf_op jit(solution)/shard_map/ppermute | solution.py:1343
  52.5 9.3 %collective-permute-done.7 = bf16[256,1024]{1,0:T(8,128)(2,1)} collective-permute-done((bf16[256,1024]{1,0:T(8,128)(2,1)S(1)}, bf16[256,1024]{1,0:T(8,128)(2,1)}, u32[]{:S(2)}, u32[]{:S(2)}) %collective-permute-start.7) | collective-permute-done | bytes 524320 | tf_op jit(solution)/shard_map/ppermute | solution.py:1343
  70.8 11.7 %aggregate.1 = (bf16[512,1024]{1,0:T(8,128)(2,1)}, bf16[1024,512]{1,0:T(8,128)(2,1)}, f32[16,48,512]{2,1,0:T(8,128)}, f32[4,48,512]{2,1,0:T(8,128)}) custom-call(s32[3]{0:T(128)} %pad_add_fusion.place_ref, f32[1]{0:T(128)} %dynamic_slice.59.alive_ref, f32[384,128]{1,0:T(8,128)} %get-tuple-element.217.own_field_ref, f32[384,128]{1,0:T(8,128)} %copy-done.34, ...), custom_call_target="tpu_custom_call" | custom-call | flops 1000 | bytes 1000 | tf_op jit(solution)/shard_map/aggregate/pallas_call | solution.py:272
  87.5 20.5 %attend.1 = (bf16[2048,512]{1,0:T(8,128)(2,1)}, bf16[3,512,1024]{2,1,0:T(8,128)(2,1)}, f32[8,2,512]{2,1,0:T(2,128)}) custom-call(s32[3]{0:T(128)} %pad_add_fusion.place_ref, bf16[512,1024]{1,0:T(8,128)(2,1)} %get-tuple-element.92.tokens_ref, f32[2,1024]{1,0:T(2,128)} %gain_ref.5, f32[2,1024]{1,0:T(2,128)} %bias_ref.3, bf16[3,1024,1024]{2,1,0:T(8,128)(2,1)} %bitcast.124, ...), custom_call_target="tpu_custom_call" | custom-call | flops 1000 | bytes 1000 | tf_op jit(solution)/shard_map/attend/pallas_call | solution.py:346
  113.4 8.5 %merge.1 = (f32[512,1024]{1,0:T(8,128)}, bf16[512,1024]{1,0:T(8,128)(2,1)}) custom-call(s32[3]{0:T(128)} %pad_add_fusion.place_ref, bf16[512,1024]{1,0:T(8,128)(2,1)} %get-tuple-element.92.tokens_ref, bf16[2048,512]{1,0:T(8,128)(2,1)} %get-tuple-element.94.pack_ref.pack_own, f32[2,1024]{1,0:T(2,128)} %gain_ref.5, f32[2,1024]{1,0:T(2,128)} %bias_ref.3, ...), custom_call_target="tpu_custom_call" | custom-call | flops 1000 | bytes 1000 | tf_op jit(solution)/shard_map/merge/pallas_call | solution.py:401
  122.9 21.6 %expand.1 = (bf16[2,512,4608]{2,1,0:T(8,128)(2,1)}, f32[1,4096]{1,0:T(1,128)}) custom-call(s32[3]{0:T(128)} %pad_add_fusion.place_ref, bf16[512,1024]{1,0:T(8,128)(2,1)} %get-tuple-element.99.second_ref.left_any, bf16[512,1024]{1,0:T(8,128)(2,1)} %fusion.out_ref.left_any, f32[1,4096]{1,0:T(1,128)} %bitcast.154, bf16[1024,4096]{1,0:T(8,128)(2,1)} %up_any.3, ...), custom_call_target="tpu_custom_call" | custom-call | flops 1000 | bytes 1000 | tf_op jit(solution)/shard_map/expand/pallas_call | solution.py:514
  147.0 17.0 %contract.1 = (bf16[512,1024]{1,0:T(8,128)(2,1)}, f32[512,1024]{1,0:T(8,128)}, bf16[512,1024]{1,0:T(8,128)(2,1)}, f32[1,1024]{1,0:T(1,128)}, f32[1,1024]{1,0:T(1,128)}, /*index=5*/f32[1,1024]{1,0:T(1,128)}) custom-call(s32[3]{0:T(128)} %pad_add_fusion.place_ref, f32[2]{0:T(128)} %pad_maximum_fusion.15.scalars_ref, f32[1,1024]{1,0:T(1,128)} %slice.66.gain_ref, ...), custom_call_target="tpu_custom_call" | custom-call | flops 1000 | bytes 1000 | tf_op jit(solution)/shard_map/contract/pallas_call | solution.py:620
  164.0 8.7 %down_grads.1 = (bf16[2,2,2,512,256]{4,3,2,1,0:T(8,128)(2,1)}, bf16[2,2,2,512,256]{4,3,2,1,0:T(8,128)(2,1)}) custom-call(s32[2]{0:T(128)} %pad_add_fusion.1.place_ref, bf16[512,1024]{1,0:T(8,128)(2,1)} %fusion.out_ref.left_any, bf16[2,512,4608]{2,1,0:T(8,128)(2,1)} %get-tuple-element.101.units_any.own_any, ...), custom_call_target="tpu_custom_call" | custom-call | flops 1000 | bytes 1000 | tf_op jit(solution)/shard_map/down_grads/pallas_call | solution.py:983
  173.1 8.9 %up_grads.1 = (bf16[2,2,2,512,256]{4,3,2,1,0:T(8,128)(2,1)}, bf16[2,2,2,512,256]{4,3,2,1,0:T(8,128)(2,1)}) custom-call(s32[2]{0:T(128)} %pad_add_fusion.1.place_ref, bf16[512,1024]{1,0:T(8,128)(2,1)} %get-tuple-element.99.second_ref.left_any, bf16[2,512,4608]{2,1,0:T(8,128)(2,1)} %get-tuple-element.101.units_any.own_any, ...), custom_call_target="tpu_custom_call" | custom-call | flops 1000 | bytes 1000 | tf_op jit(solution)/shard_map/up_grads/pallas_call | solution.py:983
  183.2 29.4 %attend_back.1 = (bf16[4,512,512]{2,1,0:T(8,128)(2,1)}, bf16[4,512,512]{2,1,0:T(8,128)(2,1)}, bf16[512,1024]{1,0:T(8,128)(2,1)}, f32[1,1024]{1,0:T(1,128)}, f32[1,1024]{1,0:T(1,128)}) custom-call(s32[3]{0:T(128)} %pad_add_fusion.place_ref, f32[512,1024]{1,0:T(8,128)} %get-tuple-element.103.grad_ref, bf16[512,1024]{1,0:T(8,128)(2,1)} %get-tuple-element.104.refs_0_.branch_ref, ...), custom_call_target="tpu_custom_call" | custom-call | flops 1000 | bytes 1000 | tf_op jit(solution)/shard_map/attend_back/pallas_call | solution.py:750
  213.3 16.0 %aggregate_back.1 = (bf16[1024,512]{1,0:T(8,128)(2,1)}, bf16[1024,512]{1,0:T(8,128)(2,1)}, f32[768,128]{1,0:T(8,128)}) custom-call(s32[3]{0:T(128)} %pad_add_fusion.place_ref, f32[1]{0:T(128)} %dynamic_slice.59.alive_ref, bf16[512,1024]{1,0:T(8,128)(2,1)} %get-tuple-element.108.token_grad_ref, f32[4,48,512]{2,1,0:T(8,128)} %get-tuple-element.109.pixels_ref, ...), custom_call_target="tpu_custom_call" | custom-call | flops 1000 | bytes 1000 | tf_op jit(solution)/shard_map/aggregate_back/pallas_call | solution.py:888
  231.5 3.9 first_sums.1
  239.7 11.3 %square_grads.1 = (bf16[4,256,512]{2,1,0:T(8,128)(2,1)}, bf16[4,256,512]{2,1,0:T(8,128)(2,1)}, bf16[2,4,256,512]{3,2,1,0:T(8,128)(2,1)}, bf16[2,4,256,512]{3,2,1,0:T(8,128)(2,1)}) custom-call(s32[2]{0:T(128)} %pad_add_fusion.2.place_ref, bf16[1024,512]{1,0:T(8,128)(2,1)} %get-tuple-element.119.after_any.tail_own, bf16[1024,512]{1,0:T(8,128)(2,1)} %copy-done.26, ...), custom_call_target="tpu_custom_call" | custom-call | flops 1000 | bytes 1000 | tf_op jit(solution)/shard_map/square_grads/pallas_call | solution.py:1106
  251.1 10.1 %collective-permute-done.27.down_brought = bf16[4,512,256]{2,1,0:T(8,128)(2,1)S(1)} collective-permute-done((bf16[4,512,256]{2,1,0:T(8,128)(2,1)}, bf16[4,512,256]{2,1,0:T(8,128)(2,1)S(1)}, u32[]{:S(2)}, u32[]{:S(2)}) %collective-permute-start.27) | collective-permute-done | bytes 1048608 | tf_op jit(solution)/shard_map/ppermute | solution.py:1343
  262.7 4.6 %second_sums.1 = (bf16[2,512,256]{2,1,0:T(8,128)(2,1)}, bf16[2,512,256]{2,1,0:T(8,128)(2,1)}, bf16[2,512,256]{2,1,0:T(8,128)(2,1)}, bf16[2,512,256]{2,1,0:T(8,128)(2,1)}) custom-call(bf16[2,2,2,512,256]{4,3,2,1,0:T(8,128)(2,1)} %get-tuple-element.106.refs_0_.refs_8_.down_keep, bf16[2,2,2,512,256]{4,3,2,1,0:T(8,128)(2,1)} %copy-done.12, ...), custom_call_target="tpu_custom_call" | custom-call | flops 1000 | bytes 1000 | tf_op jit(solution)/shard_map/second_sums/pallas_call | solution.py:1165
  269.1 3.6 collective-permute-start.36
  273.8 40.7 %collective-permute-done.29.came.cross_came = bf16[2,4,256,512]{3,2,1,0:T(8,128)(2,1)S(1)} collective-permute-done((bf16[2,4,256,512]{3,2,1,0:T(8,128)(2,1)}, bf16[2,4,256,512]{3,2,1,0:T(8,128)(2,1)S(1)}, u32[]{:S(2)}, u32[]{:S(2)}) %collective-permute-start.29) | collective-permute-done | bytes 2097184 | tf_op jit(solution)/shard_map/ppermute | solution.py:1343
  315.9 2.9 third_sums.1
  321.8 2.6 collective-permute-start.35
  326.9 18.9 %collective-permute-done.35 = bf16[2,512,256]{2,1,0:T(8,128)(2,1)S(1)} collective-permute-done((bf16[2,512,256]{2,1,0:T(8,128)(2,1)S(1)}, bf16[2,512,256]{2,1,0:T(8,128)(2,1)S(1)}, u32[]{:S(2)}, u32[]{:S(2)}) %collective-permute-start.35) | collective-permute-done | bytes 524320 | tf_op jit(solution)/shard_map/ppermute | solution.py:1343
  352.8 4.1 fourth_sums.1
  356.9 3.5 collective-permute-start.39
  363.5 10.5 %collective-permute-done.39 = bf16[512,512]{1,0:T(8,128)(2,1)} collective-permute-done((bf16[512,512]{1,0:T(8,128)(2,1)}, bf16[512,512]{1,0:T(8,128)(2,1)}, u32[]{:S(2)}, u32[]{:S(2)}) %collective-permute-start.39) | collective-permute-done | bytes 524320 | tf_op jit(solution)/shard_map/ppermute | solution.py:1343
  373.9 30.0 %collective-permute-done.38 = bf16[512,512]{1,0:T(8,128)(2,1)} collective-permute-done((bf16[512,512]{1,0:T(8,128)(2,1)}, bf16[512,512]{1,0:T(8,128)(2,1)}, u32[]{:S(2)}, u32[]{:S(2)}) %collective-permute-start.38) | collective-permute-done | bytes 524320 | tf_op jit(solution)/shard_map/ppermute | solution.py:1343
  407.1 3.6 collective-permute-done.40
  412.6 3.2 collective-permute-start.41
  419.0 3.8 collective-permute-done.42
  426.0 9.8 %collective-permute-done.44 = bf16[4,128,512]{2,1,0:T(8,128)(2,1)S(1)} collective-permute-done((bf16[4,128,512]{2,1,0:T(8,128)(2,1)S(1)}, bf16[4,128,512]{2,1,0:T(8,128)(2,1)S(1)}, u32[]{:S(2)}, u32[]{:S(2)}) %collective-permute-start.44) | collective-permute-done | bytes 524320 | tf_op jit(solution)/shard_map/ppermute | solution.py:1343
  442.4 8.3 %finish.1 = (f32[512,1024]{1,0:T(8,128)}, f32[2,1024]{1,0:T(2,128)}, f32[2,1024]{1,0:T(2,128)}, f32[1,1024]{1,0:T(1,128)}, f32[4,1024]{1,0:T(4,128)}, /*index=5*...) custom-call(s32[5]{0:T(128)} %stack.173.place_ref, ...), custom_call_target="tpu_custom_call" | custom-call | flops 1000 | bytes 1000 | tf_op jit(solution)/shard_map/finish/pallas_call | solution.py:1312
  (246 shorter events, 101.3 us)
Async XLA Ops:
  2.9 30.3 %collective-permute-start.4 = (bf16[256,1024]{1,0:T(8,128)(2,1)S(1)}, bf16[256,1024]{1,0:T(8,128)(2,1)S(1)}, u32[]{:S(2)}, u32[]{:S(2)}) collective-permute-start(bf16[256,1024]{1,0:T(8,128)(2,1)S(1)} %get-tuple-element.193), channel_id=1, source_target_pairs={{0,16},{16,0},{1,17},{17,1},{2,18},{18,2},{3,19},{19,3},{4,20},{20... | collective-permute-start | bytes 1572872 | tf_op jit(solution)/shard_map/ppermute | solution.py:1343
  16.9 52.9 %collective-permute-start.8 = (f32[384,128]{1,0:T(8,128)S(1)}, f32[384,128]{1,0:T(8,128)S(1)}, u32[]{:S(2)}, u32[]{:S(2)}) collective-permute-start(f32[384,128]{1,0:T(8,128)S(1)} %get-tuple-element.216), channel_id=1, source_target_pairs={{0,16},{16,0},{1,17},{17,1},{2,18},{18,2},{3,19},{19,3},{4,20},{20... | collective-permute-start | bytes 589832 | tf_op jit(solution)/shard_map/ppermute | solution.py:1343
  19.0 16.2 %collective-permute-start.10 = (f32[240,16]{1,0:T(8,128)}, f32[240,16]{1,0:T(8,128)S(1)}, u32[]{:S(2)}, u32[]{:S(2)}) collective-permute-start(f32[240,16]{1,0:T(8,128)} %get-tuple-element.91), channel_id=1, source_target_pairs={{0,16},{1,17},{2,18},{3,19},{4,20},{5,21},{6,22},{7,23},{8,24},{9,... | collective-permute-start | bytes 46088 | tf_op jit(solution)/shard_map/ppermute | solution.py:1482
  23.7 26.7 %collective-permute-start.11 = (bf16[1024,256]{1,0:T(8,128)(2,1)S(1)}, bf16[1024,256]{1,0:T(8,128)(2,1)S(1)}, u32[]{:S(2)}, u32[]{:S(2)}) collective-permute-start(bf16[1024,256]{1,0:T(8,128)(2,1)S(1)} %convert_element_type.90), channel_id=1, source_target_pairs={{0,16},{1,17},{2,18},{3,19},{4,20},{5,21},{6,22},{7,23},{8,24},{9,... | collective-permute-start | bytes 1572872 | tf_op jit(solution)/shard_map/ppermute | solution.py:1482
  47.7 14.1 %collective-permute-start.7 = (bf16[256,1024]{1,0:T(8,128)(2,1)S(1)}, bf16[256,1024]{1,0:T(8,128)(2,1)}, u32[]{:S(2)}, u32[]{:S(2)}) collective-permute-start(bf16[256,1024]{1,0:T(8,128)(2,1)S(1)} %get-tuple-element.89), channel_id=1, source_target_pairs={{0,16},{16,0},{1,17},{17,1},{2,18},{18,2},{3,19},{19,3},{4,20},{20... | collective-permute-start | bytes 1572872 | tf_op jit(solution)/shard_map/ppermute | solution.py:1343
  50.3 19.5 %collective-permute-start.12 = (bf16[2,256,1024]{2,1,0:T(8,128)(2,1)S(1)}, bf16[2,256,1024]{2,1,0:T(8,128)(2,1)S(1)}, u32[]{:S(2)}, u32[]{:S(2)}) collective-permute-start(bf16[2,256,1024]{2,1,0:T(8,128)(2,1)S(1)} %pad_maximum_fusion.1.brought_ref.refs_0_), channel_id=1, source_target_pairs={{0,1},{1,0},{2,3},{3,2},{4,5},{5,4},{6,7},{7,6},{8,9},{9,8},{10,11... | collective-permute-start | bytes 3145736 | tf_op jit(solution)/shard_map/ppermute | solution.py:1343
  50.3 13.1 %collective-permute-start.9 = (f32[2,24]{1,0:T(2,128)S(1)}, f32[2,24]{1,0:T(2,128)S(1)}, u32[]{:S(2)}, u32[]{:S(2)}) collective-permute-start(f32[2,24]{1,0:T(2,128)S(1)} %pad_maximum_fusion.12), channel_id=1, source_target_pairs={{0,16},{16,0},{1,17},{17,1},{2,18},{18,2},{3,19},{19,3},{4,20},{20... | collective-permute-start | bytes 584 | tf_op jit(solution)/shard_map/ppermute | solution.py:1343
  51.3 15.0 %collective-permute-start.13 = (bf16[256,1024]{1,0:T(8,128)(2,1)}, bf16[256,1024]{1,0:T(8,128)(2,1)}, u32[]{:S(2)}, u32[]{:S(2)}) collective-permute-start(bf16[256,1024]{1,0:T(8,128)(2,1)} %collective-permute-done.5), channel_id=1, source_target_pairs={{0,2},{1,3},{2,0},{3,1},{4,6},{5,7},{6,4},{7,5},{8,10},{9,11},{10,... | collective-permute-start | bytes 1572872 | tf_op jit(solution)/shard_map/ppermute | solution.py:1343
  61.8 20.8 %collective-permute-start.15 = (bf16[256,1024]{1,0:T(8,128)(2,1)}, bf16[256,1024]{1,0:T(8,128)(2,1)S(1)}, u32[]{:S(2)}, u32[]{:S(2)}) collective-permute-start(bf16[256,1024]{1,0:T(8,128)(2,1)} %collective-permute-done.7), channel_id=1, source_target_pairs={{0,2},{1,3},{2,0},{3,1},{4,6},{5,7},{6,4},{7,5},{8,10},{9,11},{10,... | collective-permute-start | bytes 1572872 | tf_op jit(solution)/shard_map/ppermute | solution.py:1343
  67.6 17.5 %collective-permute-start.14 = (bf16[2,256,1024]{2,1,0:T(8,128)(2,1)S(1)}, bf16[2,256,1024]{2,1,0:T(8,128)(2,1)S(1)}, u32[]{:S(2)}, u32[]{:S(2)}) collective-permute-start(bf16[2,256,1024]{2,1,0:T(8,128)(2,1)S(1)} %pad_maximum_fusion.2.refs_2_.refs_4_), channel_id=1, source_target_pairs={{0,1},{1,0},{2,3},{3,2},{4,5},{5,4},{6,7},{7,6},{8,9},{9,8},{10,11... | collective-permute-start | bytes 3145736 | tf_op jit(solution)/shard_map/ppermute | solution.py:1343
  67.7 16.2 %collective-permute-start.17 = (bf16[256,1024]{1,0:T(8,128)(2,1)S(1)}, bf16[256,1024]{1,0:T(8,128)(2,1)S(1)}, u32[]{:S(2)}, u32[]{:S(2)}) collective-permute-start(bf16[256,1024]{1,0:T(8,128)(2,1)S(1)} %get-tuple-element.95), channel_id=1, source_target_pairs={{0,16},{16,0},{1,17},{17,1},{2,18},{18,2},{3,19},{19,3},{4,20},{20... | collective-permute-start | bytes 1572872 | tf_op jit(solution)/shard_map/ppermute | solution.py:1343
  84.0 24.1 %collective-permute-start.18 = (bf16[256,1024]{1,0:T(8,128)(2,1)S(1)}, bf16[256,1024]{1,0:T(8,128)(2,1)S(1)}, u32[]{:S(2)}, u32[]{:S(2)}) collective-permute-start(bf16[256,1024]{1,0:T(8,128)(2,1)S(1)} %collective-permute-done.17), channel_id=1, source_target_pairs={{0,2},{1,3},{2,0},{3,1},{4,6},{5,7},{6,4},{7,5},{8,10},{9,11},{10,... | collective-permute-start | bytes 1572872 | tf_op jit(solution)/shard_map/ppermute | solution.py:1343
  108.4 13.5 %collective-permute-start.20 = (bf16[1024,512]{1,0:T(8,128)(2,1)S(1)}, bf16[1024,512]{1,0:T(8,128)(2,1)S(1)}, u32[]{:S(2)}, u32[]{:S(2)}) collective-permute-start(bf16[1024,512]{1,0:T(8,128)(2,1)S(1)} %copy-done.22), channel_id=1, source_target_pairs={{0,1},{1,0},{2,3},{3,2},{4,5},{5,4},{6,7},{7,6},{8,9},{9,8},{10,11... | collective-permute-start | bytes 3145736 | tf_op jit(solution)/shard_map/ppermute | solution.py:1343
  144.5 19.6 %collective-permute-start.21 = (bf16[2,512,4608]{2,1,0:T(8,128)(2,1)}, bf16[2,512,4608]{2,1,0:T(8,128)(2,1)}, u32[]{:S(2)}, u32[]{:S(2)}) collective-permute-start(bf16[2,512,4608]{2,1,0:T(8,128)(2,1)} %get-tuple-element.101.units_any.own_any), channel_id=1, source_target_pairs={{0,1},{1,0},{2,3},{3,2},{4,5},{5,4},{6,7},{7,6},{8,9},{9,8},{10,11... | collective-permute-start | bytes 28311560 | tf_op jit(solution)/shard_map/ppermute | solution.py:1343
  172.8 56.6 %collective-permute-start.25 = (bf16[2,2,2,512,256]{4,3,2,1,0:T(8,128)(2,1)}, bf16[2,2,2,512,256]{4,3,2,1,0:T(8,128)(2,1)S(1)}, u32[]{:S(2)}, u32[]{:S(2)}) collective-permute-start(bf16[2,2,2,512,256]{4,3,2,1,0:T(8,128)(2,1)} %get-tuple-element.123), channel_id=1, source_target_pairs={{0,16},{16,0},{1,17},{17,1},{2,18},{18,2},{3,19},{19,3},{4,20},{20... | collective-permute-start | bytes 6291464 | tf_op jit(solution)/shard_map/ppermute | solution.py:1343
  182.0 47.9 %collective-permute-start.26 = (bf16[2,2,2,512,256]{4,3,2,1,0:T(8,128)(2,1)}, bf16[2,2,2,512,256]{4,3,2,1,0:T(8,128)(2,1)S(1)}, u32[]{:S(2)}, u32[]{:S(2)}) collective-permute-start(bf16[2,2,2,512,256]{4,3,2,1,0:T(8,128)(2,1)} %get-tuple-element.124), channel_id=1, source_target_pairs={{0,2},{1,3},{2,0},{3,1},{4,6},{5,7},{6,4},{7,5},{8,10},{9,11},{10,... | collective-permute-start | bytes 6291464 | tf_op jit(solution)/shard_map/ppermute | solution.py:1343
  183.2 55.5 %collective-permute-start.23 = (bf16[2048,512]{1,0:T(8,128)(2,1)S(1)}, bf16[2048,512]{1,0:T(8,128)(2,1)}, u32[]{:S(2)}, u32[]{:S(2)}) collective-permute-start(bf16[2048,512]{1,0:T(8,128)(2,1)S(1)} %copy-done.11), channel_id=1, source_target_pairs={{0,1},{1,0},{2,3},{3,2},{4,5},{5,4},{6,7},{7,6},{8,9},{9,8},{10,11... | collective-permute-start | bytes 6291464 | tf_op jit(solution)/shard_map/ppermute | solution.py:1343
  212.7 26.0 %collective-permute-start.24 = (bf16[4,512,512]{2,1,0:T(8,128)(2,1)}, bf16[4,512,512]{2,1,0:T(8,128)(2,1)}, u32[]{:S(2)}, u32[]{:S(2)}) collective-permute-start(bf16[4,512,512]{2,1,0:T(8,128)(2,1)} %get-tuple-element.122), channel_id=1, source_target_pairs={{0,1},{1,0},{2,3},{3,2},{4,5},{5,4},{6,7},{7,6},{8,9},{9,8},{10,11... | collective-permute-start | bytes 6291464 | tf_op jit(solution)/shard_map/ppermute | solution.py:1343
  235.4 25.8 %collective-permute-start.27 = (bf16[4,512,256]{2,1,0:T(8,128)(2,1)}, bf16[4,512,256]{2,1,0:T(8,128)(2,1)S(1)}, u32[]{:S(2)}, u32[]{:S(2)}) collective-permute-start(bf16[4,512,256]{2,1,0:T(8,128)(2,1)} %get-tuple-element.125.refs_0_), channel_id=1, source_target_pairs={{0,2},{1,3},{2,0},{3,1},{4,6},{5,7},{6,4},{7,5},{8,10},{9,11},{10,... | collective-permute-start | bytes 3145736 | tf_op jit(solution)/shard_map/ppermute | solution.py:1343
  236.4 25.3 %collective-permute-start.28 = (bf16[4,512,256]{2,1,0:T(8,128)(2,1)}, bf16[4,512,256]{2,1,0:T(8,128)(2,1)S(1)}, u32[]{:S(2)}, u32[]{:S(2)}) collective-permute-start(bf16[4,512,256]{2,1,0:T(8,128)(2,1)} %get-tuple-element.126.refs_1_), channel_id=1, source_target_pairs={{0,16},{16,0},{1,17},{17,1},{2,18},{18,2},{3,19},{19,3},{4,20},{20... | collective-permute-start | bytes 3145736 | tf_op jit(solution)/shard_map/ppermute | solution.py:1343
  267.3 47.2 %collective-permute-start.29 = (bf16[2,4,256,512]{3,2,1,0:T(8,128)(2,1)}, bf16[2,4,256,512]{3,2,1,0:T(8,128)(2,1)S(1)}, u32[]{:S(2)}, u32[]{:S(2)}) collective-permute-start(bf16[2,4,256,512]{3,2,1,0:T(8,128)(2,1)} %get-tuple-element.134), channel_id=1, source_target_pairs={{0,16},{16,0},{1,17},{17,1},{2,18},{18,2},{3,19},{19,3},{4,20},{20... | collective-permute-start | bytes 6291464 | tf_op jit(solution)/shard_map/ppermute | solution.py:1343
  269.1 55.3 %collective-permute-start.36 = (bf16[2,512,256]{2,1,0:T(8,128)(2,1)}, bf16[2,512,256]{2,1,0:T(8,128)(2,1)S(1)}, u32[]{:S(2)}, u32[]{:S(2)}) collective-permute-start(bf16[2,512,256]{2,1,0:T(8,128)(2,1)} %get-tuple-element.133), channel_id=1, source_target_pairs={{0,12},{1,13},{2,14},{3,15},{4,8},{5,9},{6,10},{7,11},{8,4},{9,5},... | collective-permute-start | bytes 1572872 | tf_op jit(solution)/shard_map/ppermute | solution.py:1343
  272.7 78.4 %collective-permute-start.32 = (bf16[4,256,512]{2,1,0:T(8,128)(2,1)S(1)}, bf16[4,256,512]{2,1,0:T(8,128)(2,1)S(1)}, u32[]{:S(2)}, u32[]{:S(2)}) collective-permute-start(bf16[4,256,512]{2,1,0:T(8,128)(2,1)S(1)} %copy-done.27), channel_id=1, source_target_pairs={{0,2},{1,3},{2,0},{3,1},{4,6},{5,7},{6,4},{7,5},{8,10},{9,11},{10,... | collective-permute-start | bytes 3145736 | tf_op jit(solution)/shard_map/ppermute | solution.py:1343
  318.9 32.2 %collective-permute-start.30 = (bf16[512,1024]{1,0:T(8,128)(2,1)S(1)}, bf16[512,1024]{1,0:T(8,128)(2,1)S(1)}, u32[]{:S(2)}, u32[]{:S(2)}) collective-permute-start(bf16[512,1024]{1,0:T(8,128)(2,1)S(1)} %broadcast_select_fusion), channel_id=1, source_target_pairs={{0,16},{16,0},{1,17},{17,1},{2,18},{18,2},{3,19},{19,3},{4,20},{20... | collective-permute-start | bytes 3145736 | tf_op jit(solution)/shard_map/ppermute | solution.py:1343
  320.7 30.4 %collective-permute-start.33 = (bf16[4,256,512]{2,1,0:T(8,128)(2,1)S(1)}, bf16[4,256,512]{2,1,0:T(8,128)(2,1)S(1)}, u32[]{:S(2)}, u32[]{:S(2)}) collective-permute-start(bf16[4,256,512]{2,1,0:T(8,128)(2,1)S(1)} %copy-done.25), channel_id=1, source_target_pairs={{0,2},{1,3},{2,0},{3,1},{4,6},{5,7},{6,4},{7,5},{8,10},{9,11},{10,... | collective-permute-start | bytes 3145736 | tf_op jit(solution)/shard_map/ppermute | solution.py:1343
  321.8 24.0 %collective-permute-start.35 = (bf16[2,512,256]{2,1,0:T(8,128)(2,1)S(1)}, bf16[2,512,256]{2,1,0:T(8,128)(2,1)S(1)}, u32[]{:S(2)}, u32[]{:S(2)}) collective-permute-start(bf16[2,512,256]{2,1,0:T(8,128)(2,1)S(1)} %copy-done.45), channel_id=1, source_target_pairs={{0,8},{1,9},{2,10},{3,11},{4,12},{5,13},{6,14},{7,15},{8,0},{9,1},... | collective-permute-start | bytes 1572872 | tf_op jit(solution)/shard_map/ppermute | solution.py:1343
  324.4 22.7 %collective-permute-start.34 = (bf16[2,512,256]{2,1,0:T(8,128)(2,1)S(1)}, bf16[2,512,256]{2,1,0:T(8,128)(2,1)S(1)}, u32[]{:S(2)}, u32[]{:S(2)}) collective-permute-start(bf16[2,512,256]{2,1,0:T(8,128)(2,1)S(1)} %copy-done.44), channel_id=1, source_target_pairs={{0,4},{1,5},{2,6},{3,7},{4,0},{5,1},{6,2},{7,3},{8,12},{9,13},{10,... | collective-permute-start | bytes 1572872 | tf_op jit(solution)/shard_map/ppermute | solution.py:1343
  356.9 17.1 %collective-permute-start.39 = (bf16[512,512]{1,0:T(8,128)(2,1)}, bf16[512,512]{1,0:T(8,128)(2,1)}, u32[]{:S(2)}, u32[]{:S(2)}) collective-permute-start(bf16[512,512]{1,0:T(8,128)(2,1)} %get-tuple-element.142), channel_id=1, source_target_pairs={{0,12},{1,13},{2,14},{3,15},{4,8},{5,9},{6,10},{7,11},{8,4},{9,5},... | collective-permute-start | bytes 1572872 | tf_op jit(solution)/shard_map/ppermute | solution.py:1343
  360.4 43.6 %collective-permute-start.38 = (bf16[512,512]{1,0:T(8,128)(2,1)}, bf16[512,512]{1,0:T(8,128)(2,1)}, u32[]{:S(2)}, u32[]{:S(2)}) collective-permute-start(bf16[512,512]{1,0:T(8,128)(2,1)} %get-tuple-element.141), channel_id=1, source_target_pairs={{0,8},{1,9},{2,10},{3,11},{4,12},{5,13},{6,14},{7,15},{8,0},{9,1},... | collective-permute-start | bytes 1572872 | tf_op jit(solution)/shard_map/ppermute | solution.py:1343
  360.4 43.6 %collective-permute-start.37 = (bf16[512,512]{1,0:T(8,128)(2,1)}, bf16[512,512]{1,0:T(8,128)(2,1)}, u32[]{:S(2)}, u32[]{:S(2)}) collective-permute-start(bf16[512,512]{1,0:T(8,128)(2,1)} %get-tuple-element.140), channel_id=1, source_target_pairs={{0,4},{1,5},{2,6},{3,7},{4,0},{5,1},{6,2},{7,3},{8,12},{9,13},{10,... | collective-permute-start | bytes 1572872 | tf_op jit(solution)/shard_map/ppermute | solution.py:1343
  363.4 43.7 %collective-permute-start.48 = (bf16[2,512,128]{2,1,0:T(8,128)(2,1)S(1)}, bf16[2,512,128]{2,1,0:T(8,128)(2,1)S(1)}, u32[]{:S(2)}, u32[]{:S(2)}) collective-permute-start(bf16[2,512,128]{2,1,0:T(8,128)(2,1)S(1)} %convert_bitcast_fusion), channel_id=1, source_target_pairs={{0,1},{1,0},{2,3},{3,2},{4,5},{5,4},{6,7},{7,6},{8,9},{9,8},{10,11... | collective-permute-start | bytes 786440 | tf_op jit(solution)/shard_map/ppermute | solution.py:1343
  422.9 12.9 %collective-permute-start.44 = (bf16[4,128,512]{2,1,0:T(8,128)(2,1)S(1)}, bf16[4,128,512]{2,1,0:T(8,128)(2,1)S(1)}, u32[]{:S(2)}, u32[]{:S(2)}) collective-permute-start(bf16[4,128,512]{2,1,0:T(8,128)(2,1)S(1)} %get-tuple-element.213), channel_id=1, source_target_pairs={{0,2},{1,3},{2,0},{3,1},{4,6},{5,7},{6,4},{7,5},{8,10},{9,11},{10,... | collective-permute-start | bytes 1572872 | tf_op jit(solution)/shard_map/ppermute | solution.py:1343
  (63 other events, 478.7 us)

commit v2 on v1

--- a/solution.py
+++ b/solution.py
@@ -19,11 +19,11 @@
 HALF = D // 2
 QUARTER = D // 4
 TABLE_PAD = 256
-FF_TILE = 512
+FF_TILE = 1024
 FF_STEPS = FF // FF_TILE
 PAIRS = HEADS // 2
 LANES = 2 * HDIM
-CHUNK = 64
+CHUNK = 128
 TOKENS_BACK = 2
 
 PRECISE = lax.Precision.HIGHEST
@@ -257,10 +257,10 @@
 
     lax.fori_loop(0, HEADS, head, 0)
     wait(0)
-    heads = heads_ref[...]
+    heads = heads_ref[...].T
 
     def tile(columns):
-        merged = dot(heads, merge_ref[:, columns], 0, 0)
+        merged = dot(heads, merge_ref[:, columns], 1, 0)
         tokens_ref[:, columns] = (alive * (merged + position_ref[:, columns].astype(F32))).astype(
             BF
         )
@@ -363,55 +363,6 @@
     )(place, tokens, gain, bias, own_attend, *brought)
 
 
-def merge_kernel(
-    place_ref,
-    tokens_ref,
-    pack_ref,
-    gain_ref,
-    bias_ref,
-    own_ref,
-    brought_ref,
-    beside_ref,
-    middle_ref,
-    second_ref,
-    merge_ref,
-    sems,
-):
-    wait = section_copies(
-        place_ref, 1, [own_ref], [(brought_ref, beside_ref)], [merge_ref], sems
-    )
-    wait(0)
-    context = pack_ref[...]
-    column_tiles(
-        256,
-        lambda columns: middle_ref.__setitem__(
-            (slice(None), columns),
-            tokens_ref[:, columns].astype(F32) + dot(context, merge_ref[:, columns], 0, 0),
-        ),
-    )
-
-    def second_norm(rows):
-        xhat, _ = normalized(middle_ref[rows, :])
-        second_ref[rows, :] = (xhat * gain_ref[1:2, :] + bias_ref[1:2, :]).astype(BF)
-
-    row_chunks(second_norm)
-
-
-def merge(place, tokens, pack, gain, bias, weights):
-    return pl.pallas_call(
-        merge_kernel,
-        grid=(1,),
-        out_shape=(shape((PATCHES, D), F32), shape((PATCHES, D), BF)),
-        in_specs=[SMEM, VMEM, pl.BlockSpec((D, PATCHES), lambda i: (1, 0)), VMEM, VMEM]
-        + [ANYWHERE] * 3,
-        out_specs=(VMEM,) * 2,
-        scratch_shapes=[pltpu.VMEM((D, D), BF), pltpu.SemaphoreType.DMA((1, 4))],
-        compiler_params=params(1),
-        cost_estimate=cost(),
-        name="merge",
-    )(place, tokens, pack, gain, bias, *weights)
-
-
 def gelu_parts(hidden):
     inverse = 1.0 / (1.0 + 0.23164190 * jnp.abs(hidden))
     decay = jnp.exp2(hidden * hidden * (-0.72134752))
@@ -423,7 +374,7 @@
     return cdf, decay * 0.3989422804014327
 
 
-FF_PART = 256
+FF_PART = 1024
 UNITS = FF + HALF
 
 
@@ -447,17 +398,30 @@
 
 def expand_kernel(
     place_ref,
-    second_ref,
+    tokens_ref,
     out_ref,
+    gain_ref,
+    norm_bias_ref,
     bias_ref,
+    pack_any,
+    own_any,
+    brought_any,
+    beside_any,
     up_any,
     down_any,
     after_any,
     units_any,
+    middle_any,
+    second_any,
     sum_ref,
     up_ref,
     down_ref,
     tile_ref,
+    merge_ref,
+    context_ref,
+    middle_ref,
+    second_ref,
+    merge_sems,
     in_sems,
     out_sems,
 ):
@@ -468,17 +432,49 @@
             copy(down_any.at[part], down_ref.at[part], in_sems.at[j, 1]),
         )
 
+    def start(j):
+        for one in fetch(j):
+            one.start()
+
     def put(j, slot):
         return copy(
             tile_ref.at[slot], units_any.at[:, :, aligned(j, FF_TILE)], out_sems.at[slot]
         )
 
-    for j in range(FF_STEPS):
-        for one in fetch(j):
-            one.start()
+    context = copy(pack_any.at[pl.ds(D, D)], context_ref, in_sems.at[FF_STEPS, 0])
+    context.start()
+    wait = section_copies(
+        place_ref, 1, [own_any], [(brought_any, beside_any)], [merge_ref], merge_sems
+    )
+    start(0)
+    context.wait()
+    turned = context_ref[...].T
+    wait(0)
+    column_tiles(
+        512,
+        lambda columns: middle_ref.__setitem__(
+            (slice(None), columns),
+            tokens_ref[:, columns].astype(F32) + dot(turned, merge_ref[:, columns], 1, 0),
+        ),
+    )
+    middle_out = copy(middle_ref, middle_any, in_sems.at[FF_STEPS, 1])
+    middle_out.start()
+    start(1)
+
+    def second_norm(rows):
+        xhat, _ = normalized(middle_ref[rows, :])
+        second_ref[rows, :] = (xhat * gain_ref[1:2, :] + norm_bias_ref[1:2, :]).astype(BF)
+
+    row_chunks(second_norm)
+    second_out = copy(second_ref, second_any, out_sems.at[2])
+    second_out.start()
 
     def step(j, carry):
         slot = lax.rem(j, 2)
+
+        @pl.when(j + 2 < FF_STEPS)
+        def _():
+            start(j + 2)
 
         @pl.when(j >= 2)
         def _():
@@ -488,8 +484,8 @@
             one.wait()
         for part in range(FF_TILE // FF_PART):
             inner = slice(part * FF_PART, (part + 1) * FF_PART)
-            start = pl.multiple_of(j * FF_TILE + part * FF_PART, FF_PART)
-            columns = pl.ds(start, FF_PART)
+            begin = pl.multiple_of(j * FF_TILE + part * FF_PART, FF_PART)
+            columns = pl.ds(begin, FF_PART)
             hidden = dot(second_ref[...], up_ref[:, columns], 1, 0) + bias_ref[:, columns]
             grad = dot(out_ref[...], down_ref[columns, :], 1, 1)
             cdf, density = gelu_parts(hidden)
@@ -503,30 +499,45 @@
     lax.fori_loop(0, FF_STEPS, step, 0)
     others = aligned(1 - place_ref[1], HALF)
     put(FF_STEPS - 2, 0).wait()
-    tile_ref[0, 0] = out_ref[:, others]
-    tile_ref[0, 1] = second_ref[:, others]
-    put(FF_STEPS, 0).start()
+    tile_ref[0, 0, :, :HALF] = out_ref[:, others]
+    tile_ref[0, 1, :, :HALF] = second_ref[:, others]
+    end = copy(
+        tile_ref.at[0, :, :, pl.ds(0, HALF)], units_any.at[:, :, pl.ds(FF, HALF)], out_sems.at[0]
+    )
+    end.start()
+    middle_out.wait()
+    second_out.wait()
     put(FF_STEPS - 1, 1).wait()
-    put(FF_STEPS, 0).wait()
-
-
-def expand(place, second, out_low, up, bias, down, after):
+    end.wait()
+
+
+def expand(place, tokens, out_low, gain, norm_bias, pack, merge, up, bias, down, after):
     return pl.pallas_call(
         expand_kernel,
-        out_shape=(shape((2, PATCHES, UNITS), BF), shape((1, FF), F32)),
-        in_specs=[SMEM, VMEM, VMEM, VMEM, ANYWHERE, ANYWHERE, ANYWHERE],
-        out_specs=(ANYWHERE, VMEM),
+        out_shape=(
+            shape((2, PATCHES, UNITS), BF),
+            shape((PATCHES, D), F32),
+            shape((PATCHES, D), BF),
+            shape((1, FF), F32),
+        ),
+        in_specs=[SMEM] + [VMEM] * 5 + [ANYWHERE] * 7,
+        out_specs=(ANYWHERE, ANYWHERE, ANYWHERE, VMEM),
         scratch_shapes=[
             pltpu.VMEM((D, FF), BF),
             pltpu.VMEM((FF, D), BF),
             pltpu.VMEM((2, 2, PATCHES, FF_TILE), BF),
-            pltpu.SemaphoreType.DMA((FF_STEPS, 2)),
-            pltpu.SemaphoreType.DMA((2,)),
+            pltpu.VMEM((D, D), BF),
+            pltpu.VMEM((D, PATCHES), BF),
+            pltpu.VMEM((PATCHES, D), F32),
+            pltpu.VMEM((PATCHES, D), BF),
+            pltpu.SemaphoreType.DMA((1, 4)),
+            pltpu.SemaphoreType.DMA((FF_STEPS + 1, 2)),
+            pltpu.SemaphoreType.DMA((3,)),
         ],
         compiler_params=params(),
         cost_estimate=cost(),
         name="expand",
-    )(place, second, out_low, bias.reshape(1, FF), up, down, after)
+    )(place, tokens, out_low, gain, norm_bias, bias.reshape(1, FF), pack, *merge, up, down, after)
 
 
 DEPTHS = 4
@@ -574,14 +585,14 @@
         copy(middle_any, middle_ref, sems.at[2 * DEPTHS, 0]),
         copy(cotangent_any.at[place_ref[0]], cotangent_ref, sems.at[2 * DEPTHS, 1]),
     )
-    for n in range(2 * DEPTHS):
+    for n in range(2):
         for one in fetch(n):
             one.start()
-    for one in rest:
-        one.start()
     for n in range(2 * DEPTHS):
         which, c = divmod(n, DEPTHS)
         part = slice(c * DEPTH, (c + 1) * DEPTH)
+        for one in fetch(n + 2) if n + 2 < 2 * DEPTHS else rest if n + 2 == 2 * DEPTHS else ():
+            one.start()
         for one in fetch(n):
             one.wait()
         ref = second_ref if which else total_ref
@@ -937,7 +948,7 @@
     )
     for one in lefts:
         one.start()
-    for i in range(4):
+    for i in range(2):
         for one in fetch(i):
             one.start()
     for n, one in enumerate(lefts):
@@ -954,6 +965,8 @@
             copy(source, send_any.at[0, 0, 0], sem).wait()
 
     for i in range(4):
+        for one in fetch(i + 2) if i < 2 else ():
+            one.start()
         for one in fetch(i):
             one.wait()
         if i >= 2:
@@ -1000,7 +1013,8 @@
 
 
 ROWS = D // SPANS
-PARTS = 2 * ROWS
+PARTS = 4 * ROWS
+CROSS = ROWS
 
 
 def square_kernel(
@@ -1090,14 +1104,10 @@
         for tile in range(2):
             rows = slice(tile * HALF, (tile + 1) * HALF)
             product_ref[slot, rows] = dot(left_ref[left, rows], right_ref[right], 1, 0).astype(BF)
-        if step == 0:
-            share(slot, 0)
-        elif step == 1:
-            cross(slot, 0, 1)
-        elif step == 2:
-            cross(slot, 0, 0)
+        if step < 3:
+            share(slot, (0, 3, 2)[step])
         else:
-            cross(slot, 1, step - 3)
+            cross(slot, 0, step - 3)
     wait(0)
     wait(1)
 
@@ -1110,8 +1120,8 @@
         out_shape=(
             shape((4, PARTS, HALF), BF),
             shape((4, PARTS, HALF), BF),
-            shape((2, 4, PARTS, HALF), BF),
-            shape((2, 4, PARTS, HALF), BF),
+            shape((2, 4, CROSS, HALF), BF),
+            shape((2, 4, CROSS, HALF), BF),
         ),
         scratch_shapes=[
             pltpu.VMEM((3, D, 2 * PATCHES), BF),
@@ -1180,13 +1190,13 @@
 
 
 def third_sums(keep, came):
-    half = pl.BlockSpec((1, 4, PARTS, HALF), lambda i: (1, 0, 0, 0))
+    half = pl.BlockSpec((1, 4, CROSS, HALF), lambda i: (1, 0, 0, 0))
     return pl.pallas_call(
         third_sums_kernel,
         grid=(1,),
         in_specs=[half, half],
         out_specs=VMEM,
-        out_shape=shape((4, PARTS, HALF), BF),
+        out_shape=shape((4, CROSS, HALF), BF),
         compiler_params=params(1),
         cost_estimate=cost(),
         name="third_sums",
@@ -1202,13 +1212,13 @@
 
 
 def fourth_sums(keep, came, cross_keep, cross_came, brought, after):
-    half = pl.BlockSpec((1, 4, PARTS, HALF), lambda i: (0, 0, 0, 0))
+    half = pl.BlockSpec((1, 4, CROSS, HALF), lambda i: (0, 0, 0, 0))
     return pl.pallas_call(
         fourth_sums_kernel,
         grid=(1,),
         in_specs=[VMEM, VMEM, half, half, VMEM] + [ANYWHERE] * len(after),
         out_specs=(VMEM,) * 4,
-        out_shape=(shape((2 * PARTS, HALF), BF),) * 4,
+        out_shape=(shape((PARTS + CROSS, HALF), BF),) * 4,
         compiler_params=params(1),
         cost_estimate=cost(),
         name="fourth_sums",
@@ -1419,10 +1429,8 @@
             blocks = jnp.stack([blocks] + parts, axis=1).reshape(-1, *block.shape)
         return blocks
 
-    def total(self, block):
-        for bit in range(self.size.bit_length() - 1):
-            block = block + partner(block, "dp", 2**bit)
-        return block
+    def round(self, block, bit):
+        return block + partner(block, "dp", 2**bit)
 
 
 def on_device(
@@ -1500,9 +1508,13 @@
             jnp.sum(alive)[None],
         ]
     )
-    sums = at.total(after(sums, table_value))
+    sums = sums_y = at.round(after(sums, table_value), 1)
+    for bit in range(2, at.size.bit_length() - 1):
+        sums = at.round(sums, bit)
+    second = swap(after(jnp.where(first, quarter_of(2), quarter_of(1)), chunk_first))
+    sums = at.round(after(sums, second), 0)
     total, live_total = sums[2 * half_vars], sums[2 * half_vars + 1]
-    first_moment = after(sums, chunk_first)[:half_vars] / (total * rows * cols)
+    first_moment = sums[:half_vars] / (total * rows * cols)
     second_moment = sums[half_vars : 2 * half_vars] / (total * rows * cols)
     center_new = (1.0 - MOMENTUM) * running_stats[0] + MOMENTUM * first_moment
     spread_new = (1.0 - MOMENTUM) * running_stats[1] + MOMENTUM * (
@@ -1523,17 +1535,12 @@
     alive_own = pick(alive, pipe)[None]
     out_low = (pick(cotangent, pipe).astype(F32) * weight_hat).astype(BF)
 
-    chunk = chunk_first
-    chunks = [chunk]
-    passed = [passed_on(chunk, (sums,), ())]
-    chunk = swap(after(jnp.where(first, quarter_of(2), quarter_of(1)), chunk))
-    passed.append(passed_on(chunk, (), ()))
-    chunk = swap(after(jnp.where(first, quarter_of(0), quarter_of(2)), chunk, passed[0][0]))
-    third = chunk
-    chunk = swap(
-        after(jnp.where(first, quarter_of(1), quarter(own_merge)), chunk, passed[1][0])
-    )
-    fourth = chunk
+    passed = [passed_on(chunk_first, (sums_y,), ())]
+    passed.append(passed_on(second, (), ()))
+    third = swap(after(jnp.where(first, quarter_of(0), quarter_of(2)), second))
+    fourth = swap(
+        after(jnp.where(first, quarter_of(1), quarter(own_merge)), third, passed[0][0])
+    )
     alive_own = after(alive_own, third)
 
     tokens, heads, shares, pixels = aggregate(
@@ -1554,12 +1561,19 @@
     pack, proj, lse = attend(place, tokens, norm_gain, norm_bias, own_attend, brought)
     passed.append(passed_on(fourth, (tokens,), (lse,)))
     brought = [block for pair in passed for block in pair]
-    middle, second_low = merge(
-        place, tokens, pack, norm_gain, norm_bias, (own_merge, *brought[6:])
-    )
     pack_beside = partner(pack, "dp", 1)
-    units, hidden_sum = expand(
-        place, second_low, out_low, up_weight, hidden_bias, down_weight, heads_beside
+    units, middle, second_low, hidden_sum = expand(
+        place,
+        tokens,
+        out_low,
+        norm_gain,
+        norm_bias,
+        pack,
+        (own_merge, *brought[6:]),
+        up_weight,
+        hidden_bias,
+        down_weight,
+        heads_beside,
     )
     units_beside = partner(units, "dp", 1)
     scalars = jnp.stack([alive_own[0], weight_hat])
@@ -1679,10 +1693,9 @@
 
         whole = jnp.stack([keep, send], axis=1).reshape(SPANS, PARTS, HALF)
         cross = (cross_keep.astype(F32) + swap(cross_send).astype(F32)).astype(BF)
-        cross = cross.transpose(1, 0, 2, 3).reshape(SPANS, PARTS, HALF)
-        square = [
-            rows_of(array[:, n * ROWS : (n + 1) * ROWS]) for array in (whole, cross) for n in (0, 1)
-        ]
+        cross = cross.transpose(1, 0, 2, 3).reshape(SPANS, CROSS, HALF)
+        square = [rows_of(whole[:, n * ROWS : (n + 1) * ROWS]) for n in range(4)]
+        square.append(rows_of(cross))
         square = at.reduced(at.grouped(jnp.concatenate(square, axis=1)), groups)
         came = swap(jnp.where(first, result, tokens))
         field_halves = field_grads.reshape(2, half_vars, rows, cols)
@@ -1700,13 +1713,21 @@
     part = TAIL // at.chips
     query_part = square[:lot]
     tail = square[lot : lot + part]
-    merge_sum = square[lot + part : 2 * lot + part]
-    cross = square[2 * lot + part :]
+    merge_one = square[lot + part : 2 * lot + part]
+    merge_two = square[2 * lot + part : 3 * lot + part]
+    cross = square[3 * lot + part :]
     tail_came = swap(tail.astype(BF)).astype(F32)
-    sent = jnp.concatenate([query_part, cross], axis=0).astype(BF)
+    sent = jnp.concatenate(
+        [jnp.where(first, merge_two, merge_one), query_part, cross], axis=0
+    ).astype(BF)
     section_came = swap(sent).astype(F32)
     section_sum = jnp.stack(
-        [merge_sum, query_part + section_came[:lot], section_came[lot:], cross]
+        [
+            jnp.where(first, merge_one, merge_two) + section_came[:lot],
+            query_part + section_came[lot : 2 * lot],
+            section_came[2 * lot :],
+            cross,
+        ]
     )
     tail = (tail.astype(BF).astype(F32) + tail_came).astype(BF)
     section_sum = section_sum.reshape(4, 2, d_width, HALF).transpose(1, 0, 2, 3)

time: 457 us -> 435 us (0.952)
  Pallas kernels: 183 us -> 172 us
  waiting for transfers between devices: 156 us -> 147 us
  starting transfers between devices: 57.3 us -> 52.3 us
    ppermute x47, waiting for transfers between devices: 156 us -> 146 us  [partner(): return lax.ppermute(block, axis, [(i, i ^ distance) for i in range(size)])]
    pallas_call x1 -> x0, Pallas kernels: 8.46 us -> none  [merge(): pl.pallas_call(merge_kernel, grid=(1,), out_shape=(shape((PATCHES, D), F3...]
    ppermute x47, starting transfers between devices: 52.4 us -> 46.9 us  [partner(): return lax.ppermute(block, axis, [(i, i ^ distance) for i in range(size)])]
  transfers between devices with their start and end apart: 49 -> 49, of which waited for: 19 -> 20; matrix products, arithmetic and copies ran while one was open for 7% -> 8% of each run, Pallas kernels for 30% -> 29%
where the time goes in v2:
time: 435 us; the launch traced here: 431 us
  Pallas kernels  172 us (40%)
  waiting for transfers between devices  147 us (34%)
  starting transfers between devices  52.3 us (12%)
  other arithmetic  34.6 us (8%)
  local copies, waits for them, and re-layouts  20.5 us (5%)
  between operations  4.9 us (1%)
    ppermute x47, waiting for transfers between devices, partner(): return lax.ppermute(block, axis, [(i, i ^ distance) for i in range(size)])  146 us
    ppermute x47, starting transfers between devices, partner(): return lax.ppermute(block, axis, [(i, i ^ distance) for i in range(size)])  46.9 us
    pallas_call x1, Pallas kernels, attend_back(): pl.pallas_call(attend_back_kernel, out_shape=(shape((4, PATCHES, HALF), B...  28.5 us
    pallas_call x1, Pallas kernels, expand(): pl.pallas_call(expand_kernel, out_shape=(shape((2, PATCHES, UNITS), BF),...  21.1 us
    pallas_call x1, Pallas kernels, attend(): pl.pallas_call(attend_kernel, out_shape=(shape((2 * D, PATCHES), BF), sha...  19.9 us
    pallas_call x2, Pallas kernels, wide_grads(): pl.pallas_call(functools.partial(wide_kernel, which, by_pipe), in_specs=[...  17.6 us
    pallas_call x1, Pallas kernels, contract(): pl.pallas_call(contract_kernel, out_shape=(shape((PATCHES, D), BF), shape...  16.4 us
    pallas_call x1, Pallas kernels, aggregate_back(): pl.pallas_call(aggregate_back_kernel, out_shape=(shape((TAIL, HALF), BF),...  16 us
  transfers between devices with their start and end apart: 49, of which 20 were waited for; matrix products, arithmetic and copies ran while one was open for 8% of the time, Pallas kernels for 29%

profile of v2, /device:TPU:0, one launch (start us, length us, event | category | flops | bytes accessed | tf_op | source)
XLA Modules:
  0.0 431.0 jit_solution(12688398672427380073)
XLA Ops:
  0.7 3.0 bitcast_select_fusion.2
  3.7 2.9 collective-permute-start.3
  9.7 5.7 %tables.1 = (f32[16,1024]{1,0:T(8,128)}, f32[240,16]{1,0:T(8,128)}, f32[1024,256]{1,0:T(8,128)}) custom-call(f32[1,1024]{1,0:T(1,128)} %bitcast.151, bf16[240,1024]{1,0:T(8,128)(2,1)} %pad_maximum_fusion.9.table_ref, bf16[3,1024,1024]{2,1,0:T(8,128)(2,1)} %bitcast.123), custom_call_target="tpu_custom_call" | custom-call | flops 1000 | bytes 1000 | tf_op jit(solution)/shard_map/tables/pallas_call | solution.py:145
  18.5 3.1 collective-permute-start.9
  30.2 2.6 collective-permute-start.2
  38.5 10.3 %collective-permute-done.4 = bf16[256,1024]{1,0:T(8,128)(2,1)} collective-permute-done((bf16[256,1024]{1,0:T(8,128)(2,1)S(1)}, bf16[256,1024]{1,0:T(8,128)(2,1)}, u32[]{:S(2)}, u32[]{:S(2)}) %collective-permute-start.4) | collective-permute-done | bytes 524320 | tf_op jit(solution)/shard_map/ppermute | solution.py:1353
  48.8 2.6 collective-permute-start.6
  55.1 9.0 %collective-permute-done.6 = bf16[256,1024]{1,0:T(8,128)(2,1)} collective-permute-done((bf16[256,1024]{1,0:T(8,128)(2,1)S(1)}, bf16[256,1024]{1,0:T(8,128)(2,1)}, u32[]{:S(2)}, u32[]{:S(2)}) %collective-permute-start.6) | collective-permute-done | bytes 524320 | tf_op jit(solution)/shard_map/ppermute | solution.py:1353
  70.2 11.9 %aggregate.1 = (bf16[512,1024]{1,0:T(8,128)(2,1)}, bf16[1024,512]{1,0:T(8,128)(2,1)}, f32[16,48,512]{2,1,0:T(8,128)}, f32[4,48,512]{2,1,0:T(8,128)}) custom-call(s32[3]{0:T(128)} %pad_add_fusion.place_ref, f32[1]{0:T(128)} %dynamic_slice.61.alive_ref, f32[384,128]{1,0:T(8,128)} %get-tuple-element.218.own_field_ref, f32[384,128]{1,0:T(8,128)} %copy-done.33, ...), custom_call_target="tpu_custom_call" | custom-call | flops 1000 | bytes 1000 | tf_op jit(solution)/shard_map/aggregate/pallas_call | solution.py:272
  87.4 19.9 %attend.1 = (bf16[2048,512]{1,0:T(8,128)(2,1)}, bf16[3,512,1024]{2,1,0:T(8,128)(2,1)}, f32[8,2,512]{2,1,0:T(2,128)}) custom-call(s32[3]{0:T(128)} %pad_add_fusion.place_ref, bf16[512,1024]{1,0:T(8,128)(2,1)} %get-tuple-element.92.tokens_ref, f32[2,1024]{1,0:T(2,128)} %gain_ref.5, f32[2,1024]{1,0:T(2,128)} %norm_bias_ref.1, bf16[3,1024,1024]{2,1,0:T(8,128)(2,1)} %bitcast.124, ...), custom_call_target="tpu_custom_call" | custom-call | flops 1000 | bytes 1000 | tf_op jit(solution)/shard_map/attend/pallas_call | solution.py:346
  114.1 21.1 %expand.1 = (bf16[2,512,4608]{2,1,0:T(8,128)(2,1)}, f32[512,1024]{1,0:T(8,128)}, bf16[512,1024]{1,0:T(8,128)(2,1)}, f32[1,4096]{1,0:T(1,128)}) custom-call(s32[3]{0:T(128)} %pad_add_fusion.place_ref, bf16[512,1024]{1,0:T(8,128)(2,1)} %get-tuple-element.92.tokens_ref, bf16[512,1024]{1,0:T(8,128)(2,1)} %fusion.out_ref.left_any, f32[2,1024]{1,0:T(2,128)} %gain_ref.5, ...), custom_call_target="tpu_custom_call" | custom-call | flops 1000 | bytes 1000 | tf_op jit(solution)/shard_map/expand/pallas_call | solution.py:515
  137.8 16.4 %contract.1 = (bf16[512,1024]{1,0:T(8,128)(2,1)}, f32[512,1024]{1,0:T(8,128)}, bf16[512,1024]{1,0:T(8,128)(2,1)}, f32[1,1024]{1,0:T(1,128)}, f32[1,1024]{1,0:T(1,128)}, /*index=5*/f32[1,1024]{1,0:T(1,128)}) custom-call(s32[3]{0:T(128)} %pad_add_fusion.place_ref, f32[2]{0:T(128)} %pad_maximum_fusion.15.scalars_ref, f32[1,1024]{1,0:T(1,128)} %slice.72.gain_ref, ...), custom_call_target="tpu_custom_call" | custom-call | flops 1000 | bytes 1000 | tf_op jit(solution)/shard_map/contract/pallas_call | solution.py:631
  154.2 8.7 %down_grads.1 = (bf16[2,2,2,512,256]{4,3,2,1,0:T(8,128)(2,1)}, bf16[2,2,2,512,256]{4,3,2,1,0:T(8,128)(2,1)}) custom-call(s32[2]{0:T(128)} %pad_add_fusion.1.place_ref, bf16[512,1024]{1,0:T(8,128)(2,1)} %fusion.out_ref.left_any, bf16[2,512,4608]{2,1,0:T(8,128)(2,1)} %get-tuple-element.100.units_any.own_any, ...), custom_call_target="tpu_custom_call" | custom-call | flops 1000 | bytes 1000 | tf_op jit(solution)/shard_map/down_grads/pallas_call | solution.py:996
  164.2 8.9 %up_grads.1 = (bf16[2,2,2,512,256]{4,3,2,1,0:T(8,128)(2,1)}, bf16[2,2,2,512,256]{4,3,2,1,0:T(8,128)(2,1)}) custom-call(s32[2]{0:T(128)} %pad_add_fusion.1.place_ref, bf16[512,1024]{1,0:T(8,128)(2,1)} %get-tuple-element.106.left_any, bf16[2,512,4608]{2,1,0:T(8,128)(2,1)} %get-tuple-element.100.units_any.own_any, ...), custom_call_target="tpu_custom_call" | custom-call | flops 1000 | bytes 1000 | tf_op jit(solution)/shard_map/up_grads/pallas_call | solution.py:996
  173.9 28.5 %attend_back.1 = (bf16[4,512,512]{2,1,0:T(8,128)(2,1)}, bf16[4,512,512]{2,1,0:T(8,128)(2,1)}, bf16[512,1024]{1,0:T(8,128)(2,1)}, f32[1,1024]{1,0:T(1,128)}, f32[1,1024]{1,0:T(1,128)}) custom-call(s32[3]{0:T(128)} %pad_add_fusion.place_ref, f32[512,1024]{1,0:T(8,128)} %get-tuple-element.102.grad_ref, bf16[512,1024]{1,0:T(8,128)(2,1)} %get-tuple-element.103.refs_0_.branch_ref, ...), custom_call_target="tpu_custom_call" | custom-call | flops 1000 | bytes 1000 | tf_op jit(solution)/shard_map/attend_back/pallas_call | solution.py:761
  202.9 16.0 %aggregate_back.1 = (bf16[1024,512]{1,0:T(8,128)(2,1)}, bf16[1024,512]{1,0:T(8,128)(2,1)}, f32[768,128]{1,0:T(8,128)}) custom-call(s32[3]{0:T(128)} %pad_add_fusion.place_ref, f32[1]{0:T(128)} %dynamic_slice.61.alive_ref, bf16[512,1024]{1,0:T(8,128)(2,1)} %get-tuple-element.108.token_grad_ref, f32[4,48,512]{2,1,0:T(8,128)} %get-tuple-element.109.pixels_ref, ...), custom_call_target="tpu_custom_call" | custom-call | flops 1000 | bytes 1000 | tf_op jit(solution)/shard_map/aggregate_back/pallas_call | solution.py:899
  222.1 3.9 first_sums.1
  229.8 11.3 %square_grads.1 = (bf16[4,512,512]{2,1,0:T(8,128)(2,1)}, bf16[4,512,512]{2,1,0:T(8,128)(2,1)}, bf16[2,4,128,512]{3,2,1,0:T(8,128)(2,1)}, bf16[2,4,128,512]{3,2,1,0:T(8,128)(2,1)}) custom-call(s32[2]{0:T(128)} %pad_add_fusion.2.place_ref, bf16[1024,512]{1,0:T(8,128)(2,1)} %get-tuple-element.119.after_any.tail_own, bf16[1024,512]{1,0:T(8,128)(2,1)} %copy-done.25, ...), custom_call_target="tpu_custom_call" | custom-call | flops 1000 | bytes 1000 | tf_op jit(solution)/shard_map/square_grads/pallas_call | solution.py:1116
  241.1 9.6 %collective-permute-done.27.down_brought = bf16[4,512,256]{2,1,0:T(8,128)(2,1)S(1)} collective-permute-done((bf16[4,512,256]{2,1,0:T(8,128)(2,1)}, bf16[4,512,256]{2,1,0:T(8,128)(2,1)S(1)}, u32[]{:S(2)}, u32[]{:S(2)}) %collective-permute-start.27) | collective-permute-done | bytes 1048608 | tf_op jit(solution)/shard_map/ppermute | solution.py:1353
  252.7 4.7 %second_sums.1 = (bf16[2,512,256]{2,1,0:T(8,128)(2,1)}, bf16[2,512,256]{2,1,0:T(8,128)(2,1)}, bf16[2,512,256]{2,1,0:T(8,128)(2,1)}, bf16[2,512,256]{2,1,0:T(8,128)(2,1)}) custom-call(bf16[2,2,2,512,256]{4,3,2,1,0:T(8,128)(2,1)} %get-tuple-element.105.refs_0_.refs_8_.down_keep, bf16[2,2,2,512,256]{4,3,2,1,0:T(8,128)(2,1)} %copy-done.11, ...), custom_call_target="tpu_custom_call" | custom-call | flops 1000 | bytes 1000 | tf_op jit(solution)/shard_map/second_sums/pallas_call | solution.py:1175
  259.6 3.6 collective-permute-start.36
  263.2 18.0 %collective-permute-done.29.came.cross_came = bf16[2,4,128,512]{3,2,1,0:T(8,128)(2,1)S(1)} collective-permute-done((bf16[2,4,128,512]{3,2,1,0:T(8,128)(2,1)S(1)}, bf16[2,4,128,512]{3,2,1,0:T(8,128)(2,1)S(1)}, u32[]{:S(2)}, u32[]{:S(2)}) %collective-permute-start.29) | collective-permute-done | bytes 1048608 | tf_op jit(solution)/shard_map/ppermute | solution.py:1353
  285.5 2.6 collective-permute-start.35
  291.7 17.5 %collective-permute-done.35 = bf16[2,512,256]{2,1,0:T(8,128)(2,1)S(1)} collective-permute-done((bf16[2,512,256]{2,1,0:T(8,128)(2,1)S(1)}, bf16[2,512,256]{2,1,0:T(8,128)(2,1)S(1)}, u32[]{:S(2)}, u32[]{:S(2)}) %collective-permute-start.35) | collective-permute-done | bytes 524320 | tf_op jit(solution)/shard_map/ppermute | solution.py:1353
  317.6 4.4 %fourth_sums.1 = (bf16[640,512]{1,0:T(8,128)(2,1)}, bf16[640,512]{1,0:T(8,128)(2,1)}, bf16[640,512]{1,0:T(8,128)(2,1)}, bf16[640,512]{1,0:T(8,128)(2,1)}) custom-call(bf16[4,512,512]{2,1,0:T(8,128)(2,1)} %get-tuple-element.137.keep, bf16[4,512,512]{2,1,0:T(8,128)(2,1)} %copy-done.21, bf16[2,4,128,512]{3,2,1,0:T(8,128)(2,1)} %get-tuple-element.127.keep.cross_keep, ...), custom_call_target="tpu_custom_call" | custom-call | flops 1000 | bytes 1000 | tf_op jit(solution)/shard_map/fourth_sums/pallas_call | solution.py:1216
  322.0 3.6 collective-permute-start.39
  328.6 13.3 %collective-permute-done.39 = bf16[640,512]{1,0:T(8,128)(2,1)} collective-permute-done((bf16[640,512]{1,0:T(8,128)(2,1)}, bf16[640,512]{1,0:T(8,128)(2,1)}, u32[]{:S(2)}, u32[]{:S(2)}) %collective-permute-start.39) | collective-permute-done | bytes 655392 | tf_op jit(solution)/shard_map/ppermute | solution.py:1353
  341.9 37.9 %collective-permute-done.38 = bf16[640,512]{1,0:T(8,128)(2,1)} collective-permute-done((bf16[640,512]{1,0:T(8,128)(2,1)}, bf16[640,512]{1,0:T(8,128)(2,1)}, u32[]{:S(2)}, u32[]{:S(2)}) %collective-permute-start.38) | collective-permute-done | bytes 655392 | tf_op jit(solution)/shard_map/ppermute | solution.py:1353
  382.6 4.1 collective-permute-done.40
  395.7 4.1 collective-permute-done.42
  403.1 10.2 %collective-permute-done.44 = bf16[4,128,512]{2,1,0:T(8,128)(2,1)S(1)} collective-permute-done((bf16[4,128,512]{2,1,0:T(8,128)(2,1)S(1)}, bf16[4,128,512]{2,1,0:T(8,128)(2,1)S(1)}, u32[]{:S(2)}, u32[]{:S(2)}) %collective-permute-start.44) | collective-permute-done | bytes 524320 | tf_op jit(solution)/shard_map/ppermute | solution.py:1353
  419.7 8.3 %finish.1 = (f32[512,1024]{1,0:T(8,128)}, f32[2,1024]{1,0:T(2,128)}, f32[2,1024]{1,0:T(2,128)}, f32[1,1024]{1,0:T(1,128)}, f32[4,1024]{1,0:T(4,128)}, /*index=5*...) custom-call(s32[5]{0:T(128)} %stack.173.place_ref, ...), custom_call_target="tpu_custom_call" | custom-call | flops 1000 | bytes 1000 | tf_op jit(solution)/shard_map/finish/pallas_call | solution.py:1322
  (245 shorter events, 98.4 us)
Async XLA Ops:
  3.7 29.1 %collective-permute-start.3 = (bf16[256,1024]{1,0:T(8,128)(2,1)}, bf16[256,1024]{1,0:T(8,128)(2,1)}, u32[]{:S(2)}, u32[]{:S(2)}) collective-permute-start(bf16[256,1024]{1,0:T(8,128)(2,1)} %get-tuple-element.193), channel_id=1, source_target_pairs={{0,16},{16,0},{1,17},{17,1},{2,18},{18,2},{3,19},{19,3},{4,20},{20... | collective-permute-start | bytes 1572872 | tf_op jit(solution)/shard_map/ppermute | solution.py:1353
  18.5 18.0 %collective-permute-start.9 = (f32[240,16]{1,0:T(8,128)}, f32[240,16]{1,0:T(8,128)}, u32[]{:S(2)}, u32[]{:S(2)}) collective-permute-start(f32[240,16]{1,0:T(8,128)} %get-tuple-element.90), channel_id=1, source_target_pairs={{0,16},{1,17},{2,18},{3,19},{4,20},{5,21},{6,22},{7,23},{8,24},{9,... | collective-permute-start | bytes 46088 | tf_op jit(solution)/shard_map/ppermute | solution.py:1490
  23.7 14.0 %collective-permute-start.10 = (bf16[1024,256]{1,0:T(8,128)(2,1)}, bf16[1024,256]{1,0:T(8,128)(2,1)}, u32[]{:S(2)}, u32[]{:S(2)}) collective-permute-start(bf16[1024,256]{1,0:T(8,128)(2,1)} %convert_element_type.90), channel_id=1, source_target_pairs={{0,16},{1,17},{2,18},{3,19},{4,20},{5,21},{6,22},{7,23},{8,24},{9,... | collective-permute-start | bytes 1572872 | tf_op jit(solution)/shard_map/ppermute | solution.py:1490
  32.8 16.0 %collective-permute-start.4 = (bf16[256,1024]{1,0:T(8,128)(2,1)S(1)}, bf16[256,1024]{1,0:T(8,128)(2,1)}, u32[]{:S(2)}, u32[]{:S(2)}) collective-permute-start(bf16[256,1024]{1,0:T(8,128)(2,1)S(1)} %get-tuple-element.86), channel_id=1, source_target_pairs={{0,16},{16,0},{1,17},{17,1},{2,18},{18,2},{3,19},{19,3},{4,20},{20... | collective-permute-start | bytes 1572872 | tf_op jit(solution)/shard_map/ppermute | solution.py:1353
  32.8 18.6 %collective-permute-start.11 = (bf16[256,1024]{1,0:T(8,128)(2,1)}, bf16[256,1024]{1,0:T(8,128)(2,1)S(1)}, u32[]{:S(2)}, u32[]{:S(2)}) collective-permute-start(bf16[256,1024]{1,0:T(8,128)(2,1)} %collective-permute-done.3), channel_id=1, source_target_pairs={{0,2},{1,3},{2,0},{3,1},{4,6},{5,7},{6,4},{7,5},{8,10},{9,11},{10,... | collective-permute-start | bytes 1572872 | tf_op jit(solution)/shard_map/ppermute | solution.py:1353
  34.7 34.3 %collective-permute-start.7 = (f32[384,128]{1,0:T(8,128)S(1)}, f32[384,128]{1,0:T(8,128)S(1)}, u32[]{:S(2)}, u32[]{:S(2)}) collective-permute-start(f32[384,128]{1,0:T(8,128)S(1)} %get-tuple-element.217), channel_id=1, source_target_pairs={{0,16},{16,0},{1,17},{17,1},{2,18},{18,2},{3,19},{19,3},{4,20},{20... | collective-permute-start | bytes 589832 | tf_op jit(solution)/shard_map/ppermute | solution.py:1353
  48.8 15.3 %collective-permute-start.6 = (bf16[256,1024]{1,0:T(8,128)(2,1)S(1)}, bf16[256,1024]{1,0:T(8,128)(2,1)}, u32[]{:S(2)}, u32[]{:S(2)}) collective-permute-start(bf16[256,1024]{1,0:T(8,128)(2,1)S(1)} %get-tuple-element.88), channel_id=1, source_target_pairs={{0,16},{16,0},{1,17},{17,1},{2,18},{18,2},{3,19},{19,3},{4,20},{20... | collective-permute-start | bytes 1572872 | tf_op jit(solution)/shard_map/ppermute | solution.py:1353
  52.5 16.5 %collective-permute-start.12 = (bf16[2,256,1024]{2,1,0:T(8,128)(2,1)S(1)}, bf16[2,256,1024]{2,1,0:T(8,128)(2,1)S(1)}, u32[]{:S(2)}, u32[]{:S(2)}) collective-permute-start(bf16[2,256,1024]{2,1,0:T(8,128)(2,1)S(1)} %pad_maximum_fusion.1.brought_ref.refs_0_), channel_id=1, source_target_pairs={{0,1},{1,0},{2,3},{3,2},{4,5},{5,4},{6,7},{7,6},{8,9},{9,8},{10,11... | collective-permute-start | bytes 3145736 | tf_op jit(solution)/shard_map/ppermute | solution.py:1353
  52.8 14.7 %collective-permute-start.13 = (bf16[256,1024]{1,0:T(8,128)(2,1)}, bf16[256,1024]{1,0:T(8,128)(2,1)}, u32[]{:S(2)}, u32[]{:S(2)}) collective-permute-start(bf16[256,1024]{1,0:T(8,128)(2,1)} %collective-permute-done.4), channel_id=1, source_target_pairs={{0,2},{1,3},{2,0},{3,1},{4,6},{5,7},{6,4},{7,5},{8,10},{9,11},{10,... | collective-permute-start | bytes 1572872 | tf_op jit(solution)/shard_map/ppermute | solution.py:1353
  64.1 18.1 %collective-permute-start.15 = (bf16[256,1024]{1,0:T(8,128)(2,1)}, bf16[256,1024]{1,0:T(8,128)(2,1)S(1)}, u32[]{:S(2)}, u32[]{:S(2)}) collective-permute-start(bf16[256,1024]{1,0:T(8,128)(2,1)} %collective-permute-done.6), channel_id=1, source_target_pairs={{0,2},{1,3},{2,0},{3,1},{4,6},{5,7},{6,4},{7,5},{8,10},{9,11},{10,... | collective-permute-start | bytes 1572872 | tf_op jit(solution)/shard_map/ppermute | solution.py:1353
  68.8 16.5 %collective-permute-start.14 = (bf16[2,256,1024]{2,1,0:T(8,128)(2,1)S(1)}, bf16[2,256,1024]{2,1,0:T(8,128)(2,1)S(1)}, u32[]{:S(2)}, u32[]{:S(2)}) collective-permute-start(bf16[2,256,1024]{2,1,0:T(8,128)(2,1)S(1)} %pad_maximum_fusion.2.refs_2_.refs_4_), channel_id=1, source_target_pairs={{0,1},{1,0},{2,3},{3,2},{4,5},{5,4},{6,7},{7,6},{8,9},{9,8},{10,11... | collective-permute-start | bytes 3145736 | tf_op jit(solution)/shard_map/ppermute | solution.py:1353
  68.9 14.8 %collective-permute-start.17 = (bf16[256,1024]{1,0:T(8,128)(2,1)S(1)}, bf16[256,1024]{1,0:T(8,128)(2,1)}, u32[]{:S(2)}, u32[]{:S(2)}) collective-permute-start(bf16[256,1024]{1,0:T(8,128)(2,1)S(1)} %get-tuple-element.95), channel_id=1, source_target_pairs={{0,16},{16,0},{1,17},{17,1},{2,18},{18,2},{3,19},{19,3},{4,20},{20... | collective-permute-start | bytes 1572872 | tf_op jit(solution)/shard_map/ppermute | solution.py:1353
  83.7 23.5 %collective-permute-start.18 = (bf16[256,1024]{1,0:T(8,128)(2,1)}, bf16[256,1024]{1,0:T(8,128)(2,1)S(1)}, u32[]{:S(2)}, u32[]{:S(2)}) collective-permute-start(bf16[256,1024]{1,0:T(8,128)(2,1)} %collective-permute-done.17), channel_id=1, source_target_pairs={{0,2},{1,3},{2,0},{3,1},{4,6},{5,7},{6,4},{7,5},{8,10},{9,11},{10,... | collective-permute-start | bytes 1572872 | tf_op jit(solution)/shard_map/ppermute | solution.py:1353
  85.3 27.6 %collective-permute-start.20 = (bf16[1024,512]{1,0:T(8,128)(2,1)S(1)}, bf16[1024,512]{1,0:T(8,128)(2,1)S(1)}, u32[]{:S(2)}, u32[]{:S(2)}) collective-permute-start(bf16[1024,512]{1,0:T(8,128)(2,1)S(1)} %copy-done.23), channel_id=1, source_target_pairs={{0,1},{1,0},{2,3},{3,2},{4,5},{5,4},{6,7},{7,6},{8,9},{9,8},{10,11... | collective-permute-start | bytes 3145736 | tf_op jit(solution)/shard_map/ppermute | solution.py:1353
  135.2 19.0 %collective-permute-start.21 = (bf16[2,512,4608]{2,1,0:T(8,128)(2,1)}, bf16[2,512,4608]{2,1,0:T(8,128)(2,1)}, u32[]{:S(2)}, u32[]{:S(2)}) collective-permute-start(bf16[2,512,4608]{2,1,0:T(8,128)(2,1)} %get-tuple-element.100.units_any.own_any), channel_id=1, source_target_pairs={{0,1},{1,0},{2,3},{3,2},{4,5},{5,4},{6,7},{7,6},{8,9},{9,8},{10,11... | collective-permute-start | bytes 28311560 | tf_op jit(solution)/shard_map/ppermute | solution.py:1353
  162.9 56.1 %collective-permute-start.25 = (bf16[2,2,2,512,256]{4,3,2,1,0:T(8,128)(2,1)}, bf16[2,2,2,512,256]{4,3,2,1,0:T(8,128)(2,1)S(1)}, u32[]{:S(2)}, u32[]{:S(2)}) collective-permute-start(bf16[2,2,2,512,256]{4,3,2,1,0:T(8,128)(2,1)} %get-tuple-element.123), channel_id=1, source_target_pairs={{0,16},{16,0},{1,17},{17,1},{2,18},{18,2},{3,19},{19,3},{4,20},{20... | collective-permute-start | bytes 6291464 | tf_op jit(solution)/shard_map/ppermute | solution.py:1353
  173.1 47.7 %collective-permute-start.26 = (bf16[2,2,2,512,256]{4,3,2,1,0:T(8,128)(2,1)}, bf16[2,2,2,512,256]{4,3,2,1,0:T(8,128)(2,1)S(1)}, u32[]{:S(2)}, u32[]{:S(2)}) collective-permute-start(bf16[2,2,2,512,256]{4,3,2,1,0:T(8,128)(2,1)} %get-tuple-element.124), channel_id=1, source_target_pairs={{0,2},{1,3},{2,0},{3,1},{4,6},{5,7},{6,4},{7,5},{8,10},{9,11},{10,... | collective-permute-start | bytes 6291464 | tf_op jit(solution)/shard_map/ppermute | solution.py:1353
  173.9 54.9 %collective-permute-start.23 = (bf16[2048,512]{1,0:T(8,128)(2,1)S(1)}, bf16[2048,512]{1,0:T(8,128)(2,1)}, u32[]{:S(2)}, u32[]{:S(2)}) collective-permute-start(bf16[2048,512]{1,0:T(8,128)(2,1)S(1)} %copy-done.10), channel_id=1, source_target_pairs={{0,1},{1,0},{2,3},{3,2},{4,5},{5,4},{6,7},{7,6},{8,9},{9,8},{10,11... | collective-permute-start | bytes 6291464 | tf_op jit(solution)/shard_map/ppermute | solution.py:1353
  202.3 26.4 %collective-permute-start.24 = (bf16[4,512,512]{2,1,0:T(8,128)(2,1)}, bf16[4,512,512]{2,1,0:T(8,128)(2,1)}, u32[]{:S(2)}, u32[]{:S(2)}) collective-permute-start(bf16[4,512,512]{2,1,0:T(8,128)(2,1)} %get-tuple-element.122), channel_id=1, source_target_pairs={{0,1},{1,0},{2,3},{3,2},{4,5},{5,4},{6,7},{7,6},{8,9},{9,8},{10,11... | collective-permute-start | bytes 6291464 | tf_op jit(solution)/shard_map/ppermute | solution.py:1353
  226.0 24.7 %collective-permute-start.27 = (bf16[4,512,256]{2,1,0:T(8,128)(2,1)}, bf16[4,512,256]{2,1,0:T(8,128)(2,1)S(1)}, u32[]{:S(2)}, u32[]{:S(2)}) collective-permute-start(bf16[4,512,256]{2,1,0:T(8,128)(2,1)} %get-tuple-element.125.refs_0_), channel_id=1, source_target_pairs={{0,2},{1,3},{2,0},{3,1},{4,6},{5,7},{6,4},{7,5},{8,10},{9,11},{10,... | collective-permute-start | bytes 3145736 | tf_op jit(solution)/shard_map/ppermute | solution.py:1353
  226.9 24.9 %collective-permute-start.28 = (bf16[4,512,256]{2,1,0:T(8,128)(2,1)}, bf16[4,512,256]{2,1,0:T(8,128)(2,1)S(1)}, u32[]{:S(2)}, u32[]{:S(2)}) collective-permute-start(bf16[4,512,256]{2,1,0:T(8,128)(2,1)} %get-tuple-element.126.refs_1_), channel_id=1, source_target_pairs={{0,16},{16,0},{1,17},{17,1},{2,18},{18,2},{3,19},{19,3},{4,20},{20... | collective-permute-start | bytes 3145736 | tf_op jit(solution)/shard_map/ppermute | solution.py:1353
  257.4 23.8 %collective-permute-start.29 = (bf16[2,4,128,512]{3,2,1,0:T(8,128)(2,1)S(1)}, bf16[2,4,128,512]{3,2,1,0:T(8,128)(2,1)S(1)}, u32[]{:S(2)}, u32[]{:S(2)}) collective-permute-start(bf16[2,4,128,512]{3,2,1,0:T(8,128)(2,1)S(1)} %copy-done.43), channel_id=1, source_target_pairs={{0,16},{16,0},{1,17},{17,1},{2,18},{18,2},{3,19},{19,3},{4,20},{20... | collective-permute-start | bytes 3145736 | tf_op jit(solution)/shard_map/ppermute | solution.py:1353
  258.3 57.5 %collective-permute-start.32 = (bf16[4,512,512]{2,1,0:T(8,128)(2,1)}, bf16[4,512,512]{2,1,0:T(8,128)(2,1)S(1)}, u32[]{:S(2)}, u32[]{:S(2)}) collective-permute-start(bf16[4,512,512]{2,1,0:T(8,128)(2,1)} %get-tuple-element.138.after_any), channel_id=1, source_target_pairs={{0,2},{1,3},{2,0},{3,1},{4,6},{5,7},{6,4},{7,5},{8,10},{9,11},{10,... | collective-permute-start | bytes 6291464 | tf_op jit(solution)/shard_map/ppermute | solution.py:1353
  259.6 30.1 %collective-permute-start.36 = (bf16[2,512,256]{2,1,0:T(8,128)(2,1)}, bf16[2,512,256]{2,1,0:T(8,128)(2,1)S(1)}, u32[]{:S(2)}, u32[]{:S(2)}) collective-permute-start(bf16[2,512,256]{2,1,0:T(8,128)(2,1)} %get-tuple-element.133), channel_id=1, source_target_pairs={{0,12},{1,13},{2,14},{3,15},{4,8},{5,9},{6,10},{7,11},{8,4},{9,5},... | collective-permute-start | bytes 1572872 | tf_op jit(solution)/shard_map/ppermute | solution.py:1353
  284.5 31.3 %collective-permute-start.30 = (bf16[512,1024]{1,0:T(8,128)(2,1)S(1)}, bf16[512,1024]{1,0:T(8,128)(2,1)S(1)}, u32[]{:S(2)}, u32[]{:S(2)}) collective-permute-start(bf16[512,1024]{1,0:T(8,128)(2,1)S(1)} %broadcast_select_fusion), channel_id=1, source_target_pairs={{0,16},{16,0},{1,17},{17,1},{2,18},{18,2},{3,19},{19,3},{4,20},{20... | collective-permute-start | bytes 3145736 | tf_op jit(solution)/shard_map/ppermute | solution.py:1353
  285.5 23.7 %collective-permute-start.35 = (bf16[2,512,256]{2,1,0:T(8,128)(2,1)S(1)}, bf16[2,512,256]{2,1,0:T(8,128)(2,1)S(1)}, u32[]{:S(2)}, u32[]{:S(2)}) collective-permute-start(bf16[2,512,256]{2,1,0:T(8,128)(2,1)S(1)} %copy-done.45), channel_id=1, source_target_pairs={{0,8},{1,9},{2,10},{3,11},{4,12},{5,13},{6,14},{7,15},{8,0},{9,1},... | collective-permute-start | bytes 1572872 | tf_op jit(solution)/shard_map/ppermute | solution.py:1353
  288.1 22.2 %collective-permute-start.34 = (bf16[2,512,256]{2,1,0:T(8,128)(2,1)S(1)}, bf16[2,512,256]{2,1,0:T(8,128)(2,1)S(1)}, u32[]{:S(2)}, u32[]{:S(2)}) collective-permute-start(bf16[2,512,256]{2,1,0:T(8,128)(2,1)S(1)} %copy-done.44), channel_id=1, source_target_pairs={{0,4},{1,5},{2,6},{3,7},{4,0},{5,1},{6,2},{7,3},{8,12},{9,13},{10,... | collective-permute-start | bytes 1572872 | tf_op jit(solution)/shard_map/ppermute | solution.py:1353
  289.7 26.1 %collective-permute-start.33 = (bf16[4,128,512]{2,1,0:T(8,128)(2,1)S(1)}, bf16[4,128,512]{2,1,0:T(8,128)(2,1)S(1)}, u32[]{:S(2)}, u32[]{:S(2)}) collective-permute-start(bf16[4,128,512]{2,1,0:T(8,128)(2,1)S(1)} %copy-done.28), channel_id=1, source_target_pairs={{0,2},{1,3},{2,0},{3,1},{4,6},{5,7},{6,4},{7,5},{8,10},{9,11},{10,... | collective-permute-start | bytes 1572872 | tf_op jit(solution)/shard_map/ppermute | solution.py:1353
  322.0 19.9 %collective-permute-start.39 = (bf16[640,512]{1,0:T(8,128)(2,1)}, bf16[640,512]{1,0:T(8,128)(2,1)}, u32[]{:S(2)}, u32[]{:S(2)}) collective-permute-start(bf16[640,512]{1,0:T(8,128)(2,1)} %get-tuple-element.142), channel_id=1, source_target_pairs={{0,12},{1,13},{2,14},{3,15},{4,8},{5,9},{6,10},{7,11},{8,4},{9,5},... | collective-permute-start | bytes 1966088 | tf_op jit(solution)/shard_map/ppermute | solution.py:1353
  325.7 54.2 %collective-permute-start.38 = (bf16[640,512]{1,0:T(8,128)(2,1)}, bf16[640,512]{1,0:T(8,128)(2,1)}, u32[]{:S(2)}, u32[]{:S(2)}) collective-permute-start(bf16[640,512]{1,0:T(8,128)(2,1)} %get-tuple-element.141), channel_id=1, source_target_pairs={{0,8},{1,9},{2,10},{3,11},{4,12},{5,13},{6,14},{7,15},{8,0},{9,1},... | collective-permute-start | bytes 1966088 | tf_op jit(solution)/shard_map/ppermute | solution.py:1353
  325.7 54.2 %collective-permute-start.37 = (bf16[640,512]{1,0:T(8,128)(2,1)}, bf16[640,512]{1,0:T(8,128)(2,1)}, u32[]{:S(2)}, u32[]{:S(2)}) collective-permute-start(bf16[640,512]{1,0:T(8,128)(2,1)} %get-tuple-element.140), channel_id=1, source_target_pairs={{0,4},{1,5},{2,6},{3,7},{4,0},{5,1},{6,2},{7,3},{8,12},{9,13},{10,... | collective-permute-start | bytes 1966088 | tf_op jit(solution)/shard_map/ppermute | solution.py:1353
  328.5 54.0 %collective-permute-start.48 = (bf16[2,512,128]{2,1,0:T(8,128)(2,1)S(1)}, bf16[2,512,128]{2,1,0:T(8,128)(2,1)S(1)}, u32[]{:S(2)}, u32[]{:S(2)}) collective-permute-start(bf16[2,512,128]{2,1,0:T(8,128)(2,1)S(1)} %convert_bitcast_fusion), channel_id=1, source_target_pairs={{0,1},{1,0},{2,3},{3,2},{4,5},{5,4},{6,7},{7,6},{8,9},{9,8},{10,11... | collective-permute-start | bytes 786440 | tf_op jit(solution)/shard_map/ppermute | solution.py:1353
  (63 other events, 491.6 us)

commit v3 on v2

--- a/solution.py
+++ b/solution.py
@@ -25,6 +25,8 @@
 LANES = 2 * HDIM
 CHUNK = 128
 TOKENS_BACK = 2
+UNROLL = 4
+UNROLL_PAIR = 2
 
 PRECISE = lax.Precision.HIGHEST
 EPSILON = 1e-05
@@ -255,7 +257,7 @@
         )
         return carry
 
-    lax.fori_loop(0, HEADS, head, 0)
+    lax.fori_loop(0, HEADS, head, 0, unroll=UNROLL)
     wait(0)
     heads = heads_ref[...].T
 
@@ -339,7 +341,7 @@
             pack_ref[rows, :] = dot(value, probs, 1, 0).astype(BF)
         return carry
 
-    lax.fori_loop(0, PAIRS, pair, 0)
+    lax.fori_loop(0, PAIRS, pair, 0, unroll=UNROLL_PAIR)
 
 
 def attend(place, tokens, gain, bias, own_attend, brought):
@@ -721,7 +723,7 @@
         proj_grad_ref[2, :, columns] = jnp.where(low, value_grads[0], value_grads[1]).astype(BF)
         return carry
 
-    lax.fori_loop(0, PAIRS, pair, 0)
+    lax.fori_loop(0, PAIRS, pair, 0, unroll=UNROLL_PAIR)
     core = place_ref[1]
     owns = pl.ds(pl.multiple_of(core * HALF, HALF), HALF)
     others = pl.ds(pl.multiple_of((1 - core) * HALF, HALF), HALF)
@@ -858,7 +860,7 @@
             key_grad_ref[piece, :] += jnp.where(lane == h, total, 0.0)
         return carry
 
-    lax.fori_loop(0, HEADS, head, 0)
+    lax.fori_loop(0, HEADS, head, 0, unroll=UNROLL)
     for ref, start in ((keep_ref, core * HALF), (send_ref, (1 - core) * HALF)):
         for part in range(2):
             rows = pl.ds(pl.multiple_of(start + part * TABLE_PAD, TABLE_PAD), TABLE_PAD)

time: 435 us -> 444 us (1.021)
  Pallas kernels: 172 us -> 177 us
    pallas_call x1, Pallas kernels: 21.1 us -> 34.6 us  [expand(): pl.pallas_call(expand_kernel, out_shape=(shape((2, PATCHES, UNITS), BF),...]
  transfers between devices with their start and end apart: 49 -> 49, of which waited for: 20 -> 20; matrix products, arithmetic and copies ran while one was open for 8% -> 8% of each run, Pallas kernels for 29% -> 26%
where the time goes in v3:
time: 444 us; the launch traced here: 440 us
  Pallas kernels  177 us (40%)
  waiting for transfers between devices  149 us (34%)
  starting transfers between devices  52.9 us (12%)
  other arithmetic  34.6 us (8%)
  local copies, waits for them, and re-layouts  21.2 us (5%)
  between operations  4.91 us (1%)
    ppermute x47, waiting for transfers between devices, partner(): return lax.ppermute(block, axis, [(i, i ^ distance) for i in range(size)])  149 us
    ppermute x47, starting transfers between devices, partner(): return lax.ppermute(block, axis, [(i, i ^ distance) for i in range(size)])  47.3 us
    pallas_call x1, Pallas kernels, expand(): pl.pallas_call(expand_kernel, out_shape=(shape((2, PATCHES, UNITS), BF),...  34.6 us
    pallas_call x1, Pallas kernels, attend_back(): pl.pallas_call(attend_back_kernel, out_shape=(shape((4, PATCHES, HALF), B...  27.1 us
    pallas_call x1, Pallas kernels, attend(): pl.pallas_call(attend_kernel, out_shape=(shape((2 * D, PATCHES), BF), sha...  19.2 us
    pallas_call x2, Pallas kernels, wide_grads(): pl.pallas_call(functools.partial(wide_kernel, which, by_pipe), in_specs=[...  17.6 us
    pallas_call x1, Pallas kernels, contract(): pl.pallas_call(contract_kernel, out_shape=(shape((PATCHES, D), BF), shape...  15.9 us
    pallas_call x1, Pallas kernels, aggregate_back(): pl.pallas_call(aggregate_back_kernel, out_shape=(shape((TAIL, HALF), BF),...  13.1 us
  transfers between devices with their start and end apart: 49, of which 20 were waited for; matrix products, arithmetic and copies ran while one was open for 8% of the time, Pallas kernels for 26%

profile of v3, /device:TPU:0, one launch (start us, length us, event | category | flops | bytes accessed | tf_op | source)
XLA Modules:
  0.0 440.0 jit_solution(9939506414008687656)
XLA Ops:
  0.7 3.0 bitcast_select_fusion.2
  3.7 2.9 collective-permute-start.3
  9.7 5.7 %tables.1 = (f32[16,1024]{1,0:T(8,128)}, f32[240,16]{1,0:T(8,128)}, f32[1024,256]{1,0:T(8,128)}) custom-call(f32[1,1024]{1,0:T(1,128)} %bitcast.151, bf16[240,1024]{1,0:T(8,128)(2,1)} %pad_maximum_fusion.9.table_ref, bf16[3,1024,1024]{2,1,0:T(8,128)(2,1)} %bitcast.123), custom_call_target="tpu_custom_call" | custom-call | flops 1000 | bytes 1000 | tf_op jit(solution)/shard_map/tables/pallas_call | solution.py:147
  18.5 3.1 collective-permute-start.9
  38.5 10.3 %collective-permute-done.4 = bf16[256,1024]{1,0:T(8,128)(2,1)} collective-permute-done((bf16[256,1024]{1,0:T(8,128)(2,1)S(1)}, bf16[256,1024]{1,0:T(8,128)(2,1)}, u32[]{:S(2)}, u32[]{:S(2)}) %collective-permute-start.4) | collective-permute-done | bytes 524320 | tf_op jit(solution)/shard_map/ppermute | solution.py:1355
  55.1 9.0 %collective-permute-done.6 = bf16[256,1024]{1,0:T(8,128)(2,1)} collective-permute-done((bf16[256,1024]{1,0:T(8,128)(2,1)S(1)}, bf16[256,1024]{1,0:T(8,128)(2,1)}, u32[]{:S(2)}, u32[]{:S(2)}) %collective-permute-start.6) | collective-permute-done | bytes 524320 | tf_op jit(solution)/shard_map/ppermute | solution.py:1355
  70.2 9.0 %aggregate.1 = (bf16[512,1024]{1,0:T(8,128)(2,1)}, bf16[1024,512]{1,0:T(8,128)(2,1)}, f32[16,48,512]{2,1,0:T(8,128)}, f32[4,48,512]{2,1,0:T(8,128)}) custom-call(s32[3]{0:T(128)} %pad_add_fusion.place_ref, f32[1]{0:T(128)} %dynamic_slice.61.alive_ref, f32[384,128]{1,0:T(8,128)} %get-tuple-element.218.own_field_ref, f32[384,128]{1,0:T(8,128)} %copy-done.33, ...), custom_call_target="tpu_custom_call" | custom-call | flops 1000 | bytes 1000 | tf_op jit(solution)/shard_map/aggregate/pallas_call | solution.py:274
  80.7 2.6 collective-permute-done.17
  85.7 19.2 %attend.1 = (bf16[2048,512]{1,0:T(8,128)(2,1)}, bf16[3,512,1024]{2,1,0:T(8,128)(2,1)}, f32[8,2,512]{2,1,0:T(2,128)}) custom-call(s32[3]{0:T(128)} %pad_add_fusion.place_ref, bf16[512,1024]{1,0:T(8,128)(2,1)} %get-tuple-element.92.tokens_ref, f32[2,1024]{1,0:T(2,128)} %gain_ref.5, f32[2,1024]{1,0:T(2,128)} %norm_bias_ref.1, bf16[3,1024,1024]{2,1,0:T(8,128)(2,1)} %bitcast.124, ...), custom_call_target="tpu_custom_call" | custom-call | flops 1000 | bytes 1000 | tf_op jit(solution)/shard_map/attend/pallas_call | solution.py:348
  111.8 34.6 %expand.1 = (bf16[2,512,4608]{2,1,0:T(8,128)(2,1)}, f32[512,1024]{1,0:T(8,128)}, bf16[512,1024]{1,0:T(8,128)(2,1)}, f32[1,4096]{1,0:T(1,128)}) custom-call(s32[3]{0:T(128)} %pad_add_fusion.place_ref, bf16[512,1024]{1,0:T(8,128)(2,1)} %get-tuple-element.92.tokens_ref, bf16[512,1024]{1,0:T(8,128)(2,1)} %fusion.out_ref.left_any, f32[2,1024]{1,0:T(2,128)} %gain_ref.5, ...), custom_call_target="tpu_custom_call" | custom-call | flops 1000 | bytes 1000 | tf_op jit(solution)/shard_map/expand/pallas_call | solution.py:517
  149.0 15.9 %contract.1 = (bf16[512,1024]{1,0:T(8,128)(2,1)}, f32[512,1024]{1,0:T(8,128)}, bf16[512,1024]{1,0:T(8,128)(2,1)}, f32[1,1024]{1,0:T(1,128)}, f32[1,1024]{1,0:T(1,128)}, /*index=5*/f32[1,1024]{1,0:T(1,128)}) custom-call(s32[3]{0:T(128)} %pad_add_fusion.place_ref, f32[2]{0:T(128)} %pad_maximum_fusion.15.scalars_ref, f32[1,1024]{1,0:T(1,128)} %slice.72.gain_ref, ...), custom_call_target="tpu_custom_call" | custom-call | flops 1000 | bytes 1000 | tf_op jit(solution)/shard_map/contract/pallas_call | solution.py:633
  164.9 8.7 %down_grads.1 = (bf16[2,2,2,512,256]{4,3,2,1,0:T(8,128)(2,1)}, bf16[2,2,2,512,256]{4,3,2,1,0:T(8,128)(2,1)}) custom-call(s32[2]{0:T(128)} %pad_add_fusion.1.place_ref, bf16[512,1024]{1,0:T(8,128)(2,1)} %fusion.out_ref.left_any, bf16[2,512,4608]{2,1,0:T(8,128)(2,1)} %get-tuple-element.100.units_any.own_any, ...), custom_call_target="tpu_custom_call" | custom-call | flops 1000 | bytes 1000 | tf_op jit(solution)/shard_map/down_grads/pallas_call | solution.py:998
  175.0 8.9 %up_grads.1 = (bf16[2,2,2,512,256]{4,3,2,1,0:T(8,128)(2,1)}, bf16[2,2,2,512,256]{4,3,2,1,0:T(8,128)(2,1)}) custom-call(s32[2]{0:T(128)} %pad_add_fusion.1.place_ref, bf16[512,1024]{1,0:T(8,128)(2,1)} %get-tuple-element.106.left_any, bf16[2,512,4608]{2,1,0:T(8,128)(2,1)} %get-tuple-element.100.units_any.own_any, ...), custom_call_target="tpu_custom_call" | custom-call | flops 1000 | bytes 1000 | tf_op jit(solution)/shard_map/up_grads/pallas_call | solution.py:998
  184.6 27.1 %attend_back.1 = (bf16[4,512,512]{2,1,0:T(8,128)(2,1)}, bf16[4,512,512]{2,1,0:T(8,128)(2,1)}, bf16[512,1024]{1,0:T(8,128)(2,1)}, f32[1,1024]{1,0:T(1,128)}, f32[1,1024]{1,0:T(1,128)}) custom-call(s32[3]{0:T(128)} %pad_add_fusion.place_ref, f32[512,1024]{1,0:T(8,128)} %get-tuple-element.102.grad_ref, bf16[512,1024]{1,0:T(8,128)(2,1)} %get-tuple-element.103.refs_0_.branch_ref, ...), custom_call_target="tpu_custom_call" | custom-call | flops 1000 | bytes 1000 | tf_op jit(solution)/shard_map/attend_back/pallas_call | solution.py:763
  212.1 13.1 %aggregate_back.1 = (bf16[1024,512]{1,0:T(8,128)(2,1)}, bf16[1024,512]{1,0:T(8,128)(2,1)}, f32[768,128]{1,0:T(8,128)}) custom-call(s32[3]{0:T(128)} %pad_add_fusion.place_ref, f32[1]{0:T(128)} %dynamic_slice.61.alive_ref, bf16[512,1024]{1,0:T(8,128)(2,1)} %get-tuple-element.108.token_grad_ref, f32[4,48,512]{2,1,0:T(8,128)} %get-tuple-element.109.pixels_ref, ...), custom_call_target="tpu_custom_call" | custom-call | flops 1000 | bytes 1000 | tf_op jit(solution)/shard_map/aggregate_back/pallas_call | solution.py:901
  225.4 6.4 %collective-permute-done.26.up_came = bf16[2,2,2,512,256]{4,3,2,1,0:T(8,128)(2,1)S(1)} collective-permute-done((bf16[2,2,2,512,256]{4,3,2,1,0:T(8,128)(2,1)}, bf16[2,2,2,512,256]{4,3,2,1,0:T(8,128)(2,1)S(1)}, u32[]{:S(2)}, u32[]{:S(2)}) %collective-permute-start.26) | collective-permute-done | bytes 2097184 | tf_op jit(solution)/shard_map/ppermute | solution.py:1355
  233.1 3.9 first_sums.1
  241.1 11.3 %square_grads.1 = (bf16[4,512,512]{2,1,0:T(8,128)(2,1)}, bf16[4,512,512]{2,1,0:T(8,128)(2,1)}, bf16[2,4,128,512]{3,2,1,0:T(8,128)(2,1)}, bf16[2,4,128,512]{3,2,1,0:T(8,128)(2,1)}) custom-call(s32[2]{0:T(128)} %pad_add_fusion.2.place_ref, bf16[1024,512]{1,0:T(8,128)(2,1)} %get-tuple-element.119.after_any.tail_own, bf16[1024,512]{1,0:T(8,128)(2,1)} %copy-done.25, ...), custom_call_target="tpu_custom_call" | custom-call | flops 1000 | bytes 1000 | tf_op jit(solution)/shard_map/square_grads/pallas_call | solution.py:1118
  252.5 9.1 %collective-permute-done.27.down_brought = bf16[4,512,256]{2,1,0:T(8,128)(2,1)S(1)} collective-permute-done((bf16[4,512,256]{2,1,0:T(8,128)(2,1)}, bf16[4,512,256]{2,1,0:T(8,128)(2,1)S(1)}, u32[]{:S(2)}, u32[]{:S(2)}) %collective-permute-start.27) | collective-permute-done | bytes 1048608 | tf_op jit(solution)/shard_map/ppermute | solution.py:1355
  263.4 4.7 %second_sums.1 = (bf16[2,512,256]{2,1,0:T(8,128)(2,1)}, bf16[2,512,256]{2,1,0:T(8,128)(2,1)}, bf16[2,512,256]{2,1,0:T(8,128)(2,1)}, bf16[2,512,256]{2,1,0:T(8,128)(2,1)}) custom-call(bf16[2,2,2,512,256]{4,3,2,1,0:T(8,128)(2,1)} %get-tuple-element.105.refs_0_.refs_8_.down_keep, bf16[2,2,2,512,256]{4,3,2,1,0:T(8,128)(2,1)} %copy-done.11, ...), custom_call_target="tpu_custom_call" | custom-call | flops 1000 | bytes 1000 | tf_op jit(solution)/shard_map/second_sums/pallas_call | solution.py:1177
  270.1 3.6 collective-permute-start.36
  273.7 17.8 %collective-permute-done.29.came.cross_came = bf16[2,4,128,512]{3,2,1,0:T(8,128)(2,1)S(1)} collective-permute-done((bf16[2,4,128,512]{3,2,1,0:T(8,128)(2,1)S(1)}, bf16[2,4,128,512]{3,2,1,0:T(8,128)(2,1)S(1)}, u32[]{:S(2)}, u32[]{:S(2)}) %collective-permute-start.29) | collective-permute-done | bytes 1048608 | tf_op jit(solution)/shard_map/ppermute | solution.py:1355
  295.9 2.6 collective-permute-start.35
  301.9 17.3 %collective-permute-done.35 = bf16[2,512,256]{2,1,0:T(8,128)(2,1)S(1)} collective-permute-done((bf16[2,512,256]{2,1,0:T(8,128)(2,1)S(1)}, bf16[2,512,256]{2,1,0:T(8,128)(2,1)S(1)}, u32[]{:S(2)}, u32[]{:S(2)}) %collective-permute-start.35) | collective-permute-done | bytes 524320 | tf_op jit(solution)/shard_map/ppermute | solution.py:1355
  328.0 4.4 fourth_sums.1
  332.4 3.6 collective-permute-start.39
  339.0 13.3 %collective-permute-done.39 = bf16[640,512]{1,0:T(8,128)(2,1)} collective-permute-done((bf16[640,512]{1,0:T(8,128)(2,1)}, bf16[640,512]{1,0:T(8,128)(2,1)}, u32[]{:S(2)}, u32[]{:S(2)}) %collective-permute-start.39) | collective-permute-done | bytes 655392 | tf_op jit(solution)/shard_map/ppermute | solution.py:1355
  352.3 37.0 %collective-permute-done.38 = bf16[640,512]{1,0:T(8,128)(2,1)} collective-permute-done((bf16[640,512]{1,0:T(8,128)(2,1)}, bf16[640,512]{1,0:T(8,128)(2,1)}, u32[]{:S(2)}, u32[]{:S(2)}) %collective-permute-start.38) | collective-permute-done | bytes 655392 | tf_op jit(solution)/shard_map/ppermute | solution.py:1355
  392.7 3.6 collective-permute-done.40
  404.9 4.0 collective-permute-done.42
  413.0 9.3 %collective-permute-done.44 = bf16[4,128,512]{2,1,0:T(8,128)(2,1)S(1)} collective-permute-done((bf16[4,128,512]{2,1,0:T(8,128)(2,1)S(1)}, bf16[4,128,512]{2,1,0:T(8,128)(2,1)S(1)}, u32[]{:S(2)}, u32[]{:S(2)}) %collective-permute-start.44) | collective-permute-done | bytes 524320 | tf_op jit(solution)/shard_map/ppermute | solution.py:1355
  428.8 8.3 %finish.1 = (f32[512,1024]{1,0:T(8,128)}, f32[2,1024]{1,0:T(2,128)}, f32[2,1024]{1,0:T(2,128)}, f32[1,1024]{1,0:T(1,128)}, f32[4,1024]{1,0:T(4,128)}, /*index=5*...) custom-call(s32[5]{0:T(128)} %stack.173.place_ref, ...), custom_call_target="tpu_custom_call" | custom-call | flops 1000 | bytes 1000 | tf_op jit(solution)/shard_map/finish/pallas_call | solution.py:1324
  (245 shorter events, 101.8 us)
Async XLA Ops:
  3.7 29.3 %collective-permute-start.3 = (bf16[256,1024]{1,0:T(8,128)(2,1)}, bf16[256,1024]{1,0:T(8,128)(2,1)}, u32[]{:S(2)}, u32[]{:S(2)}) collective-permute-start(bf16[256,1024]{1,0:T(8,128)(2,1)} %get-tuple-element.193), channel_id=1, source_target_pairs={{0,16},{16,0},{1,17},{17,1},{2,18},{18,2},{3,19},{19,3},{4,20},{20... | collective-permute-start | bytes 1572872 | tf_op jit(solution)/shard_map/ppermute | solution.py:1355
  18.5 18.2 %collective-permute-start.9 = (f32[240,16]{1,0:T(8,128)}, f32[240,16]{1,0:T(8,128)}, u32[]{:S(2)}, u32[]{:S(2)}) collective-permute-start(f32[240,16]{1,0:T(8,128)} %get-tuple-element.90), channel_id=1, source_target_pairs={{0,16},{1,17},{2,18},{3,19},{4,20},{5,21},{6,22},{7,23},{8,24},{9,... | collective-permute-start | bytes 46088 | tf_op jit(solution)/shard_map/ppermute | solution.py:1492
  33.0 15.7 %collective-permute-start.4 = (bf16[256,1024]{1,0:T(8,128)(2,1)S(1)}, bf16[256,1024]{1,0:T(8,128)(2,1)}, u32[]{:S(2)}, u32[]{:S(2)}) collective-permute-start(bf16[256,1024]{1,0:T(8,128)(2,1)S(1)} %get-tuple-element.86), channel_id=1, source_target_pairs={{0,16},{16,0},{1,17},{17,1},{2,18},{18,2},{3,19},{19,3},{4,20},{20... | collective-permute-start | bytes 1572872 | tf_op jit(solution)/shard_map/ppermute | solution.py:1355
  33.0 18.3 %collective-permute-start.11 = (bf16[256,1024]{1,0:T(8,128)(2,1)}, bf16[256,1024]{1,0:T(8,128)(2,1)S(1)}, u32[]{:S(2)}, u32[]{:S(2)}) collective-permute-start(bf16[256,1024]{1,0:T(8,128)(2,1)} %collective-permute-done.3), channel_id=1, source_target_pairs={{0,2},{1,3},{2,0},{3,1},{4,6},{5,7},{6,4},{7,5},{8,10},{9,11},{10,... | collective-permute-start | bytes 1572872 | tf_op jit(solution)/shard_map/ppermute | solution.py:1355
  34.9 34.1 %collective-permute-start.7 = (f32[384,128]{1,0:T(8,128)S(1)}, f32[384,128]{1,0:T(8,128)S(1)}, u32[]{:S(2)}, u32[]{:S(2)}) collective-permute-start(f32[384,128]{1,0:T(8,128)S(1)} %get-tuple-element.217), channel_id=1, source_target_pairs={{0,16},{16,0},{1,17},{17,1},{2,18},{18,2},{3,19},{19,3},{4,20},{20... | collective-permute-start | bytes 589832 | tf_op jit(solution)/shard_map/ppermute | solution.py:1355
  48.8 15.3 %collective-permute-start.6 = (bf16[256,1024]{1,0:T(8,128)(2,1)S(1)}, bf16[256,1024]{1,0:T(8,128)(2,1)}, u32[]{:S(2)}, u32[]{:S(2)}) collective-permute-start(bf16[256,1024]{1,0:T(8,128)(2,1)S(1)} %get-tuple-element.88), channel_id=1, source_target_pairs={{0,16},{16,0},{1,17},{17,1},{2,18},{18,2},{3,19},{19,3},{4,20},{20... | collective-permute-start | bytes 1572872 | tf_op jit(solution)/shard_map/ppermute | solution.py:1355
  52.5 16.5 %collective-permute-start.12 = (bf16[2,256,1024]{2,1,0:T(8,128)(2,1)S(1)}, bf16[2,256,1024]{2,1,0:T(8,128)(2,1)S(1)}, u32[]{:S(2)}, u32[]{:S(2)}) collective-permute-start(bf16[2,256,1024]{2,1,0:T(8,128)(2,1)S(1)} %pad_maximum_fusion.1.brought_ref.refs_0_), channel_id=1, source_target_pairs={{0,1},{1,0},{2,3},{3,2},{4,5},{5,4},{6,7},{7,6},{8,9},{9,8},{10,11... | collective-permute-start | bytes 3145736 | tf_op jit(solution)/shard_map/ppermute | solution.py:1355
  52.8 14.7 %collective-permute-start.13 = (bf16[256,1024]{1,0:T(8,128)(2,1)}, bf16[256,1024]{1,0:T(8,128)(2,1)}, u32[]{:S(2)}, u32[]{:S(2)}) collective-permute-start(bf16[256,1024]{1,0:T(8,128)(2,1)} %collective-permute-done.4), channel_id=1, source_target_pairs={{0,2},{1,3},{2,0},{3,1},{4,6},{5,7},{6,4},{7,5},{8,10},{9,11},{10,... | collective-permute-start | bytes 1572872 | tf_op jit(solution)/shard_map/ppermute | solution.py:1355
  64.1 15.1 %collective-permute-start.15 = (bf16[256,1024]{1,0:T(8,128)(2,1)}, bf16[256,1024]{1,0:T(8,128)(2,1)S(1)}, u32[]{:S(2)}, u32[]{:S(2)}) collective-permute-start(bf16[256,1024]{1,0:T(8,128)(2,1)} %collective-permute-done.6), channel_id=1, source_target_pairs={{0,2},{1,3},{2,0},{3,1},{4,6},{5,7},{6,4},{7,5},{8,10},{9,11},{10,... | collective-permute-start | bytes 1572872 | tf_op jit(solution)/shard_map/ppermute | solution.py:1355
  68.8 14.8 %collective-permute-start.14 = (bf16[2,256,1024]{2,1,0:T(8,128)(2,1)S(1)}, bf16[2,256,1024]{2,1,0:T(8,128)(2,1)S(1)}, u32[]{:S(2)}, u32[]{:S(2)}) collective-permute-start(bf16[2,256,1024]{2,1,0:T(8,128)(2,1)S(1)} %pad_maximum_fusion.2.refs_2_.refs_4_), channel_id=1, source_target_pairs={{0,1},{1,0},{2,3},{3,2},{4,5},{5,4},{6,7},{7,6},{8,9},{9,8},{10,11... | collective-permute-start | bytes 3145736 | tf_op jit(solution)/shard_map/ppermute | solution.py:1355
  68.9 14.4 %collective-permute-start.17 = (bf16[256,1024]{1,0:T(8,128)(2,1)S(1)}, bf16[256,1024]{1,0:T(8,128)(2,1)}, u32[]{:S(2)}, u32[]{:S(2)}) collective-permute-start(bf16[256,1024]{1,0:T(8,128)(2,1)S(1)} %get-tuple-element.95), channel_id=1, source_target_pairs={{0,16},{16,0},{1,17},{17,1},{2,18},{18,2},{3,19},{19,3},{4,20},{20... | collective-permute-start | bytes 1572872 | tf_op jit(solution)/shard_map/ppermute | solution.py:1355
  83.3 21.5 %collective-permute-start.18 = (bf16[256,1024]{1,0:T(8,128)(2,1)}, bf16[256,1024]{1,0:T(8,128)(2,1)S(1)}, u32[]{:S(2)}, u32[]{:S(2)}) collective-permute-start(bf16[256,1024]{1,0:T(8,128)(2,1)} %collective-permute-done.17), channel_id=1, source_target_pairs={{0,2},{1,3},{2,0},{3,1},{4,6},{5,7},{6,4},{7,5},{8,10},{9,11},{10,... | collective-permute-start | bytes 1572872 | tf_op jit(solution)/shard_map/ppermute | solution.py:1355
  83.6 26.9 %collective-permute-start.20 = (bf16[1024,512]{1,0:T(8,128)(2,1)S(1)}, bf16[1024,512]{1,0:T(8,128)(2,1)S(1)}, u32[]{:S(2)}, u32[]{:S(2)}) collective-permute-start(bf16[1024,512]{1,0:T(8,128)(2,1)S(1)} %copy-done.23), channel_id=1, source_target_pairs={{0,1},{1,0},{2,3},{3,2},{4,5},{5,4},{6,7},{7,6},{8,9},{9,8},{10,11... | collective-permute-start | bytes 3145736 | tf_op jit(solution)/shard_map/ppermute | solution.py:1355
  146.5 18.5 %collective-permute-start.21 = (bf16[2,512,4608]{2,1,0:T(8,128)(2,1)}, bf16[2,512,4608]{2,1,0:T(8,128)(2,1)}, u32[]{:S(2)}, u32[]{:S(2)}) collective-permute-start(bf16[2,512,4608]{2,1,0:T(8,128)(2,1)} %get-tuple-element.100.units_any.own_any), channel_id=1, source_target_pairs={{0,1},{1,0},{2,3},{3,2},{4,5},{5,4},{6,7},{7,6},{8,9},{9,8},{10,11... | collective-permute-start | bytes 28311560 | tf_op jit(solution)/shard_map/ppermute | solution.py:1355
  173.7 51.7 %collective-permute-start.25 = (bf16[2,2,2,512,256]{4,3,2,1,0:T(8,128)(2,1)}, bf16[2,2,2,512,256]{4,3,2,1,0:T(8,128)(2,1)S(1)}, u32[]{:S(2)}, u32[]{:S(2)}) collective-permute-start(bf16[2,2,2,512,256]{4,3,2,1,0:T(8,128)(2,1)} %get-tuple-element.123), channel_id=1, source_target_pairs={{0,16},{16,0},{1,17},{17,1},{2,18},{18,2},{3,19},{19,3},{4,20},{20... | collective-permute-start | bytes 6291464 | tf_op jit(solution)/shard_map/ppermute | solution.py:1355
  183.9 47.9 %collective-permute-start.26 = (bf16[2,2,2,512,256]{4,3,2,1,0:T(8,128)(2,1)}, bf16[2,2,2,512,256]{4,3,2,1,0:T(8,128)(2,1)S(1)}, u32[]{:S(2)}, u32[]{:S(2)}) collective-permute-start(bf16[2,2,2,512,256]{4,3,2,1,0:T(8,128)(2,1)} %get-tuple-element.124), channel_id=1, source_target_pairs={{0,2},{1,3},{2,0},{3,1},{4,6},{5,7},{6,4},{7,5},{8,10},{9,11},{10,... | collective-permute-start | bytes 6291464 | tf_op jit(solution)/shard_map/ppermute | solution.py:1355
  184.5 55.6 %collective-permute-start.23 = (bf16[2048,512]{1,0:T(8,128)(2,1)S(1)}, bf16[2048,512]{1,0:T(8,128)(2,1)}, u32[]{:S(2)}, u32[]{:S(2)}) collective-permute-start(bf16[2048,512]{1,0:T(8,128)(2,1)S(1)} %copy-done.10), channel_id=1, source_target_pairs={{0,1},{1,0},{2,3},{3,2},{4,5},{5,4},{6,7},{7,6},{8,9},{9,8},{10,11... | collective-permute-start | bytes 6291464 | tf_op jit(solution)/shard_map/ppermute | solution.py:1355
  211.6 28.5 %collective-permute-start.24 = (bf16[4,512,512]{2,1,0:T(8,128)(2,1)}, bf16[4,512,512]{2,1,0:T(8,128)(2,1)}, u32[]{:S(2)}, u32[]{:S(2)}) collective-permute-start(bf16[4,512,512]{2,1,0:T(8,128)(2,1)} %get-tuple-element.122), channel_id=1, source_target_pairs={{0,1},{1,0},{2,3},{3,2},{4,5},{5,4},{6,7},{7,6},{8,9},{9,8},{10,11... | collective-permute-start | bytes 6291464 | tf_op jit(solution)/shard_map/ppermute | solution.py:1355
  225.2 14.9 %collective-permute-start.22 = (bf16[1024,512]{1,0:T(8,128)(2,1)}, bf16[1024,512]{1,0:T(8,128)(2,1)S(1)}, u32[]{:S(2)}, u32[]{:S(2)}) collective-permute-start(bf16[1024,512]{1,0:T(8,128)(2,1)} %get-tuple-element.120), channel_id=1, source_target_pairs={{0,1},{1,0},{2,3},{3,2},{4,5},{5,4},{6,7},{7,6},{8,9},{9,8},{10,11... | collective-permute-start | bytes 3145736 | tf_op jit(solution)/shard_map/ppermute | solution.py:1355
  237.0 24.5 %collective-permute-start.27 = (bf16[4,512,256]{2,1,0:T(8,128)(2,1)}, bf16[4,512,256]{2,1,0:T(8,128)(2,1)S(1)}, u32[]{:S(2)}, u32[]{:S(2)}) collective-permute-start(bf16[4,512,256]{2,1,0:T(8,128)(2,1)} %get-tuple-element.125.refs_0_), channel_id=1, source_target_pairs={{0,2},{1,3},{2,0},{3,1},{4,6},{5,7},{6,4},{7,5},{8,10},{9,11},{10,... | collective-permute-start | bytes 3145736 | tf_op jit(solution)/shard_map/ppermute | solution.py:1355
  237.8 24.6 %collective-permute-start.28 = (bf16[4,512,256]{2,1,0:T(8,128)(2,1)}, bf16[4,512,256]{2,1,0:T(8,128)(2,1)S(1)}, u32[]{:S(2)}, u32[]{:S(2)}) collective-permute-start(bf16[4,512,256]{2,1,0:T(8,128)(2,1)} %get-tuple-element.126.refs_1_), channel_id=1, source_target_pairs={{0,16},{16,0},{1,17},{17,1},{2,18},{18,2},{3,19},{19,3},{4,20},{20... | collective-permute-start | bytes 3145736 | tf_op jit(solution)/shard_map/ppermute | solution.py:1355
  268.0 23.5 %collective-permute-start.29 = (bf16[2,4,128,512]{3,2,1,0:T(8,128)(2,1)S(1)}, bf16[2,4,128,512]{3,2,1,0:T(8,128)(2,1)S(1)}, u32[]{:S(2)}, u32[]{:S(2)}) collective-permute-start(bf16[2,4,128,512]{3,2,1,0:T(8,128)(2,1)S(1)} %copy-done.43), channel_id=1, source_target_pairs={{0,16},{16,0},{1,17},{17,1},{2,18},{18,2},{3,19},{19,3},{4,20},{20... | collective-permute-start | bytes 3145736 | tf_op jit(solution)/shard_map/ppermute | solution.py:1355
  269.5 56.7 %collective-permute-start.32 = (bf16[4,512,512]{2,1,0:T(8,128)(2,1)}, bf16[4,512,512]{2,1,0:T(8,128)(2,1)S(1)}, u32[]{:S(2)}, u32[]{:S(2)}) collective-permute-start(bf16[4,512,512]{2,1,0:T(8,128)(2,1)} %get-tuple-element.138.after_any), channel_id=1, source_target_pairs={{0,2},{1,3},{2,0},{3,1},{4,6},{5,7},{6,4},{7,5},{8,10},{9,11},{10,... | collective-permute-start | bytes 6291464 | tf_op jit(solution)/shard_map/ppermute | solution.py:1355
  270.1 29.9 %collective-permute-start.36 = (bf16[2,512,256]{2,1,0:T(8,128)(2,1)}, bf16[2,512,256]{2,1,0:T(8,128)(2,1)S(1)}, u32[]{:S(2)}, u32[]{:S(2)}) collective-permute-start(bf16[2,512,256]{2,1,0:T(8,128)(2,1)} %get-tuple-element.133), channel_id=1, source_target_pairs={{0,12},{1,13},{2,14},{3,15},{4,8},{5,9},{6,10},{7,11},{8,4},{9,5},... | collective-permute-start | bytes 1572872 | tf_op jit(solution)/shard_map/ppermute | solution.py:1355
  294.8 31.4 %collective-permute-start.30 = (bf16[512,1024]{1,0:T(8,128)(2,1)S(1)}, bf16[512,1024]{1,0:T(8,128)(2,1)S(1)}, u32[]{:S(2)}, u32[]{:S(2)}) collective-permute-start(bf16[512,1024]{1,0:T(8,128)(2,1)S(1)} %broadcast_select_fusion), channel_id=1, source_target_pairs={{0,16},{16,0},{1,17},{17,1},{2,18},{18,2},{3,19},{19,3},{4,20},{20... | collective-permute-start | bytes 3145736 | tf_op jit(solution)/shard_map/ppermute | solution.py:1355
  295.9 23.3 %collective-permute-start.35 = (bf16[2,512,256]{2,1,0:T(8,128)(2,1)S(1)}, bf16[2,512,256]{2,1,0:T(8,128)(2,1)S(1)}, u32[]{:S(2)}, u32[]{:S(2)}) collective-permute-start(bf16[2,512,256]{2,1,0:T(8,128)(2,1)S(1)} %copy-done.45), channel_id=1, source_target_pairs={{0,8},{1,9},{2,10},{3,11},{4,12},{5,13},{6,14},{7,15},{8,0},{9,1},... | collective-permute-start | bytes 1572872 | tf_op jit(solution)/shard_map/ppermute | solution.py:1355
  298.5 21.6 %collective-permute-start.34 = (bf16[2,512,256]{2,1,0:T(8,128)(2,1)S(1)}, bf16[2,512,256]{2,1,0:T(8,128)(2,1)S(1)}, u32[]{:S(2)}, u32[]{:S(2)}) collective-permute-start(bf16[2,512,256]{2,1,0:T(8,128)(2,1)S(1)} %copy-done.44), channel_id=1, source_target_pairs={{0,4},{1,5},{2,6},{3,7},{4,0},{5,1},{6,2},{7,3},{8,12},{9,13},{10,... | collective-permute-start | bytes 1572872 | tf_op jit(solution)/shard_map/ppermute | solution.py:1355
  300.0 26.1 %collective-permute-start.33 = (bf16[4,128,512]{2,1,0:T(8,128)(2,1)S(1)}, bf16[4,128,512]{2,1,0:T(8,128)(2,1)S(1)}, u32[]{:S(2)}, u32[]{:S(2)}) collective-permute-start(bf16[4,128,512]{2,1,0:T(8,128)(2,1)S(1)} %copy-done.28), channel_id=1, source_target_pairs={{0,2},{1,3},{2,0},{3,1},{4,6},{5,7},{6,4},{7,5},{8,10},{9,11},{10,... | collective-permute-start | bytes 1572872 | tf_op jit(solution)/shard_map/ppermute | solution.py:1355
  332.4 19.9 %collective-permute-start.39 = (bf16[640,512]{1,0:T(8,128)(2,1)}, bf16[640,512]{1,0:T(8,128)(2,1)}, u32[]{:S(2)}, u32[]{:S(2)}) collective-permute-start(bf16[640,512]{1,0:T(8,128)(2,1)} %get-tuple-element.142), channel_id=1, source_target_pairs={{0,12},{1,13},{2,14},{3,15},{4,8},{5,9},{6,10},{7,11},{8,4},{9,5},... | collective-permute-start | bytes 1966088 | tf_op jit(solution)/shard_map/ppermute | solution.py:1355
  336.0 53.3 %collective-permute-start.38 = (bf16[640,512]{1,0:T(8,128)(2,1)}, bf16[640,512]{1,0:T(8,128)(2,1)}, u32[]{:S(2)}, u32[]{:S(2)}) collective-permute-start(bf16[640,512]{1,0:T(8,128)(2,1)} %get-tuple-element.141), channel_id=1, source_target_pairs={{0,8},{1,9},{2,10},{3,11},{4,12},{5,13},{6,14},{7,15},{8,0},{9,1},... | collective-permute-start | bytes 1966088 | tf_op jit(solution)/shard_map/ppermute | solution.py:1355
  336.0 53.3 %collective-permute-start.37 = (bf16[640,512]{1,0:T(8,128)(2,1)}, bf16[640,512]{1,0:T(8,128)(2,1)}, u32[]{:S(2)}, u32[]{:S(2)}) collective-permute-start(bf16[640,512]{1,0:T(8,128)(2,1)} %get-tuple-element.140), channel_id=1, source_target_pairs={{0,4},{1,5},{2,6},{3,7},{4,0},{5,1},{6,2},{7,3},{8,12},{9,13},{10,... | collective-permute-start | bytes 1966088 | tf_op jit(solution)/shard_map/ppermute | solution.py:1355
  338.9 53.6 %collective-permute-start.48 = (bf16[2,512,128]{2,1,0:T(8,128)(2,1)S(1)}, bf16[2,512,128]{2,1,0:T(8,128)(2,1)S(1)}, u32[]{:S(2)}, u32[]{:S(2)}) collective-permute-start(bf16[2,512,128]{2,1,0:T(8,128)(2,1)S(1)} %convert_bitcast_fusion), channel_id=1, source_target_pairs={{0,1},{1,0},{2,3},{3,2},{4,5},{5,4},{6,7},{7,6},{8,9},{9,8},{10,11... | collective-permute-start | bytes 786440 | tf_op jit(solution)/shard_map/ppermute | solution.py:1355
  (63 other events, 511.5 us)

commit v4 on v3

--- a/solution.py
+++ b/solution.py
@@ -25,8 +25,8 @@
 LANES = 2 * HDIM
 CHUNK = 128
 TOKENS_BACK = 2
-UNROLL = 4
-UNROLL_PAIR = 2
+UNROLL = 2
+UNROLL_PAIR = 1
 
 PRECISE = lax.Precision.HIGHEST
 EPSILON = 1e-05

time: 444 us -> 431 us (0.971)
  Pallas kernels: 177 us -> 167 us
    pallas_call x1, Pallas kernels: 34.6 us -> 21.1 us  [expand(): pl.pallas_call(expand_kernel, out_shape=(shape((2, PATCHES, UNITS), BF),...]
  transfers between devices with their start and end apart: 49 -> 49, of which waited for: 20 -> 21; matrix products, arithmetic and copies ran while one was open for 8% -> 8% of each run, Pallas kernels for 26% -> 28%
where the time goes in v4:
time: 431 us; the launch traced here: 428 us
  Pallas kernels  167 us (39%)
  waiting for transfers between devices  147 us (34%)
  starting transfers between devices  52.6 us (12%)
  other arithmetic  34.6 us (8%)
  local copies, waits for them, and re-layouts  20.9 us (5%)
  between operations  4.89 us (1%)
    ppermute x47, waiting for transfers between devices, partner(): return lax.ppermute(block, axis, [(i, i ^ distance) for i in range(size)])  147 us
    ppermute x47, starting transfers between devices, partner(): return lax.ppermute(block, axis, [(i, i ^ distance) for i in range(size)])  47.3 us
    pallas_call x1, Pallas kernels, attend_back(): pl.pallas_call(attend_back_kernel, out_shape=(shape((4, PATCHES, HALF), B...  28.5 us
    pallas_call x1, Pallas kernels, expand(): pl.pallas_call(expand_kernel, out_shape=(shape((2, PATCHES, UNITS), BF),...  21.1 us
    pallas_call x1, Pallas kernels, attend(): pl.pallas_call(attend_kernel, out_shape=(shape((2 * D, PATCHES), BF), sha...  19.8 us
    pallas_call x2, Pallas kernels, wide_grads(): pl.pallas_call(functools.partial(wide_kernel, which, by_pipe), in_specs=[...  17.6 us
    pallas_call x1, Pallas kernels, contract(): pl.pallas_call(contract_kernel, out_shape=(shape((PATCHES, D), BF), shape...  16.4 us
    pallas_call x1, Pallas kernels, aggregate_back(): pl.pallas_call(aggregate_back_kernel, out_shape=(shape((TAIL, HALF), BF),...  13.5 us
  transfers between devices with their start and end apart: 49, of which 21 were waited for; matrix products, arithmetic and copies ran while one was open for 8% of the time, Pallas kernels for 28%

profile of v4, /device:TPU:0, one launch (start us, length us, event | category | flops | bytes accessed | tf_op | source)
XLA Modules:
  0.0 427.8 jit_solution(9384385960884581221)
XLA Ops:
  0.7 3.0 bitcast_select_fusion.2
  3.7 2.9 collective-permute-start.3
  9.7 5.7 %tables.1 = (f32[16,1024]{1,0:T(8,128)}, f32[240,16]{1,0:T(8,128)}, f32[1024,256]{1,0:T(8,128)}) custom-call(f32[1,1024]{1,0:T(1,128)} %bitcast.151, bf16[240,1024]{1,0:T(8,128)(2,1)} %pad_maximum_fusion.9.table_ref, bf16[3,1024,1024]{2,1,0:T(8,128)(2,1)} %bitcast.123), custom_call_target="tpu_custom_call" | custom-call | flops 1000 | bytes 1000 | tf_op jit(solution)/shard_map/tables/pallas_call | solution.py:147
  18.5 3.1 collective-permute-start.9
  30.2 2.6 collective-permute-start.2
  38.5 10.3 %collective-permute-done.4 = bf16[256,1024]{1,0:T(8,128)(2,1)} collective-permute-done((bf16[256,1024]{1,0:T(8,128)(2,1)S(1)}, bf16[256,1024]{1,0:T(8,128)(2,1)}, u32[]{:S(2)}, u32[]{:S(2)}) %collective-permute-start.4) | collective-permute-done | bytes 524320 | tf_op jit(solution)/shard_map/ppermute | solution.py:1355
  55.1 9.0 %collective-permute-done.6 = bf16[256,1024]{1,0:T(8,128)(2,1)} collective-permute-done((bf16[256,1024]{1,0:T(8,128)(2,1)S(1)}, bf16[256,1024]{1,0:T(8,128)(2,1)}, u32[]{:S(2)}, u32[]{:S(2)}) %collective-permute-start.6) | collective-permute-done | bytes 524320 | tf_op jit(solution)/shard_map/ppermute | solution.py:1355
  70.2 9.8 %aggregate.1 = (bf16[512,1024]{1,0:T(8,128)(2,1)}, bf16[1024,512]{1,0:T(8,128)(2,1)}, f32[16,48,512]{2,1,0:T(8,128)}, f32[4,48,512]{2,1,0:T(8,128)}) custom-call(s32[3]{0:T(128)} %pad_add_fusion.place_ref, f32[1]{0:T(128)} %dynamic_slice.61.alive_ref, f32[384,128]{1,0:T(8,128)} %get-tuple-element.218.own_field_ref, f32[384,128]{1,0:T(8,128)} %copy-done.33, ...), custom_call_target="tpu_custom_call" | custom-call | flops 1000 | bytes 1000 | tf_op jit(solution)/shard_map/aggregate/pallas_call | solution.py:274
  85.7 19.8 %attend.1 = (bf16[2048,512]{1,0:T(8,128)(2,1)}, bf16[3,512,1024]{2,1,0:T(8,128)(2,1)}, f32[8,2,512]{2,1,0:T(2,128)}) custom-call(s32[3]{0:T(128)} %pad_add_fusion.place_ref, bf16[512,1024]{1,0:T(8,128)(2,1)} %get-tuple-element.92.tokens_ref, f32[2,1024]{1,0:T(2,128)} %gain_ref.5, f32[2,1024]{1,0:T(2,128)} %norm_bias_ref.1, bf16[3,1024,1024]{2,1,0:T(8,128)(2,1)} %bitcast.124, ...), custom_call_target="tpu_custom_call" | custom-call | flops 1000 | bytes 1000 | tf_op jit(solution)/shard_map/attend/pallas_call | solution.py:348
  112.5 21.1 %expand.1 = (bf16[2,512,4608]{2,1,0:T(8,128)(2,1)}, f32[512,1024]{1,0:T(8,128)}, bf16[512,1024]{1,0:T(8,128)(2,1)}, f32[1,4096]{1,0:T(1,128)}) custom-call(s32[3]{0:T(128)} %pad_add_fusion.place_ref, bf16[512,1024]{1,0:T(8,128)(2,1)} %get-tuple-element.92.tokens_ref, bf16[512,1024]{1,0:T(8,128)(2,1)} %fusion.out_ref.left_any, f32[2,1024]{1,0:T(2,128)} %gain_ref.5, ...), custom_call_target="tpu_custom_call" | custom-call | flops 1000 | bytes 1000 | tf_op jit(solution)/shard_map/expand/pallas_call | solution.py:517
  136.1 16.4 %contract.1 = (bf16[512,1024]{1,0:T(8,128)(2,1)}, f32[512,1024]{1,0:T(8,128)}, bf16[512,1024]{1,0:T(8,128)(2,1)}, f32[1,1024]{1,0:T(1,128)}, f32[1,1024]{1,0:T(1,128)}, /*index=5*/f32[1,1024]{1,0:T(1,128)}) custom-call(s32[3]{0:T(128)} %pad_add_fusion.place_ref, f32[2]{0:T(128)} %pad_maximum_fusion.15.scalars_ref, f32[1,1024]{1,0:T(1,128)} %slice.72.gain_ref, ...), custom_call_target="tpu_custom_call" | custom-call | flops 1000 | bytes 1000 | tf_op jit(solution)/shard_map/contract/pallas_call | solution.py:633
  152.5 8.7 %down_grads.1 = (bf16[2,2,2,512,256]{4,3,2,1,0:T(8,128)(2,1)}, bf16[2,2,2,512,256]{4,3,2,1,0:T(8,128)(2,1)}) custom-call(s32[2]{0:T(128)} %pad_add_fusion.1.place_ref, bf16[512,1024]{1,0:T(8,128)(2,1)} %fusion.out_ref.left_any, bf16[2,512,4608]{2,1,0:T(8,128)(2,1)} %get-tuple-element.100.units_any.own_any, ...), custom_call_target="tpu_custom_call" | custom-call | flops 1000 | bytes 1000 | tf_op jit(solution)/shard_map/down_grads/pallas_call | solution.py:998
  162.6 8.9 %up_grads.1 = (bf16[2,2,2,512,256]{4,3,2,1,0:T(8,128)(2,1)}, bf16[2,2,2,512,256]{4,3,2,1,0:T(8,128)(2,1)}) custom-call(s32[2]{0:T(128)} %pad_add_fusion.1.place_ref, bf16[512,1024]{1,0:T(8,128)(2,1)} %get-tuple-element.106.left_any, bf16[2,512,4608]{2,1,0:T(8,128)(2,1)} %get-tuple-element.100.units_any.own_any, ...), custom_call_target="tpu_custom_call" | custom-call | flops 1000 | bytes 1000 | tf_op jit(solution)/shard_map/up_grads/pallas_call | solution.py:998
  172.1 28.5 %attend_back.1 = (bf16[4,512,512]{2,1,0:T(8,128)(2,1)}, bf16[4,512,512]{2,1,0:T(8,128)(2,1)}, bf16[512,1024]{1,0:T(8,128)(2,1)}, f32[1,1024]{1,0:T(1,128)}, f32[1,1024]{1,0:T(1,128)}) custom-call(s32[3]{0:T(128)} %pad_add_fusion.place_ref, f32[512,1024]{1,0:T(8,128)} %get-tuple-element.102.grad_ref, bf16[512,1024]{1,0:T(8,128)(2,1)} %get-tuple-element.103.refs_0_.branch_ref, ...), custom_call_target="tpu_custom_call" | custom-call | flops 1000 | bytes 1000 | tf_op jit(solution)/shard_map/attend_back/pallas_call | solution.py:763
  201.1 13.5 %aggregate_back.1 = (bf16[1024,512]{1,0:T(8,128)(2,1)}, bf16[1024,512]{1,0:T(8,128)(2,1)}, f32[768,128]{1,0:T(8,128)}) custom-call(s32[3]{0:T(128)} %pad_add_fusion.place_ref, f32[1]{0:T(128)} %dynamic_slice.61.alive_ref, bf16[512,1024]{1,0:T(8,128)(2,1)} %get-tuple-element.108.token_grad_ref, f32[4,48,512]{2,1,0:T(8,128)} %get-tuple-element.109.pixels_ref, ...), custom_call_target="tpu_custom_call" | custom-call | flops 1000 | bytes 1000 | tf_op jit(solution)/shard_map/aggregate_back/pallas_call | solution.py:901
  214.8 4.6 %collective-permute-done.26.up_came = bf16[2,2,2,512,256]{4,3,2,1,0:T(8,128)(2,1)S(1)} collective-permute-done((bf16[2,2,2,512,256]{4,3,2,1,0:T(8,128)(2,1)}, bf16[2,2,2,512,256]{4,3,2,1,0:T(8,128)(2,1)S(1)}, u32[]{:S(2)}, u32[]{:S(2)}) %collective-permute-start.26) | collective-permute-done | bytes 2097184 | tf_op jit(solution)/shard_map/ppermute | solution.py:1355
  220.7 3.9 first_sums.1
  228.7 11.3 %square_grads.1 = (bf16[4,512,512]{2,1,0:T(8,128)(2,1)}, bf16[4,512,512]{2,1,0:T(8,128)(2,1)}, bf16[2,4,128,512]{3,2,1,0:T(8,128)(2,1)}, bf16[2,4,128,512]{3,2,1,0:T(8,128)(2,1)}) custom-call(s32[2]{0:T(128)} %pad_add_fusion.2.place_ref, bf16[1024,512]{1,0:T(8,128)(2,1)} %get-tuple-element.119.after_any.tail_own, bf16[1024,512]{1,0:T(8,128)(2,1)} %copy-done.25, ...), custom_call_target="tpu_custom_call" | custom-call | flops 1000 | bytes 1000 | tf_op jit(solution)/shard_map/square_grads/pallas_call | solution.py:1118
  240.1 9.1 %collective-permute-done.27.down_brought = bf16[4,512,256]{2,1,0:T(8,128)(2,1)S(1)} collective-permute-done((bf16[4,512,256]{2,1,0:T(8,128)(2,1)}, bf16[4,512,256]{2,1,0:T(8,128)(2,1)S(1)}, u32[]{:S(2)}, u32[]{:S(2)}) %collective-permute-start.27) | collective-permute-done | bytes 1048608 | tf_op jit(solution)/shard_map/ppermute | solution.py:1355
  250.9 4.7 %second_sums.1 = (bf16[2,512,256]{2,1,0:T(8,128)(2,1)}, bf16[2,512,256]{2,1,0:T(8,128)(2,1)}, bf16[2,512,256]{2,1,0:T(8,128)(2,1)}, bf16[2,512,256]{2,1,0:T(8,128)(2,1)}) custom-call(bf16[2,2,2,512,256]{4,3,2,1,0:T(8,128)(2,1)} %get-tuple-element.105.refs_0_.refs_8_.down_keep, bf16[2,2,2,512,256]{4,3,2,1,0:T(8,128)(2,1)} %copy-done.11, ...), custom_call_target="tpu_custom_call" | custom-call | flops 1000 | bytes 1000 | tf_op jit(solution)/shard_map/second_sums/pallas_call | solution.py:1177
  257.7 3.6 collective-permute-start.36
  261.3 17.8 %collective-permute-done.29.came.cross_came = bf16[2,4,128,512]{3,2,1,0:T(8,128)(2,1)S(1)} collective-permute-done((bf16[2,4,128,512]{3,2,1,0:T(8,128)(2,1)S(1)}, bf16[2,4,128,512]{3,2,1,0:T(8,128)(2,1)S(1)}, u32[]{:S(2)}, u32[]{:S(2)}) %collective-permute-start.29) | collective-permute-done | bytes 1048608 | tf_op jit(solution)/shard_map/ppermute | solution.py:1355
  283.5 2.6 collective-permute-start.35
  289.5 17.2 %collective-permute-done.35 = bf16[2,512,256]{2,1,0:T(8,128)(2,1)S(1)} collective-permute-done((bf16[2,512,256]{2,1,0:T(8,128)(2,1)S(1)}, bf16[2,512,256]{2,1,0:T(8,128)(2,1)S(1)}, u32[]{:S(2)}, u32[]{:S(2)}) %collective-permute-start.35) | collective-permute-done | bytes 524320 | tf_op jit(solution)/shard_map/ppermute | solution.py:1355
  315.6 4.4 %fourth_sums.1 = (bf16[640,512]{1,0:T(8,128)(2,1)}, bf16[640,512]{1,0:T(8,128)(2,1)}, bf16[640,512]{1,0:T(8,128)(2,1)}, bf16[640,512]{1,0:T(8,128)(2,1)}) custom-call(bf16[4,512,512]{2,1,0:T(8,128)(2,1)} %get-tuple-element.137.keep, bf16[4,512,512]{2,1,0:T(8,128)(2,1)} %copy-done.21, bf16[2,4,128,512]{3,2,1,0:T(8,128)(2,1)} %get-tuple-element.127.keep.cross_keep, ...), custom_call_target="tpu_custom_call" | custom-call | flops 1000 | bytes 1000 | tf_op jit(solution)/shard_map/fourth_sums/pallas_call | solution.py:1218
  320.0 3.6 collective-permute-start.39
  326.6 13.3 %collective-permute-done.39 = bf16[640,512]{1,0:T(8,128)(2,1)} collective-permute-done((bf16[640,512]{1,0:T(8,128)(2,1)}, bf16[640,512]{1,0:T(8,128)(2,1)}, u32[]{:S(2)}, u32[]{:S(2)}) %collective-permute-start.39) | collective-permute-done | bytes 655392 | tf_op jit(solution)/shard_map/ppermute | solution.py:1355
  339.9 37.1 %collective-permute-done.38 = bf16[640,512]{1,0:T(8,128)(2,1)} collective-permute-done((bf16[640,512]{1,0:T(8,128)(2,1)}, bf16[640,512]{1,0:T(8,128)(2,1)}, u32[]{:S(2)}, u32[]{:S(2)}) %collective-permute-start.38) | collective-permute-done | bytes 655392 | tf_op jit(solution)/shard_map/ppermute | solution.py:1355
  380.3 3.7 collective-permute-done.40
  392.7 4.0 collective-permute-done.42
  400.7 9.3 %collective-permute-done.44 = bf16[4,128,512]{2,1,0:T(8,128)(2,1)S(1)} collective-permute-done((bf16[4,128,512]{2,1,0:T(8,128)(2,1)S(1)}, bf16[4,128,512]{2,1,0:T(8,128)(2,1)S(1)}, u32[]{:S(2)}, u32[]{:S(2)}) %collective-permute-start.44) | collective-permute-done | bytes 524320 | tf_op jit(solution)/shard_map/ppermute | solution.py:1355
  416.5 8.3 %finish.1 = (f32[512,1024]{1,0:T(8,128)}, f32[2,1024]{1,0:T(2,128)}, f32[2,1024]{1,0:T(2,128)}, f32[1,1024]{1,0:T(1,128)}, f32[4,1024]{1,0:T(4,128)}, /*index=5*...) custom-call(s32[5]{0:T(128)} %stack.173.place_ref, ...), custom_call_target="tpu_custom_call" | custom-call | flops 1000 | bytes 1000 | tf_op jit(solution)/shard_map/finish/pallas_call | solution.py:1324
  (245 shorter events, 101.1 us)
Async XLA Ops:
  3.7 29.1 %collective-permute-start.3 = (bf16[256,1024]{1,0:T(8,128)(2,1)}, bf16[256,1024]{1,0:T(8,128)(2,1)}, u32[]{:S(2)}, u32[]{:S(2)}) collective-permute-start(bf16[256,1024]{1,0:T(8,128)(2,1)} %get-tuple-element.193), channel_id=1, source_target_pairs={{0,16},{16,0},{1,17},{17,1},{2,18},{18,2},{3,19},{19,3},{4,20},{20... | collective-permute-start | bytes 1572872 | tf_op jit(solution)/shard_map/ppermute | solution.py:1355
  18.5 18.0 %collective-permute-start.9 = (f32[240,16]{1,0:T(8,128)}, f32[240,16]{1,0:T(8,128)}, u32[]{:S(2)}, u32[]{:S(2)}) collective-permute-start(f32[240,16]{1,0:T(8,128)} %get-tuple-element.90), channel_id=1, source_target_pairs={{0,16},{1,17},{2,18},{3,19},{4,20},{5,21},{6,22},{7,23},{8,24},{9,... | collective-permute-start | bytes 46088 | tf_op jit(solution)/shard_map/ppermute | solution.py:1492
  23.7 14.0 %collective-permute-start.10 = (bf16[1024,256]{1,0:T(8,128)(2,1)}, bf16[1024,256]{1,0:T(8,128)(2,1)}, u32[]{:S(2)}, u32[]{:S(2)}) collective-permute-start(bf16[1024,256]{1,0:T(8,128)(2,1)} %convert_element_type.90), channel_id=1, source_target_pairs={{0,16},{1,17},{2,18},{3,19},{4,20},{5,21},{6,22},{7,23},{8,24},{9,... | collective-permute-start | bytes 1572872 | tf_op jit(solution)/shard_map/ppermute | solution.py:1492
  32.8 16.0 %collective-permute-start.4 = (bf16[256,1024]{1,0:T(8,128)(2,1)S(1)}, bf16[256,1024]{1,0:T(8,128)(2,1)}, u32[]{:S(2)}, u32[]{:S(2)}) collective-permute-start(bf16[256,1024]{1,0:T(8,128)(2,1)S(1)} %get-tuple-element.86), channel_id=1, source_target_pairs={{0,16},{16,0},{1,17},{17,1},{2,18},{18,2},{3,19},{19,3},{4,20},{20... | collective-permute-start | bytes 1572872 | tf_op jit(solution)/shard_map/ppermute | solution.py:1355
  32.8 18.6 %collective-permute-start.11 = (bf16[256,1024]{1,0:T(8,128)(2,1)}, bf16[256,1024]{1,0:T(8,128)(2,1)S(1)}, u32[]{:S(2)}, u32[]{:S(2)}) collective-permute-start(bf16[256,1024]{1,0:T(8,128)(2,1)} %collective-permute-done.3), channel_id=1, source_target_pairs={{0,2},{1,3},{2,0},{3,1},{4,6},{5,7},{6,4},{7,5},{8,10},{9,11},{10,... | collective-permute-start | bytes 1572872 | tf_op jit(solution)/shard_map/ppermute | solution.py:1355
  34.7 34.3 %collective-permute-start.7 = (f32[384,128]{1,0:T(8,128)S(1)}, f32[384,128]{1,0:T(8,128)S(1)}, u32[]{:S(2)}, u32[]{:S(2)}) collective-permute-start(f32[384,128]{1,0:T(8,128)S(1)} %get-tuple-element.217), channel_id=1, source_target_pairs={{0,16},{16,0},{1,17},{17,1},{2,18},{18,2},{3,19},{19,3},{4,20},{20... | collective-permute-start | bytes 589832 | tf_op jit(solution)/shard_map/ppermute | solution.py:1355
  48.8 15.3 %collective-permute-start.6 = (bf16[256,1024]{1,0:T(8,128)(2,1)S(1)}, bf16[256,1024]{1,0:T(8,128)(2,1)}, u32[]{:S(2)}, u32[]{:S(2)}) collective-permute-start(bf16[256,1024]{1,0:T(8,128)(2,1)S(1)} %get-tuple-element.88), channel_id=1, source_target_pairs={{0,16},{16,0},{1,17},{17,1},{2,18},{18,2},{3,19},{19,3},{4,20},{20... | collective-permute-start | bytes 1572872 | tf_op jit(solution)/shard_map/ppermute | solution.py:1355
  52.5 16.5 %collective-permute-start.12 = (bf16[2,256,1024]{2,1,0:T(8,128)(2,1)S(1)}, bf16[2,256,1024]{2,1,0:T(8,128)(2,1)S(1)}, u32[]{:S(2)}, u32[]{:S(2)}) collective-permute-start(bf16[2,256,1024]{2,1,0:T(8,128)(2,1)S(1)} %pad_maximum_fusion.1.brought_ref.refs_0_), channel_id=1, source_target_pairs={{0,1},{1,0},{2,3},{3,2},{4,5},{5,4},{6,7},{7,6},{8,9},{9,8},{10,11... | collective-permute-start | bytes 3145736 | tf_op jit(solution)/shard_map/ppermute | solution.py:1355
  52.8 14.7 %collective-permute-start.13 = (bf16[256,1024]{1,0:T(8,128)(2,1)}, bf16[256,1024]{1,0:T(8,128)(2,1)}, u32[]{:S(2)}, u32[]{:S(2)}) collective-permute-start(bf16[256,1024]{1,0:T(8,128)(2,1)} %collective-permute-done.4), channel_id=1, source_target_pairs={{0,2},{1,3},{2,0},{3,1},{4,6},{5,7},{6,4},{7,5},{8,10},{9,11},{10,... | collective-permute-start | bytes 1572872 | tf_op jit(solution)/shard_map/ppermute | solution.py:1355
  64.1 15.9 %collective-permute-start.15 = (bf16[256,1024]{1,0:T(8,128)(2,1)}, bf16[256,1024]{1,0:T(8,128)(2,1)S(1)}, u32[]{:S(2)}, u32[]{:S(2)}) collective-permute-start(bf16[256,1024]{1,0:T(8,128)(2,1)} %collective-permute-done.6), channel_id=1, source_target_pairs={{0,2},{1,3},{2,0},{3,1},{4,6},{5,7},{6,4},{7,5},{8,10},{9,11},{10,... | collective-permute-start | bytes 1572872 | tf_op jit(solution)/shard_map/ppermute | solution.py:1355
  68.8 14.8 %collective-permute-start.14 = (bf16[2,256,1024]{2,1,0:T(8,128)(2,1)S(1)}, bf16[2,256,1024]{2,1,0:T(8,128)(2,1)S(1)}, u32[]{:S(2)}, u32[]{:S(2)}) collective-permute-start(bf16[2,256,1024]{2,1,0:T(8,128)(2,1)S(1)} %pad_maximum_fusion.2.refs_2_.refs_4_), channel_id=1, source_target_pairs={{0,1},{1,0},{2,3},{3,2},{4,5},{5,4},{6,7},{7,6},{8,9},{9,8},{10,11... | collective-permute-start | bytes 3145736 | tf_op jit(solution)/shard_map/ppermute | solution.py:1355
  68.9 14.4 %collective-permute-start.17 = (bf16[256,1024]{1,0:T(8,128)(2,1)S(1)}, bf16[256,1024]{1,0:T(8,128)(2,1)}, u32[]{:S(2)}, u32[]{:S(2)}) collective-permute-start(bf16[256,1024]{1,0:T(8,128)(2,1)S(1)} %get-tuple-element.95), channel_id=1, source_target_pairs={{0,16},{16,0},{1,17},{17,1},{2,18},{18,2},{3,19},{19,3},{4,20},{20... | collective-permute-start | bytes 1572872 | tf_op jit(solution)/shard_map/ppermute | solution.py:1355
  83.3 22.2 %collective-permute-start.18 = (bf16[256,1024]{1,0:T(8,128)(2,1)}, bf16[256,1024]{1,0:T(8,128)(2,1)S(1)}, u32[]{:S(2)}, u32[]{:S(2)}) collective-permute-start(bf16[256,1024]{1,0:T(8,128)(2,1)} %collective-permute-done.17), channel_id=1, source_target_pairs={{0,2},{1,3},{2,0},{3,1},{4,6},{5,7},{6,4},{7,5},{8,10},{9,11},{10,... | collective-permute-start | bytes 1572872 | tf_op jit(solution)/shard_map/ppermute | solution.py:1355
  83.6 27.6 %collective-permute-start.20 = (bf16[1024,512]{1,0:T(8,128)(2,1)S(1)}, bf16[1024,512]{1,0:T(8,128)(2,1)S(1)}, u32[]{:S(2)}, u32[]{:S(2)}) collective-permute-start(bf16[1024,512]{1,0:T(8,128)(2,1)S(1)} %copy-done.23), channel_id=1, source_target_pairs={{0,1},{1,0},{2,3},{3,2},{4,5},{5,4},{6,7},{7,6},{8,9},{9,8},{10,11... | collective-permute-start | bytes 3145736 | tf_op jit(solution)/shard_map/ppermute | solution.py:1355
  133.6 18.9 %collective-permute-start.21 = (bf16[2,512,4608]{2,1,0:T(8,128)(2,1)}, bf16[2,512,4608]{2,1,0:T(8,128)(2,1)}, u32[]{:S(2)}, u32[]{:S(2)}) collective-permute-start(bf16[2,512,4608]{2,1,0:T(8,128)(2,1)} %get-tuple-element.100.units_any.own_any), channel_id=1, source_target_pairs={{0,1},{1,0},{2,3},{3,2},{4,5},{5,4},{6,7},{7,6},{8,9},{9,8},{10,11... | collective-permute-start | bytes 28311560 | tf_op jit(solution)/shard_map/ppermute | solution.py:1355
  161.2 53.6 %collective-permute-start.25 = (bf16[2,2,2,512,256]{4,3,2,1,0:T(8,128)(2,1)}, bf16[2,2,2,512,256]{4,3,2,1,0:T(8,128)(2,1)S(1)}, u32[]{:S(2)}, u32[]{:S(2)}) collective-permute-start(bf16[2,2,2,512,256]{4,3,2,1,0:T(8,128)(2,1)} %get-tuple-element.123), channel_id=1, source_target_pairs={{0,16},{16,0},{1,17},{17,1},{2,18},{18,2},{3,19},{19,3},{4,20},{20... | collective-permute-start | bytes 6291464 | tf_op jit(solution)/shard_map/ppermute | solution.py:1355
  171.5 47.9 %collective-permute-start.26 = (bf16[2,2,2,512,256]{4,3,2,1,0:T(8,128)(2,1)}, bf16[2,2,2,512,256]{4,3,2,1,0:T(8,128)(2,1)S(1)}, u32[]{:S(2)}, u32[]{:S(2)}) collective-permute-start(bf16[2,2,2,512,256]{4,3,2,1,0:T(8,128)(2,1)} %get-tuple-element.124), channel_id=1, source_target_pairs={{0,2},{1,3},{2,0},{3,1},{4,6},{5,7},{6,4},{7,5},{8,10},{9,11},{10,... | collective-permute-start | bytes 6291464 | tf_op jit(solution)/shard_map/ppermute | solution.py:1355
  172.1 55.6 %collective-permute-start.23 = (bf16[2048,512]{1,0:T(8,128)(2,1)S(1)}, bf16[2048,512]{1,0:T(8,128)(2,1)}, u32[]{:S(2)}, u32[]{:S(2)}) collective-permute-start(bf16[2048,512]{1,0:T(8,128)(2,1)S(1)} %copy-done.10), channel_id=1, source_target_pairs={{0,1},{1,0},{2,3},{3,2},{4,5},{5,4},{6,7},{7,6},{8,9},{9,8},{10,11... | collective-permute-start | bytes 6291464 | tf_op jit(solution)/shard_map/ppermute | solution.py:1355
  200.6 27.1 %collective-permute-start.24 = (bf16[4,512,512]{2,1,0:T(8,128)(2,1)}, bf16[4,512,512]{2,1,0:T(8,128)(2,1)}, u32[]{:S(2)}, u32[]{:S(2)}) collective-permute-start(bf16[4,512,512]{2,1,0:T(8,128)(2,1)} %get-tuple-element.122), channel_id=1, source_target_pairs={{0,1},{1,0},{2,3},{3,2},{4,5},{5,4},{6,7},{7,6},{8,9},{9,8},{10,11... | collective-permute-start | bytes 6291464 | tf_op jit(solution)/shard_map/ppermute | solution.py:1355
  224.6 24.5 %collective-permute-start.27 = (bf16[4,512,256]{2,1,0:T(8,128)(2,1)}, bf16[4,512,256]{2,1,0:T(8,128)(2,1)S(1)}, u32[]{:S(2)}, u32[]{:S(2)}) collective-permute-start(bf16[4,512,256]{2,1,0:T(8,128)(2,1)} %get-tuple-element.125.refs_0_), channel_id=1, source_target_pairs={{0,2},{1,3},{2,0},{3,1},{4,6},{5,7},{6,4},{7,5},{8,10},{9,11},{10,... | collective-permute-start | bytes 3145736 | tf_op jit(solution)/shard_map/ppermute | solution.py:1355
  225.4 24.6 %collective-permute-start.28 = (bf16[4,512,256]{2,1,0:T(8,128)(2,1)}, bf16[4,512,256]{2,1,0:T(8,128)(2,1)S(1)}, u32[]{:S(2)}, u32[]{:S(2)}) collective-permute-start(bf16[4,512,256]{2,1,0:T(8,128)(2,1)} %get-tuple-element.126.refs_1_), channel_id=1, source_target_pairs={{0,16},{16,0},{1,17},{17,1},{2,18},{18,2},{3,19},{19,3},{4,20},{20... | collective-permute-start | bytes 3145736 | tf_op jit(solution)/shard_map/ppermute | solution.py:1355
  255.6 23.5 %collective-permute-start.29 = (bf16[2,4,128,512]{3,2,1,0:T(8,128)(2,1)S(1)}, bf16[2,4,128,512]{3,2,1,0:T(8,128)(2,1)S(1)}, u32[]{:S(2)}, u32[]{:S(2)}) collective-permute-start(bf16[2,4,128,512]{3,2,1,0:T(8,128)(2,1)S(1)} %copy-done.43), channel_id=1, source_target_pairs={{0,16},{16,0},{1,17},{17,1},{2,18},{18,2},{3,19},{19,3},{4,20},{20... | collective-permute-start | bytes 3145736 | tf_op jit(solution)/shard_map/ppermute | solution.py:1355
  257.1 56.7 %collective-permute-start.32 = (bf16[4,512,512]{2,1,0:T(8,128)(2,1)}, bf16[4,512,512]{2,1,0:T(8,128)(2,1)S(1)}, u32[]{:S(2)}, u32[]{:S(2)}) collective-permute-start(bf16[4,512,512]{2,1,0:T(8,128)(2,1)} %get-tuple-element.138.after_any), channel_id=1, source_target_pairs={{0,2},{1,3},{2,0},{3,1},{4,6},{5,7},{6,4},{7,5},{8,10},{9,11},{10,... | collective-permute-start | bytes 6291464 | tf_op jit(solution)/shard_map/ppermute | solution.py:1355
  257.7 30.0 %collective-permute-start.36 = (bf16[2,512,256]{2,1,0:T(8,128)(2,1)}, bf16[2,512,256]{2,1,0:T(8,128)(2,1)S(1)}, u32[]{:S(2)}, u32[]{:S(2)}) collective-permute-start(bf16[2,512,256]{2,1,0:T(8,128)(2,1)} %get-tuple-element.133), channel_id=1, source_target_pairs={{0,12},{1,13},{2,14},{3,15},{4,8},{5,9},{6,10},{7,11},{8,4},{9,5},... | collective-permute-start | bytes 1572872 | tf_op jit(solution)/shard_map/ppermute | solution.py:1355
  282.3 31.5 %collective-permute-start.30 = (bf16[512,1024]{1,0:T(8,128)(2,1)S(1)}, bf16[512,1024]{1,0:T(8,128)(2,1)S(1)}, u32[]{:S(2)}, u32[]{:S(2)}) collective-permute-start(bf16[512,1024]{1,0:T(8,128)(2,1)S(1)} %broadcast_select_fusion), channel_id=1, source_target_pairs={{0,16},{16,0},{1,17},{17,1},{2,18},{18,2},{3,19},{19,3},{4,20},{20... | collective-permute-start | bytes 3145736 | tf_op jit(solution)/shard_map/ppermute | solution.py:1355
  283.5 23.3 %collective-permute-start.35 = (bf16[2,512,256]{2,1,0:T(8,128)(2,1)S(1)}, bf16[2,512,256]{2,1,0:T(8,128)(2,1)S(1)}, u32[]{:S(2)}, u32[]{:S(2)}) collective-permute-start(bf16[2,512,256]{2,1,0:T(8,128)(2,1)S(1)} %copy-done.45), channel_id=1, source_target_pairs={{0,8},{1,9},{2,10},{3,11},{4,12},{5,13},{6,14},{7,15},{8,0},{9,1},... | collective-permute-start | bytes 1572872 | tf_op jit(solution)/shard_map/ppermute | solution.py:1355
  286.1 21.6 %collective-permute-start.34 = (bf16[2,512,256]{2,1,0:T(8,128)(2,1)S(1)}, bf16[2,512,256]{2,1,0:T(8,128)(2,1)S(1)}, u32[]{:S(2)}, u32[]{:S(2)}) collective-permute-start(bf16[2,512,256]{2,1,0:T(8,128)(2,1)S(1)} %copy-done.44), channel_id=1, source_target_pairs={{0,4},{1,5},{2,6},{3,7},{4,0},{5,1},{6,2},{7,3},{8,12},{9,13},{10,... | collective-permute-start | bytes 1572872 | tf_op jit(solution)/shard_map/ppermute | solution.py:1355
  287.7 26.1 %collective-permute-start.33 = (bf16[4,128,512]{2,1,0:T(8,128)(2,1)S(1)}, bf16[4,128,512]{2,1,0:T(8,128)(2,1)S(1)}, u32[]{:S(2)}, u32[]{:S(2)}) collective-permute-start(bf16[4,128,512]{2,1,0:T(8,128)(2,1)S(1)} %copy-done.28), channel_id=1, source_target_pairs={{0,2},{1,3},{2,0},{3,1},{4,6},{5,7},{6,4},{7,5},{8,10},{9,11},{10,... | collective-permute-start | bytes 1572872 | tf_op jit(solution)/shard_map/ppermute | solution.py:1355
  320.0 19.9 %collective-permute-start.39 = (bf16[640,512]{1,0:T(8,128)(2,1)}, bf16[640,512]{1,0:T(8,128)(2,1)}, u32[]{:S(2)}, u32[]{:S(2)}) collective-permute-start(bf16[640,512]{1,0:T(8,128)(2,1)} %get-tuple-element.142), channel_id=1, source_target_pairs={{0,12},{1,13},{2,14},{3,15},{4,8},{5,9},{6,10},{7,11},{8,4},{9,5},... | collective-permute-start | bytes 1966088 | tf_op jit(solution)/shard_map/ppermute | solution.py:1355
  323.6 53.3 %collective-permute-start.38 = (bf16[640,512]{1,0:T(8,128)(2,1)}, bf16[640,512]{1,0:T(8,128)(2,1)}, u32[]{:S(2)}, u32[]{:S(2)}) collective-permute-start(bf16[640,512]{1,0:T(8,128)(2,1)} %get-tuple-element.141), channel_id=1, source_target_pairs={{0,8},{1,9},{2,10},{3,11},{4,12},{5,13},{6,14},{7,15},{8,0},{9,1},... | collective-permute-start | bytes 1966088 | tf_op jit(solution)/shard_map/ppermute | solution.py:1355
  323.7 53.3 %collective-permute-start.37 = (bf16[640,512]{1,0:T(8,128)(2,1)}, bf16[640,512]{1,0:T(8,128)(2,1)}, u32[]{:S(2)}, u32[]{:S(2)}) collective-permute-start(bf16[640,512]{1,0:T(8,128)(2,1)} %get-tuple-element.140), channel_id=1, source_target_pairs={{0,4},{1,5},{2,6},{3,7},{4,0},{5,1},{6,2},{7,3},{8,12},{9,13},{10,... | collective-permute-start | bytes 1966088 | tf_op jit(solution)/shard_map/ppermute | solution.py:1355
  326.5 53.7 %collective-permute-start.48 = (bf16[2,512,128]{2,1,0:T(8,128)(2,1)S(1)}, bf16[2,512,128]{2,1,0:T(8,128)(2,1)S(1)}, u32[]{:S(2)}, u32[]{:S(2)}) collective-permute-start(bf16[2,512,128]{2,1,0:T(8,128)(2,1)S(1)} %convert_bitcast_fusion), channel_id=1, source_target_pairs={{0,1},{1,0},{2,3},{3,2},{4,5},{5,4},{6,7},{7,6},{8,9},{9,8},{10,11... | collective-permute-start | bytes 786440 | tf_op jit(solution)/shard_map/ppermute | solution.py:1355
  (63 other events, 494.6 us)
